TPU v7x, 32 devices: a whole 2x2x4 slice. The times are simulated.
32 devices in a mesh: member: 2 (over y), cell: 16 (over z, x, core).
Axes of the slice: x: 2, y: 2, z: 4, core: 2. Of those that a mesh axis runs over, the one named last changes fastest.
Arguments:
- wave_energy: float32 [2304, 2048], P(('member', 'cell')), parts along dimension 0, may hold values from -6 to 6
- courant: float32 [1152], replicated, may hold values from -0.9 to 0.9
- sea_mask: int32 [2048], replicated, may hold values 0 or 1
- lift_weight: bfloat16 [1024, 1152], replicated, may hold values from -0.1875 to 0.1875
- back_weight: bfloat16 [1152, 1024], replicated, may hold values from -0.1875 to 0.1875
Outputs:
- wave_next: float32 [2304, 2048], P(('member', 'cell')), parts along dimension 0
There are 2 independent parts, one for each index of `member`. A program takes and returns all parts, laid end to end along the dimension named above; an argument that names none is the same for every part. Nothing has to cross between parts.
All inputs are finite; a program needn't handle non-finite values.
Results may differ from a plain program's by a relative error of at most 0.0026.
Values sent between devices are 32-bit elements; how exact they have to be, the bound alone decides.
No kernel may reach another device: no remote copies, remote signals or barrier semaphores. Data moves between devices by JAX's collectives and lax.ppermute only.
A program may use at most 64 MiB of HBM per device.

v0:
```python
import jax
import jax.numpy as jnp
from jax import lax
from jax.sharding import PartitionSpec as P

STEPS = 2


coupling = 0.25


def with_halo(value, sides, width):
    for axis, dim in sides:
        devices, length = (lax.axis_size(axis), value.shape[dim])
        up = [(i, (i + 1) % devices) for i in range(devices - 1)]
        down = [(j, i) for i, j in up]
        last = lax.slice_in_dim(value, length - width, length, axis=dim)
        first = lax.slice_in_dim(value, 0, width, axis=dim)
        before = lax.ppermute(last, axis, up)
        after = lax.ppermute(first, axis, down)
        value = jnp.concatenate([before, value, after], axis=dim)
    return value


def minmod(first_term, second_term):
    return (
        0.5
        * (jnp.sign(first_term) + jnp.sign(second_term))
        * jnp.minimum(jnp.abs(first_term), jnp.abs(second_term))
    )


def substep(spectra, sea_field, speeds):
    extent_cells = spectra.shape[1]
    differences = spectra[:, 1:] - spectra[:, :-1]
    slopes = minmod(differences[:, 1:], differences[:, :-1])
    forward_speed = jnp.maximum(speeds, 0.0)
    backward_speed = jnp.minimum(speeds, 0.0)
    open_faces = sea_field[1 : extent_cells - 2] * sea_field[2 : extent_cells - 1]
    fluxes = forward_speed * (
        spectra[:, 1 : extent_cells - 2]
        + 0.5 * (1.0 - forward_speed) * slopes[:, 0 : extent_cells - 3]
    )
    fluxes = fluxes + backward_speed * (
        spectra[:, 2 : extent_cells - 1]
        - 0.5 * (1.0 + backward_speed) * slopes[:, 1 : extent_cells - 2]
    )
    fluxes = fluxes * open_faces
    return spectra[:, 2 : extent_cells - 2] - (fluxes[:, 1:] - fluxes[:, :-1])


def shards(wave_energy, courant, sea_mask, lift_weight, back_weight):
    devices_count = lax.axis_size("cell")
    device_rank = lax.axis_index("cell")
    groups, all_cells = wave_energy.shape
    tile_cells = all_cells // devices_count
    sea_field = sea_mask.astype(jnp.float32)
    tile_state = lax.all_to_all(wave_energy, "cell", split_axis=1, concat_axis=0, tiled=True)
    speeds = courant[:, None]
    local_sea = lax.dynamic_slice_in_dim(
        jnp.pad(sea_field, 4), device_rank * tile_cells, tile_cells + 8
    )
    for repeat in range(STEPS):
        advance_tile_state = tile_state
        for turn_index in range(2):
            extended = with_halo(advance_tile_state, (("cell", 1),), 2)
            advance_tile_state = substep(extended, local_sea[2:-2], speeds)
        lifted = jnp.dot(
            lift_weight, advance_tile_state.astype(jnp.bfloat16), preferred_element_type=jnp.float32
        )
        squared = (lifted * lifted).astype(jnp.bfloat16)
        source = jnp.dot(back_weight, squared, preferred_element_type=jnp.float32)
        tile_state = advance_tile_state + coupling * source
    return lax.all_to_all(tile_state, "cell", split_axis=0, concat_axis=1, tiled=True)


def solution(mesh):
    placed = (P(("member", "cell"), None), P(), P(), P(), P())
    return jax.shard_map(
        shards, mesh=mesh, in_specs=placed, out_specs=P(("member", "cell"), None), check_vma=False
    )
```

profile of v0, /device:TPU:0, one launch (start us, length us, event | category | flops | bytes accessed | tf_op | source)
XLA Modules:
  0.0 93.8 jit_solution(6976342103805384461)
XLA Ops:
  0.0 0.0 copy-start
  0.0 0.0 copy-start.8
  0.0 0.0 copy-start.7
  0.0 2.1 %copy_bitcast_fusion.1 = f32[72,16,128]{2,0,1:T(8,128)} fusion(f32[72,2048]{1,0:T(8,128)} %param.5), kind=kLoop, calls=%fused_computation.63 | loop fusion | bytes 1179648 | tf_op jit(solution)/shard_map/all_to_all | solution.py:58
  2.1 7.4 %all-to-all-start = ((f32[72,16,128]{2,0,1:T(8,128)}), f32[72,16,128]{2,0,1:T(8,128)S(1)}, u32[]{:S(2)}, u32[]{:S(2)}) async-start(f32[72,16,128]{2,0,1:T(8,128)} %copy_bitcast_fusion.1), calls=%async_computation | async-start | bytes 1179648 | tf_op jit(solution)/shard_map/all_to_all | solution.py:58
  9.4 0.0 copy-done.8
  9.5 0.7 pad_dynamic-slice_fusion
  10.1 0.0 copy-done.7
  10.1 0.6 broadcast_maximum_fusion
  10.8 14.2 %all-to-all-done = f32[72,16,128]{2,0,1:T(8,128)S(1)} async-done(((f32[72,16,128]{2,0,1:T(8,128)}), f32[72,16,128]{2,0,1:T(8,128)S(1)}, u32[]{:S(2)}, u32[]{:S(2)}) %all-to-all-start) | async-done | bytes 589856 | tf_op jit(solution)/shard_map/all_to_all | solution.py:58
  25.0 0.2 copy.30
  25.2 1.9 %collective-permute-start = (f32[1152,2]{0,1:T(2,128)S(1)}, f32[1152,2]{0,1:T(2,128)S(1)}, u32[]{:S(2)}, u32[]{:S(2)}) collective-permute-start(f32[1152,2]{0,1:T(2,128)S(1)} %get-tuple-element.11), channel_id=1, source_target_pairs={{0,1},{1,2},{2,3},{3,4},{4,5},{5,6},{6,7},{7,8},{8,9},{9,10},{10,1... | collective-permute-start | bytes 27656 | tf_op jit(solution)/shard_map/ppermute | solution.py:19
  27.2 1.3 %collective-permute-start.1 = (f32[1152,2]{0,1:T(2,128)S(1)}, f32[1152,2]{0,1:T(2,128)S(1)}, u32[]{:S(2)}, u32[]{:S(2)}) collective-permute-start(f32[1152,2]{0,1:T(2,128)S(1)} %get-tuple-element.12), channel_id=1, source_target_pairs={{1,0},{2,1},{3,2},{4,3},{5,4},{6,5},{7,6},{8,7},{9,8},{10,9},{11,1... | collective-permute-start | bytes 27656 | tf_op jit(solution)/shard_map/ppermute | solution.py:20
  28.5 0.8 slice_multiply_fusion.8
  29.3 0.0 copy-start.5
  29.3 0.0 copy-start.1
  29.3 0.0 copy-start.3
  29.3 0.0 collective-permute-done
  29.3 1.1 %collective-permute-done.1 = f32[1152,2]{0,1:T(2,128)S(1)} collective-permute-done((f32[1152,2]{0,1:T(2,128)S(1)}, f32[1152,2]{0,1:T(2,128)S(1)}, u32[]{:S(2)}, u32[]{:S(2)}) %collective-permute-start.1) | collective-permute-done | bytes 9248 | tf_op jit(solution)/shard_map/ppermute | solution.py:20
  30.4 0.1 pad_maximum_fusion.8
  30.5 0.1 slice_subtract_fusion.3
  30.5 0.4 minimum_multiply_fusion.3
  31.0 0.0 copy-done.1
  31.0 0.0 copy-done.3
  31.0 0.3 fusion.27
  31.3 0.1 fusion.33
  31.4 4.3 %collective-permute-start.2 = (f32[1152,2]{0,1:T(2,128)S(1)}, f32[1152,2]{0,1:T(2,128)S(1)}, u32[]{:S(2)}, u32[]{:S(2)}) collective-permute-start(f32[1152,2]{0,1:T(2,128)S(1)} %get-tuple-element.9), channel_id=1, source_target_pairs={{0,1},{1,2},{2,3},{3,4},{4,5},{5,6},{6,7},{7,8},{8,9},{9,10},{10,1... | collective-permute-start | bytes 27656 | tf_op jit(solution)/shard_map/ppermute | solution.py:19
  35.7 1.3 %collective-permute-start.3 = (f32[1152,2]{0,1:T(2,128)S(1)}, f32[1152,2]{0,1:T(2,128)S(1)}, u32[]{:S(2)}, u32[]{:S(2)}) collective-permute-start(f32[1152,2]{0,1:T(2,128)S(1)} %get-tuple-element.10), channel_id=1, source_target_pairs={{1,0},{2,1},{3,2},{4,3},{5,4},{6,5},{7,6},{8,7},{9,8},{10,9},{11,1... | collective-permute-start | bytes 27656 | tf_op jit(solution)/shard_map/ppermute | solution.py:20
  37.0 0.0 collective-permute-done.2
  37.0 1.8 %collective-permute-done.3 = f32[1152,2]{0,1:T(2,128)S(1)} collective-permute-done((f32[1152,2]{0,1:T(2,128)S(1)}, f32[1152,2]{0,1:T(2,128)S(1)}, u32[]{:S(2)}, u32[]{:S(2)}) %collective-permute-start.3) | collective-permute-done | bytes 9248 | tf_op jit(solution)/shard_map/ppermute | solution.py:20
  38.8 0.1 pad_maximum_fusion.9
  38.9 0.1 slice_subtract_fusion.2
  38.9 0.4 minimum_multiply_fusion.2
  39.4 0.0 copy-done.5
  39.4 1.1 %fusion.21 = f32[1152,129]{0,1:T(8,128)} fusion(f32[1152,130]{0,1:T(8,128)S(1)} %minimum_multiply_fusion.2, f32[1152,2]{0,1:T(2,128)S(1)} %collective-permute-done.3, f32[1152,128]{0,1:T(8,128)S(1)} %fusion.33, f32[1152,2]{0,1:T(2,128)S(1)} %collective-permute-done.2, f32[129]{0:T(256)S(1)} %slice_multiply_fusion.8, f32[1152]{0:T(1024)S(1)} %get-tuple-element.14, ...), kind=kLoop, calls=%fused_computation.36 | loop fusion | flops 1486080 | bytes 2410500 | tf_op jit(solution)/shard_map/mul | solution.py:48
  40.5 0.0 copy-done
  40.5 4.2 %fusion.1 = f32[1152,128]{0,1:T(8,128)S(1)} fusion(bf16[1152,1024]{1,0:T(8,128)(2,1)S(1)} %copy-done, bf16[1024,1152]{1,0:T(8,128)(2,1)} %param.8, f32[1152,128]{0,1:T(8,128)S(1)} %fusion.33, f32[1152,129]{0,1:T(8,128)} %fusion.21), kind=kOutput, calls=%fused_computation.3 | convolution fusion | flops 605274112 | bytes 8847360 | tf_op jit(solution)/shard_map/dot_general | solution.py:72
  44.7 5.4 %collective-permute-start.4 = (f32[1152,2]{0,1:T(2,128)S(1)}, f32[1152,2]{0,1:T(2,128)S(1)}, u32[]{:S(2)}, u32[]{:S(2)}) collective-permute-start(f32[1152,2]{0,1:T(2,128)S(1)} %get-tuple-element.7), channel_id=1, source_target_pairs={{0,1},{1,2},{2,3},{3,4},{4,5},{5,6},{6,7},{7,8},{8,9},{9,10},{10,1... | collective-permute-start | bytes 27656 | tf_op jit(solution)/shard_map/ppermute | solution.py:19
  50.1 0.0 copy-start.2
  50.1 0.0 copy-start.4
  50.1 0.0 copy-start.6
  50.1 1.4 %collective-permute-start.5 = (f32[1152,2]{0,1:T(2,128)S(1)}, f32[1152,2]{0,1:T(2,128)S(1)}, u32[]{:S(2)}, u32[]{:S(2)}) collective-permute-start(f32[1152,2]{0,1:T(2,128)S(1)} %get-tuple-element.8), channel_id=1, source_target_pairs={{1,0},{2,1},{3,2},{4,3},{5,4},{6,5},{7,6},{8,7},{9,8},{10,9},{11,1... | collective-permute-start | bytes 27656 | tf_op jit(solution)/shard_map/ppermute | solution.py:20
  51.6 0.0 collective-permute-done.4
  51.6 1.8 %collective-permute-done.5 = f32[1152,2]{0,1:T(2,128)S(1)} collective-permute-done((f32[1152,2]{0,1:T(2,128)S(1)}, f32[1152,2]{0,1:T(2,128)S(1)}, u32[]{:S(2)}, u32[]{:S(2)}) %collective-permute-start.5) | collective-permute-done | bytes 9248 | tf_op jit(solution)/shard_map/ppermute | solution.py:20
  53.3 0.1 pad_maximum_fusion.10
  53.4 0.1 slice_subtract_fusion.1
  53.5 0.4 minimum_multiply_fusion.1
  53.9 0.0 copy-done.2
  53.9 0.0 copy-done.4
  53.9 0.0 copy-done.6
  53.9 0.3 fusion.15
  54.2 0.1 fusion.31
  54.3 4.7 %collective-permute-start.6 = (f32[1152,2]{0,1:T(2,128)S(1)}, f32[1152,2]{0,1:T(2,128)S(1)}, u32[]{:S(2)}, u32[]{:S(2)}) collective-permute-start(f32[1152,2]{0,1:T(2,128)S(1)} %get-tuple-element.5), channel_id=1, source_target_pairs={{0,1},{1,2},{2,3},{3,4},{4,5},{5,6},{6,7},{7,8},{8,9},{9,10},{10,1... | collective-permute-start | bytes 27656 | tf_op jit(solution)/shard_map/ppermute | solution.py:19
  59.1 1.3 %collective-permute-start.7 = (f32[1152,2]{0,1:T(2,128)S(1)}, f32[1152,2]{0,1:T(2,128)S(1)}, u32[]{:S(2)}, u32[]{:S(2)}) collective-permute-start(f32[1152,2]{0,1:T(2,128)S(1)} %get-tuple-element.6), channel_id=1, source_target_pairs={{1,0},{2,1},{3,2},{4,3},{5,4},{6,5},{7,6},{8,7},{9,8},{10,9},{11,1... | collective-permute-start | bytes 27656 | tf_op jit(solution)/shard_map/ppermute | solution.py:20
  60.4 0.0 collective-permute-done.6
  60.4 1.8 %collective-permute-done.7 = f32[1152,2]{0,1:T(2,128)S(1)} collective-permute-done((f32[1152,2]{0,1:T(2,128)S(1)}, f32[1152,2]{0,1:T(2,128)S(1)}, u32[]{:S(2)}, u32[]{:S(2)}) %collective-permute-start.7) | collective-permute-done | bytes 9248 | tf_op jit(solution)/shard_map/ppermute | solution.py:20
  62.2 0.1 pad_maximum_fusion.11
  62.2 0.1 slice_subtract_fusion
  62.3 0.4 minimum_multiply_fusion
  62.7 1.1 %fusion.9 = f32[1152,129]{0,1:T(8,128)} fusion(f32[1152,130]{0,1:T(8,128)S(1)} %minimum_multiply_fusion, f32[1152,2]{0,1:T(2,128)S(1)} %collective-permute-done.7, f32[1152,128]{0,1:T(8,128)S(1)} %fusion.31, f32[1152,2]{0,1:T(2,128)S(1)} %collective-permute-done.6, f32[129]{0:T(256)S(1)} %copy-done.6, f32[1152]{0:T(1024)S(1)} %get-tuple-element.14, ...), kind=kLoop, calls=%fused_computation.14 | loop fusion | flops 1486080 | bytes 2410500 | tf_op jit(solution)/shard_map/mul | solution.py:48
  63.9 4.2 %fusion.3 = f32[1152,128]{0,1:T(8,128)S(1)} fusion(bf16[1152,1024]{1,0:T(8,128)(2,1)S(1)} %copy-done, bf16[1024,1152]{1,0:T(8,128)(2,1)} %param.8, f32[1152,128]{0,1:T(8,128)S(1)} %fusion.31, f32[1152,129]{0,1:T(8,128)} %fusion.9), kind=kOutput, calls=%fused_computation.5 | convolution fusion | flops 605274112 | bytes 8847360 | tf_op jit(solution)/shard_map/dot_general | solution.py:72
  68.0 0.2 copy.31
  68.3 24.7 %all_to_all.38 = f32[16,72,128]{2,1,0:T(8,128)S(1)} all-to-all(f32[16,72,128]{2,1,0:T(8,128)S(1)} %bitcast.28), channel_id=1, replica_groups=mesh['member'=2,'cell'=16] {'cell'}, dimensions={0} | all-to-all | bytes 1179648 | tf_op jit(solution)/shard_map/all_to_all | solution.py:74
  93.0 0.9 copy_bitcast_fusion
  (5 shorter events, 0.0 us)
Async XLA Ops:
  0.0 40.5 %copy-start = (bf16[1152,1024]{1,0:T(8,128)(2,1)S(1)}, bf16[1152,1024]{1,0:T(8,128)(2,1)}, u32[]{:S(2)}) copy-start(bf16[1152,1024]{1,0:T(8,128)(2,1)} %param.9) | copy-start | bytes 7077892
  0.0 9.4 %copy-start.8 = (s32[2048]{0:T(1024)S(1)}, s32[2048]{0:T(1024)}, u32[]{:S(2)}) copy-start(s32[2048]{0:T(1024)} %param.7) | copy-start | bytes 24580
  0.0 10.1 %copy-start.7 = (f32[1152]{0:T(1024)S(1)}, f32[1152]{0:T(1024)}, u32[]{:S(2)}) copy-start(f32[1152]{0:T(1024)} %param.6) | copy-start | bytes 13828
  2.1 22.9 %all-to-all-start = ((f32[72,16,128]{2,0,1:T(8,128)}), f32[72,16,128]{2,0,1:T(8,128)S(1)}, u32[]{:S(2)}, u32[]{:S(2)}) async-start(f32[72,16,128]{2,0,1:T(8,128)} %copy_bitcast_fusion.1), calls=%async_computation | async-start | bytes 1179648 | tf_op jit(solution)/shard_map/all_to_all | solution.py:58
  25.2 4.1 %collective-permute-start = (f32[1152,2]{0,1:T(2,128)S(1)}, f32[1152,2]{0,1:T(2,128)S(1)}, u32[]{:S(2)}, u32[]{:S(2)}) collective-permute-start(f32[1152,2]{0,1:T(2,128)S(1)} %get-tuple-element.11), channel_id=1, source_target_pairs={{0,1},{1,2},{2,3},{3,4},{4,5},{5,6},{6,7},{7,8},{8,9},{9,10},{10,1... | collective-permute-start | bytes 27656 | tf_op jit(solution)/shard_map/ppermute | solution.py:19
  27.2 3.2 %collective-permute-start.1 = (f32[1152,2]{0,1:T(2,128)S(1)}, f32[1152,2]{0,1:T(2,128)S(1)}, u32[]{:S(2)}, u32[]{:S(2)}) collective-permute-start(f32[1152,2]{0,1:T(2,128)S(1)} %get-tuple-element.12), channel_id=1, source_target_pairs={{1,0},{2,1},{3,2},{4,3},{5,4},{6,5},{7,6},{8,7},{9,8},{10,9},{11,1... | collective-permute-start | bytes 27656 | tf_op jit(solution)/shard_map/ppermute | solution.py:20
  29.3 10.1 %copy-start.5 = (f32[129]{0:T(256)}, f32[129]{0:T(256)S(1)}, u32[]{:S(2)}) copy-start(f32[129]{0:T(256)S(1)} %slice_multiply_fusion.8) | copy-start | bytes 1552
  29.3 1.7 %copy-start.1 = (f32[1152]{0:T(1024)S(1)}, f32[1152]{0:T(1024)}, u32[]{:S(2)}) copy-start(f32[1152]{0:T(1024)} %get-tuple-element.15) | copy-start | bytes 13828
  29.3 1.7 %copy-start.3 = (f32[1152]{0:T(1024)S(1)}, f32[1152]{0:T(1024)}, u32[]{:S(2)}) copy-start(f32[1152]{0:T(1024)} %get-tuple-element.16) | copy-start | bytes 13828
  31.4 5.6 %collective-permute-start.2 = (f32[1152,2]{0,1:T(2,128)S(1)}, f32[1152,2]{0,1:T(2,128)S(1)}, u32[]{:S(2)}, u32[]{:S(2)}) collective-permute-start(f32[1152,2]{0,1:T(2,128)S(1)} %get-tuple-element.9), channel_id=1, source_target_pairs={{0,1},{1,2},{2,3},{3,4},{4,5},{5,6},{6,7},{7,8},{8,9},{9,10},{10,1... | collective-permute-start | bytes 27656 | tf_op jit(solution)/shard_map/ppermute | solution.py:19
  35.7 3.1 %collective-permute-start.3 = (f32[1152,2]{0,1:T(2,128)S(1)}, f32[1152,2]{0,1:T(2,128)S(1)}, u32[]{:S(2)}, u32[]{:S(2)}) collective-permute-start(f32[1152,2]{0,1:T(2,128)S(1)} %get-tuple-element.10), channel_id=1, source_target_pairs={{1,0},{2,1},{3,2},{4,3},{5,4},{6,5},{7,6},{8,7},{9,8},{10,9},{11,1... | collective-permute-start | bytes 27656 | tf_op jit(solution)/shard_map/ppermute | solution.py:20
  44.7 6.8 %collective-permute-start.4 = (f32[1152,2]{0,1:T(2,128)S(1)}, f32[1152,2]{0,1:T(2,128)S(1)}, u32[]{:S(2)}, u32[]{:S(2)}) collective-permute-start(f32[1152,2]{0,1:T(2,128)S(1)} %get-tuple-element.7), channel_id=1, source_target_pairs={{0,1},{1,2},{2,3},{3,4},{4,5},{5,6},{6,7},{7,8},{8,9},{9,10},{10,1... | collective-permute-start | bytes 27656 | tf_op jit(solution)/shard_map/ppermute | solution.py:19
  50.1 3.8 %copy-start.2 = (f32[1152]{0:T(1024)S(1)}, f32[1152]{0:T(1024)}, u32[]{:S(2)}) copy-start(f32[1152]{0:T(1024)} %get-tuple-element.15) | copy-start | bytes 13828
  50.1 3.8 %copy-start.4 = (f32[1152]{0:T(1024)S(1)}, f32[1152]{0:T(1024)}, u32[]{:S(2)}) copy-start(f32[1152]{0:T(1024)} %get-tuple-element.16) | copy-start | bytes 13828
  50.1 3.8 %copy-start.6 = (f32[129]{0:T(256)S(1)}, f32[129]{0:T(256)}, u32[]{:S(2)}) copy-start(f32[129]{0:T(256)} %copy-done.5) | copy-start | bytes 1552
  50.1 3.2 %collective-permute-start.5 = (f32[1152,2]{0,1:T(2,128)S(1)}, f32[1152,2]{0,1:T(2,128)S(1)}, u32[]{:S(2)}, u32[]{:S(2)}) collective-permute-start(f32[1152,2]{0,1:T(2,128)S(1)} %get-tuple-element.8), channel_id=1, source_target_pairs={{1,0},{2,1},{3,2},{4,3},{5,4},{6,5},{7,6},{8,7},{9,8},{10,9},{11,1... | collective-permute-start | bytes 27656 | tf_op jit(solution)/shard_map/ppermute | solution.py:20
  54.3 6.1 %collective-permute-start.6 = (f32[1152,2]{0,1:T(2,128)S(1)}, f32[1152,2]{0,1:T(2,128)S(1)}, u32[]{:S(2)}, u32[]{:S(2)}) collective-permute-start(f32[1152,2]{0,1:T(2,128)S(1)} %get-tuple-element.5), channel_id=1, source_target_pairs={{0,1},{1,2},{2,3},{3,4},{4,5},{5,6},{6,7},{7,8},{8,9},{9,10},{10,1... | collective-permute-start | bytes 27656 | tf_op jit(solution)/shard_map/ppermute | solution.py:19
  59.1 3.1 %collective-permute-start.7 = (f32[1152,2]{0,1:T(2,128)S(1)}, f32[1152,2]{0,1:T(2,128)S(1)}, u32[]{:S(2)}, u32[]{:S(2)}) collective-permute-start(f32[1152,2]{0,1:T(2,128)S(1)} %get-tuple-element.6), channel_id=1, source_target_pairs={{1,0},{2,1},{3,2},{4,3},{5,4},{6,5},{7,6},{8,7},{9,8},{10,9},{11,1... | collective-permute-start | bytes 27656 | tf_op jit(solution)/shard_map/ppermute | solution.py:20
where the time goes:
time: 94.3 us; the launch traced here: 93.8 us
  starting transfers between devices  29 us (31%)
  blocking collectives  24.7 us (26%)
  waiting for transfers between devices  20.6 us (22%)
  matrix products  8.34 us (9%)
  other arithmetic  6.69 us (7%)
  local copies, waits for them, and re-layouts  4.13 us (4%)
    all_to_all x1, blocking collectives, shards(): lax.all_to_all(tile_state, 'cell', split_axis=0, concat_axis=1, tiled=True)  24.7 us
    ppermute x4, starting transfers between devices, with_halo(): before = lax.ppermute(last, axis, up)  16.3 us
    all_to_all x1, waiting for transfers between devices, shards(): lax.all_to_all(wave_energy, 'cell', split_axis=1, concat_axis=0, tiled=True)  14.2 us
    dot_general x2, matrix products, shards(): source = jnp.dot(back_weight, squared, preferred_element_type=jnp.float32)  8.34 us
    all_to_all x1, starting transfers between devices, shards(): lax.all_to_all(wave_energy, 'cell', split_axis=1, concat_axis=0, tiled=True)  7.36 us
    ppermute x4, waiting for transfers between devices, with_halo(): after = lax.ppermute(first, axis, down)  6.37 us
    ppermute x4, starting transfers between devices, with_halo(): after = lax.ppermute(first, axis, down)  5.3 us
    mul x4, other arithmetic, substep(): fluxes = fluxes * open_faces  2.82 us
  transfers between devices with their start and end apart: 9, of which 5 were waited for; matrix products, arithmetic and copies ran while one was open for 2% of the time, Pallas kernels for 0%

commit v1 on v0

--- a/solution.py
+++ b/solution.py
@@ -1,6 +1,10 @@
+import functools
+
 import jax
 import jax.numpy as jnp
 from jax import lax
+from jax.experimental import pallas as pl
+from jax.experimental.pallas import tpu as pltpu
 from jax.sharding import PartitionSpec as P
 
 STEPS = 2
@@ -49,29 +53,234 @@
     return spectra[:, 2 : extent_cells - 2] - (fluxes[:, 1:] - fluxes[:, :-1])
 
 
-def shards(wave_energy, courant, sea_mask, lift_weight, back_weight):
+def general_shards(wave_energy, courant, sea_mask, lift_weight, back_weight):
     devices_count = lax.axis_size("cell")
     device_rank = lax.axis_index("cell")
     groups, all_cells = wave_energy.shape
     tile_cells = all_cells // devices_count
     sea_field = sea_mask.astype(jnp.float32)
-    tile_state = lax.all_to_all(wave_energy, "cell", split_axis=1, concat_axis=0, tiled=True)
+    own_speeds = lax.dynamic_slice_in_dim(courant, device_rank * groups, groups)[:, None]
+    start_state = wave_energy
+    for turn_index in range(2):
+        start_state = substep(
+            jnp.pad(start_state, ((0, 0), (2, 2))), jnp.pad(sea_field, 2), own_speeds
+        )
+    tile_state = lax.all_to_all(start_state, "cell", split_axis=1, concat_axis=0, tiled=True)
     speeds = courant[:, None]
     local_sea = lax.dynamic_slice_in_dim(
         jnp.pad(sea_field, 4), device_rank * tile_cells, tile_cells + 8
     )
     for repeat in range(STEPS):
-        advance_tile_state = tile_state
-        for turn_index in range(2):
-            extended = with_halo(advance_tile_state, (("cell", 1),), 2)
-            advance_tile_state = substep(extended, local_sea[2:-2], speeds)
+        if repeat:
+            extended = with_halo(tile_state, (("cell", 1),), 4)
+            extended = substep(extended, local_sea, speeds)
+            tile_state = substep(extended, local_sea[2:-2], speeds)
         lifted = jnp.dot(
-            lift_weight, advance_tile_state.astype(jnp.bfloat16), preferred_element_type=jnp.float32
+            lift_weight, tile_state.astype(jnp.bfloat16), preferred_element_type=jnp.float32
         )
         squared = (lifted * lifted).astype(jnp.bfloat16)
         source = jnp.dot(back_weight, squared, preferred_element_type=jnp.float32)
-        tile_state = advance_tile_state + coupling * source
+        tile_state = tile_state + coupling * source
     return lax.all_to_all(tile_state, "cell", split_axis=0, concat_axis=1, tiled=True)
+
+
+LANES = 128
+ROWS = 8
+HALO = 4
+
+
+def lane_index(shape):
+    return lax.broadcasted_iota(jnp.int32, shape, len(shape) - 1)
+
+
+def next_tiles(tiles, after):
+    last = lane_index(tiles[0].shape) == LANES - 1
+    turned = [pltpu.roll(tile, LANES - 1, 1) for tile in tiles]
+    follow = turned[1:] + [turned[0] if after is None else after]
+    return [jnp.where(last, b, a) for a, b in zip(turned, follow)]
+
+
+def previous_tiles(tiles, before):
+    first = lane_index(tiles[0].shape) == 0
+    turned = [pltpu.roll(tile, 1, 1) for tile in tiles]
+    ahead = [turned[-1] if before is None else before] + turned[:-1]
+    return [jnp.where(first, b, a) for a, b in zip(turned, ahead)]
+
+
+def tile_substep(tiles, opens, speed, slope_speed, forward, ring):
+    zero = None if ring else jnp.zeros_like(tiles[0])
+    right = next_tiles(tiles, zero)
+    steps = [b - a for a, b in zip(tiles, right)]
+    left_steps = previous_tiles(steps, None if ring else tiles[0])
+    slopes = [
+        jnp.maximum(jnp.minimum(a, b), jnp.minimum(jnp.maximum(a, b), 0.0))
+        for a, b in zip(steps, left_steps)
+    ]
+    amounts = [speed * u + slope_speed * s for u, s in zip(tiles, slopes)]
+    right_amounts = next_tiles(amounts, zero)
+    fluxes = [
+        face * jnp.where(forward, a, b) for face, a, b in zip(opens, amounts, right_amounts)
+    ]
+    left_fluxes = previous_tiles(fluxes, zero)
+    return [u - (f - g) for u, f, g in zip(tiles, fluxes, left_fluxes)]
+
+
+def speed_terms(speed):
+    size = jnp.abs(speed)
+    return speed, 0.5 * size * (1.0 - size), speed >= 0.0
+
+
+def spread_speeds(courant_ref, speeds_ref):
+    parts = courant_ref.shape[0]
+    square = jnp.concatenate(
+        [courant_ref[...], jnp.zeros((LANES - parts, LANES), jnp.float32)], axis=0
+    )
+    turned = jnp.transpose(square)
+    for part in range(parts):
+        speeds_ref[pl.ds(part * LANES, LANES), :] = jnp.broadcast_to(
+            turned[:, part : part + 1], (LANES, LANES)
+        )
+
+
+def face_rows(sea_ref):
+    sea = sea_ref[...].astype(jnp.float32)
+    tiles = sea.shape[0]
+    turned = pltpu.roll(sea, LANES - 1, 1)
+    below = jnp.concatenate([turned[1:], jnp.zeros((1, LANES), jnp.float32)], axis=0)
+    return sea * jnp.where(lane_index(sea.shape) == LANES - 1, below, turned)
+
+
+def start_kernel(energy_ref, courant_ref, sea_ref, out_ref, speeds_ref, faces_ref):
+    groups = energy_ref.shape[0]
+    tiles = out_ref.shape[0]
+    rank = lax.axis_index("cell")
+    spread_speeds(courant_ref, speeds_ref)
+    faces_ref[...] = face_rows(sea_ref)
+    out_ref[:, groups:, :] = jnp.zeros((tiles, ROWS, LANES), jnp.float32)
+    lane = lane_index((ROWS, LANES))
+    zero = jnp.zeros((ROWS, LANES), jnp.float32)
+
+    def body(group, carry):
+        row = pl.multiple_of(group * ROWS, ROWS)
+        speed = speeds_ref[pl.ds(pl.multiple_of(rank * groups + row, ROWS), ROWS), :]
+        terms = speed_terms(speed)
+        state = [
+            energy_ref[pl.ds(row, ROWS), pl.ds(tile * LANES, LANES)] for tile in range(tiles)
+        ]
+        opens = [
+            jnp.broadcast_to(faces_ref[tile : tile + 1, :], (ROWS, LANES)) for tile in range(tiles)
+        ]
+        for turn in range(2):
+            state = tile_substep(state, opens, *terms, False)
+        mine = (lane >= row) & (lane < row + ROWS)
+        for tile in range(tiles):
+            out_ref[tile, pl.ds(row, ROWS), :] = state[tile]
+            right = state[tile + 1] if tile + 1 < tiles else zero
+            left = state[tile - 1] if tile else zero
+            edges = pltpu.roll(jnp.where(lane < LANES // 2, right, left), row + HALO, 1)
+            halo = out_ref[tile, groups:, :]
+            out_ref[tile, groups:, :] = jnp.where(mine, edges, halo)
+        return carry
+
+    lax.fori_loop(0, groups // ROWS, body, 0)
+
+
+def middle_kernel(
+    state_ref, courant_ref, sea_ref, lift_ref, back_ref, out_ref,
+    speeds_ref, faces_ref, wide_ref, source_ref, half_ref,
+):
+    sources, rows, _ = state_ref.shape
+    groups = rows - ROWS
+    modes = sources * groups
+    rank = lax.axis_index("cell")
+    tiles = faces_ref.shape[0]
+    spread_speeds(courant_ref, speeds_ref)
+    faces_ref[...] = face_rows(sea_ref)
+
+    for source in range(sources):
+        halo = state_ref[source, groups:, :]
+        for group in range(groups // ROWS):
+            row = source * groups + group * ROWS
+            own = state_ref[source, pl.ds(group * ROWS, ROWS), :]
+            beside = pltpu.roll(halo, (2 * LANES - group * ROWS - HALO) % LANES, 1)
+            wide_ref[pl.ds(row, ROWS), pl.ds(0, LANES)] = own
+            wide_ref[pl.ds(row, ROWS), pl.ds(LANES, LANES)] = beside
+    half_ref[...] = wide_ref[...].astype(jnp.bfloat16)
+
+    lifted = jnp.dot(lift_ref[...], half_ref[...], preferred_element_type=jnp.float32)
+    squared = (lifted * lifted).astype(jnp.bfloat16)
+    source_ref[...] = jnp.dot(back_ref[...], squared, preferred_element_type=jnp.float32)
+
+    own_faces = faces_ref[pl.ds(rank, 1), :]
+    after_faces = faces_ref[pl.ds(jnp.minimum(rank + 1, tiles - 1), 1), :]
+    before_faces = faces_ref[pl.ds(jnp.maximum(rank - 1, 0), 1), :]
+    after_faces = jnp.where(rank < tiles - 1, after_faces, 0.0)
+    before_faces = jnp.where(rank > 0, before_faces, 0.0)
+    beside_faces = jnp.where(lane_index((1, LANES)) < LANES // 2, after_faces, before_faces)
+    opens = [jnp.broadcast_to(own_faces, (ROWS, LANES)), jnp.broadcast_to(beside_faces, (ROWS, LANES))]
+
+    def body(group, carry):
+        row = pl.multiple_of(group * ROWS, ROWS)
+        terms = speed_terms(speeds_ref[pl.ds(row, ROWS), :])
+        state = [
+            wide_ref[pl.ds(row, ROWS), pl.ds(tile * LANES, LANES)]
+            + coupling * source_ref[pl.ds(row, ROWS), pl.ds(tile * LANES, LANES)]
+            for tile in range(2)
+        ]
+        for turn in range(2):
+            state = tile_substep(state, opens, *terms, True)
+        wide_ref[pl.ds(row, ROWS), pl.ds(0, LANES)] = state[0]
+        return carry
+
+    lax.fori_loop(0, modes // ROWS, body, 0, unroll=8)
+
+    advanced = wide_ref[:, :LANES]
+    lifted = jnp.dot(lift_ref[...], advanced.astype(jnp.bfloat16), preferred_element_type=jnp.float32)
+    squared = (lifted * lifted).astype(jnp.bfloat16)
+    source = jnp.dot(back_ref[...], squared, preferred_element_type=jnp.float32)
+    out_ref[...] = wide_ref[:, :LANES] + coupling * source
+
+
+def tiled_shards(wave_energy, courant, sea_mask, lift_weight, back_weight):
+    devices = lax.axis_size("cell")
+    groups, cells = wave_energy.shape
+    components, tiles = courant.shape[0], cells // LANES
+    courant = courant.reshape(components // LANES, LANES)
+    sea_mask = sea_mask.reshape(tiles, LANES)
+    start = pl.pallas_call(
+        start_kernel,
+        out_shape=jax.ShapeDtypeStruct((tiles, groups + ROWS, LANES), jnp.float32),
+        scratch_shapes=[
+            pltpu.VMEM((components, LANES), jnp.float32),
+            pltpu.VMEM((tiles, LANES), jnp.float32),
+        ],
+        compiler_params=pltpu.CompilerParams(vmem_limit_bytes=16 << 20),
+        name="start",
+    )(wave_energy, courant, sea_mask)
+    state = lax.all_to_all(start, "cell", split_axis=0, concat_axis=0, tiled=True)
+    final = pl.pallas_call(
+        middle_kernel,
+        out_shape=jax.ShapeDtypeStruct((components, LANES), jnp.float32),
+        scratch_shapes=[
+            pltpu.VMEM((components, LANES), jnp.float32),
+            pltpu.VMEM((tiles, LANES), jnp.float32),
+            pltpu.VMEM((components, 2 * LANES), jnp.float32),
+            pltpu.VMEM((components, 2 * LANES), jnp.float32),
+            pltpu.VMEM((components, 2 * LANES), jnp.bfloat16),
+        ],
+        compiler_params=pltpu.CompilerParams(vmem_limit_bytes=40 << 20),
+        name="middle",
+    )(state, courant, sea_mask, lift_weight, back_weight)
+    return lax.all_to_all(final, "cell", split_axis=0, concat_axis=1, tiled=True)
+
+
+def shards(wave_energy, courant, sea_mask, lift_weight, back_weight):
+    devices = lax.axis_size("cell")
+    groups, cells = wave_energy.shape
+    whole = cells == devices * LANES and groups % ROWS == 0 and groups * ROWS <= ROWS * LANES
+    whole = whole and courant.shape[0] % LANES == 0 and devices > 1
+    run = tiled_shards if whole else general_shards
+    return run(wave_energy, courant, sea_mask, lift_weight, back_weight)
 
 
 def solution(mesh):

time: 94.3 us -> 145 us (1.54)
  Pallas kernels: 0 us -> 93.6 us
  starting transfers between devices: 29 us -> 0 us
  blocking collectives: 24.7 us -> 45.7 us
  waiting for transfers between devices: 20.6 us -> 0 us
  matrix products: 8.34 us -> 0 us
  other arithmetic: 6.69 us -> 0 us
    pallas_call x0 -> x2, Pallas kernels: none -> 93.6 us  [the longest x1 86.6 us: tiled_shards(): pl.pallas_call(middle_kernel, out_shape=jax.ShapeDtypeStruct((components,...]
    ppermute x8 -> x0, starting transfers between devices: 21.6 us -> none  [the longest x4 16.3 us: with_halo(): before = lax.ppermute(last, axis, up)]
    all_to_all x1 -> x2, blocking collectives: 24.7 us -> 45.7 us  [the longest x1 25.4 us: tiled_shards(): lax.all_to_all(start, 'cell', split_axis=0, concat_axis=0, tiled=True)]
    all_to_all x1 -> x0, waiting for transfers between devices: 14.2 us -> none  [shards(): lax.all_to_all(wave_energy, 'cell', split_axis=1, concat_axis=0, tiled=True)]
    dot_general x2 -> x0, matrix products: 8.34 us -> none  [shards(): source = jnp.dot(back_weight, squared, preferred_element_type=jnp.float32)]
    all_to_all x1 -> x0, starting transfers between devices: 7.36 us -> none  [shards(): lax.all_to_all(wave_energy, 'cell', split_axis=1, concat_axis=0, tiled=True)]
    ppermute x8 -> x0, waiting for transfers between devices: 6.39 us -> none  [the longest x4 6.37 us: with_halo(): after = lax.ppermute(first, axis, down)]
    mul x9 -> x0, other arithmetic: 5.44 us -> none  [the longest x4 2.82 us: substep(): fluxes = fluxes * open_faces]
  transfers between devices with their start and end apart: 9 -> 0, of which waited for: 5 -> 0; matrix products, arithmetic and copies ran while one was open for 2% -> 0% of each run, Pallas kernels for 0% -> 0%
where the time goes in v1:
time: 145 us
  Pallas kernels  93.6 us (65%)
  blocking collectives  45.7 us (32%)
  local copies, waits for them, and re-layouts  5.14 us (4%)
    pallas_call x1, Pallas kernels, tiled_shards(): pl.pallas_call(middle_kernel, out_shape=jax.ShapeDtypeStruct((components,...  86.6 us
    all_to_all x1, blocking collectives, tiled_shards(): lax.all_to_all(start, 'cell', split_axis=0, concat_axis=0, tiled=True)  25.4 us
    all_to_all x1, blocking collectives, tiled_shards(): lax.all_to_all(final, 'cell', split_axis=0, concat_axis=1, tiled=True)  20.3 us
    pallas_call x1, Pallas kernels, tiled_shards(): pl.pallas_call(start_kernel, out_shape=jax.ShapeDtypeStruct((tiles, group...  7.01 us
    unnamed x14, local copies, waits for them, and re-layouts  4.28 us

profile of v1, /device:TPU:0, one launch (start us, length us, event | category | flops | bytes accessed | tf_op | source)
XLA Modules:
  0.0 144.6 jit_solution(1398545907844352082)
XLA Ops:
  0.0 0.0 copy-start
  0.0 0.0 copy-start.2
  0.0 1.2 copy-done.2
  1.2 0.0 copy-start.3
  1.2 0.7 copy-done.3
  1.9 0.0 copy-start.5
  1.9 0.7 copy-done.5
  2.6 0.0 copy-start.4
  2.6 0.0 copy-start.6
  2.6 7.0 %start.1 = f32[16,80,128]{2,1,0:T(8,128)S(1)} custom-call(f32[72,2048]{1,0:T(8,128)S(1)} %copy-done.2, f32[9,128]{1,0:T(8,128)S(1)} %bitcast.10, s32[16,128]{1,0:T(8,128)S(1)} %bitcast.12), custom_call_target="tpu_custom_call" | custom-call | tf_op jit(solution)/shard_map/start/pallas_call | solution.py:250
  9.6 25.4 %all_to_all.24.state_ref = f32[16,80,128]{2,1,0:T(8,128)S(1)} all-to-all(f32[16,80,128]{2,1,0:T(8,128)S(1)} %start.1), channel_id=1, replica_groups=mesh['member'=2,'cell'=16] {'cell'}, dimensions={0} | all-to-all | bytes 1310720 | tf_op jit(solution)/shard_map/all_to_all | solution.py:260
  35.0 0.0 copy-done
  35.0 0.0 copy-done.4
  35.0 0.0 copy-done.6
  35.0 0.0 copy-start.1
  35.1 1.7 %copy-done.1 = bf16[1152,1024]{1,0:T(8,128)(2,1)S(1)} copy-done((bf16[1152,1024]{1,0:T(8,128)(2,1)S(1)}, bf16[1152,1024]{1,0:T(8,128)(2,1)}, u32[]{:S(2)}) %copy-start.1) | copy-done | bytes 2359320
  36.7 86.6 %middle.1 = f32[1152,128]{1,0:T(8,128)S(1)} custom-call(f32[16,80,128]{2,1,0:T(8,128)S(1)} %all_to_all.24.state_ref, f32[9,128]{1,0:T(8,128)S(1)} %bitcast.11, s32[16,128]{1,0:T(8,128)S(1)} %bitcast.13, bf16[1024,1152]{1,0:T(8,128)(2,1)S(1)} %copy-done, bf16[1152,1024]{1,0:T(8,128)(2,1)S(1)} %copy-done.1), custom_call_target="tpu_custom_call" | custom-call | tf_op jit(solution)/shard_map/middle/pallas_call | solution.py:261
  123.3 20.3 %all_to_all.25 = f32[16,72,128]{2,1,0:T(8,128)S(1)} all-to-all(f32[16,72,128]{2,1,0:T(8,128)S(1)} %bitcast.9), channel_id=1, replica_groups=mesh['member'=2,'cell'=16] {'cell'}, dimensions={0} | all-to-all | bytes 1179648 | tf_op jit(solution)/shard_map/all_to_all | solution.py:274
  143.7 0.9 copy_bitcast_fusion
Async XLA Ops:
  0.0 35.0 %copy-start = (bf16[1024,1152]{1,0:T(8,128)(2,1)S(1)}, bf16[1024,1152]{1,0:T(8,128)(2,1)}, u32[]{:S(2)}) copy-start(bf16[1024,1152]{1,0:T(8,128)(2,1)} %lift_ref.1) | copy-start | bytes 7077892
  0.0 1.2 copy-start.2
  1.2 0.7 copy-start.3
  1.9 0.7 copy-start.5
  2.6 32.4 %copy-start.4 = (f32[1152]{0:T(1024)S(1)}, f32[1152]{0:T(1024)}, u32[]{:S(2)}) copy-start(f32[1152]{0:T(1024)} %param.6) | copy-start | bytes 13828
  2.6 32.4 %copy-start.6 = (s32[2048]{0:T(1024)S(1)}, s32[2048]{0:T(1024)}, u32[]{:S(2)}) copy-start(s32[2048]{0:T(1024)} %param.7) | copy-start | bytes 24580
  35.0 1.7 %copy-start.1 = (bf16[1152,1024]{1,0:T(8,128)(2,1)S(1)}, bf16[1152,1024]{1,0:T(8,128)(2,1)}, u32[]{:S(2)}) copy-start(bf16[1152,1024]{1,0:T(8,128)(2,1)} %back_ref.1) | copy-start | bytes 7077892

commit v2 on v1

--- a/solution.py
+++ b/solution.py
@@ -1,5 +1,3 @@
-import functools
-
 import jax
 import jax.numpy as jnp
 from jax import lax
@@ -150,6 +148,9 @@
     return sea * jnp.where(lane_index(sea.shape) == LANES - 1, below, turned)
 
 
+START_ROWS = 24
+
+
 def start_kernel(energy_ref, courant_ref, sea_ref, out_ref, speeds_ref, faces_ref):
     groups = energy_ref.shape[0]
     tiles = out_ref.shape[0]
@@ -159,86 +160,109 @@
     out_ref[:, groups:, :] = jnp.zeros((tiles, ROWS, LANES), jnp.float32)
     lane = lane_index((ROWS, LANES))
     zero = jnp.zeros((ROWS, LANES), jnp.float32)
-
-    def body(group, carry):
-        row = pl.multiple_of(group * ROWS, ROWS)
-        speed = speeds_ref[pl.ds(pl.multiple_of(rank * groups + row, ROWS), ROWS), :]
-        terms = speed_terms(speed)
-        state = [
-            energy_ref[pl.ds(row, ROWS), pl.ds(tile * LANES, LANES)] for tile in range(tiles)
-        ]
-        opens = [
-            jnp.broadcast_to(faces_ref[tile : tile + 1, :], (ROWS, LANES)) for tile in range(tiles)
-        ]
+    rows = max(r for r in range(ROWS, START_ROWS + 1, ROWS) if groups % r == 0)
+
+    for base in range(0, groups, rows):
+        own = pl.multiple_of(rank * groups + base, ROWS)
+        terms = speed_terms(speeds_ref[pl.ds(own, rows), :])
+        state = [energy_ref[base : base + rows, pl.ds(tile * LANES, LANES)] for tile in range(tiles)]
+        opens = [faces_ref[tile : tile + 1, :] for tile in range(tiles)]
         for turn in range(2):
             state = tile_substep(state, opens, *terms, False)
-        mine = (lane >= row) & (lane < row + ROWS)
         for tile in range(tiles):
-            out_ref[tile, pl.ds(row, ROWS), :] = state[tile]
-            right = state[tile + 1] if tile + 1 < tiles else zero
-            left = state[tile - 1] if tile else zero
-            edges = pltpu.roll(jnp.where(lane < LANES // 2, right, left), row + HALO, 1)
-            halo = out_ref[tile, groups:, :]
-            out_ref[tile, groups:, :] = jnp.where(mine, edges, halo)
-        return carry
-
-    lax.fori_loop(0, groups // ROWS, body, 0)
+            out_ref[tile, base : base + rows, :] = state[tile]
+        for row in range(base, base + rows, ROWS):
+            part = slice(row - base, row - base + ROWS)
+            mine = (lane >= row) & (lane < row + ROWS)
+            for tile in range(tiles):
+                right = state[tile + 1][part] if tile + 1 < tiles else zero
+                left = state[tile - 1][part] if tile else zero
+                edges = pltpu.roll(jnp.where(lane < LANES // 2, right, left), row + HALO, 1)
+                halo = out_ref[tile, groups:, :]
+                out_ref[tile, groups:, :] = jnp.where(mine, edges, halo)
+
+
+def row_index(shape):
+    return lax.broadcasted_iota(jnp.int32, shape, 0)
+
+
+def row_substep(state, opens, speed, slope_speed, forward):
+    rows = state.shape[0]
+    steps = pltpu.roll(state, rows - 1, 0) - state
+    left_steps = pltpu.roll(steps, 1, 0)
+    slopes = jnp.maximum(
+        jnp.minimum(steps, left_steps), jnp.minimum(jnp.maximum(steps, left_steps), 0.0)
+    )
+    amounts = speed * state + slope_speed * slopes
+    fluxes = opens * jnp.where(forward, amounts, pltpu.roll(amounts, rows - 1, 0))
+    return state - (fluxes - pltpu.roll(fluxes, 1, 0))
 
 
 def middle_kernel(
     state_ref, courant_ref, sea_ref, lift_ref, back_ref, out_ref,
-    speeds_ref, faces_ref, wide_ref, source_ref, half_ref,
+    faces_ref, own_ref, half_ref, squared_ref,
 ):
     sources, rows, _ = state_ref.shape
     groups = rows - ROWS
     modes = sources * groups
+    blocks = modes // LANES
     rank = lax.axis_index("cell")
     tiles = faces_ref.shape[0]
-    spread_speeds(courant_ref, speeds_ref)
+    lane = lane_index((LANES, LANES))
+
     faces_ref[...] = face_rows(sea_ref)
-
-    for source in range(sources):
-        halo = state_ref[source, groups:, :]
-        for group in range(groups // ROWS):
-            row = source * groups + group * ROWS
-            own = state_ref[source, pl.ds(group * ROWS, ROWS), :]
-            beside = pltpu.roll(halo, (2 * LANES - group * ROWS - HALO) % LANES, 1)
-            wide_ref[pl.ds(row, ROWS), pl.ds(0, LANES)] = own
-            wide_ref[pl.ds(row, ROWS), pl.ds(LANES, LANES)] = beside
-    half_ref[...] = wide_ref[...].astype(jnp.bfloat16)
-
-    lifted = jnp.dot(lift_ref[...], half_ref[...], preferred_element_type=jnp.float32)
-    squared = (lifted * lifted).astype(jnp.bfloat16)
-    source_ref[...] = jnp.dot(back_ref[...], squared, preferred_element_type=jnp.float32)
-
     own_faces = faces_ref[pl.ds(rank, 1), :]
     after_faces = faces_ref[pl.ds(jnp.minimum(rank + 1, tiles - 1), 1), :]
     before_faces = faces_ref[pl.ds(jnp.maximum(rank - 1, 0), 1), :]
     after_faces = jnp.where(rank < tiles - 1, after_faces, 0.0)
     before_faces = jnp.where(rank > 0, before_faces, 0.0)
-    beside_faces = jnp.where(lane_index((1, LANES)) < LANES // 2, after_faces, before_faces)
-    opens = [jnp.broadcast_to(own_faces, (ROWS, LANES)), jnp.broadcast_to(beside_faces, (ROWS, LANES))]
-
-    def body(group, carry):
-        row = pl.multiple_of(group * ROWS, ROWS)
-        terms = speed_terms(speeds_ref[pl.ds(row, ROWS), :])
-        state = [
-            wide_ref[pl.ds(row, ROWS), pl.ds(tile * LANES, LANES)]
-            + coupling * source_ref[pl.ds(row, ROWS), pl.ds(tile * LANES, LANES)]
-            for tile in range(2)
-        ]
+    square = jnp.concatenate(
+        [own_faces, before_faces, after_faces, jnp.zeros((LANES - 3, LANES), jnp.float32)], axis=0
+    )
+    turned = jnp.transpose(square)
+    column = jnp.concatenate(
+        [turned[LANES - ROWS :, 1:2], turned[:, 0:1], turned[:ROWS, 2:3]], axis=0
+    )
+    opens = jnp.broadcast_to(column, (LANES + 2 * ROWS, LANES))
+
+    for source in range(sources):
+        halo = state_ref[source, groups:, :]
+        for group in range(groups // ROWS):
+            row = source * groups + group * ROWS
+            own = state_ref[source, group * ROWS : (group + 1) * ROWS, :]
+            shift = -group * ROWS % LANES
+            own_ref[row : row + ROWS, :LANES] = own
+            own_ref[row : row + ROWS, LANES:] = pltpu.roll(halo, shift, 1) if shift else halo
+    half_ref[...] = own_ref[...].astype(jnp.bfloat16)
+
+    lifted = jnp.dot(lift_ref[...], half_ref[...], preferred_element_type=jnp.float32)
+    squared_ref[...] = (lifted * lifted).astype(jnp.bfloat16)
+    own_ref[...] += coupling * jnp.dot(
+        back_ref[...], squared_ref[...], preferred_element_type=jnp.float32
+    )
+
+    merged = jnp.zeros((LANES, LANES), jnp.float32)
+    for block in range(blocks):
+        here = own_ref[block * LANES : (block + 1) * LANES, LANES:]
+        here = pltpu.roll(here, block * ROWS, 1) if block else here
+        merged = jnp.where((lane >= block * ROWS) & (lane < (block + 1) * ROWS), here, merged)
+    halos = jnp.transpose(merged)
+    for block in range(blocks):
+        part = slice(block * LANES, (block + 1) * LANES)
+        halo = halos[block * ROWS : (block + 1) * ROWS]
+        turned = pltpu.roll(halo, HALO, 0)
+        state = jnp.concatenate([turned, jnp.transpose(own_ref[part, :LANES]), turned], axis=0)
+        terms = speed_terms(courant_ref[block : block + 1, :])
         for turn in range(2):
-            state = tile_substep(state, opens, *terms, True)
-        wide_ref[pl.ds(row, ROWS), pl.ds(0, LANES)] = state[0]
-        return carry
-
-    lax.fori_loop(0, modes // ROWS, body, 0, unroll=8)
-
-    advanced = wide_ref[:, :LANES]
-    lifted = jnp.dot(lift_ref[...], advanced.astype(jnp.bfloat16), preferred_element_type=jnp.float32)
-    squared = (lifted * lifted).astype(jnp.bfloat16)
-    source = jnp.dot(back_ref[...], squared, preferred_element_type=jnp.float32)
-    out_ref[...] = wide_ref[:, :LANES] + coupling * source
+            state = row_substep(state, opens, *terms)
+        advanced = jnp.transpose(state[ROWS : ROWS + LANES])
+        own_ref[part, :LANES] = advanced
+        half_ref[part, :LANES] = advanced.astype(jnp.bfloat16)
+
+    lifted = jnp.dot(lift_ref[...], half_ref[:, :LANES], preferred_element_type=jnp.float32)
+    squared_ref[:, :LANES] = (lifted * lifted).astype(jnp.bfloat16)
+    source = jnp.dot(back_ref[...], squared_ref[:, :LANES], preferred_element_type=jnp.float32)
+    out_ref[...] = own_ref[:, :LANES] + coupling * source
 
 
 def tiled_shards(wave_energy, courant, sea_mask, lift_weight, back_weight):
@@ -262,13 +286,12 @@
         middle_kernel,
         out_shape=jax.ShapeDtypeStruct((components, LANES), jnp.float32),
         scratch_shapes=[
-            pltpu.VMEM((components, LANES), jnp.float32),
             pltpu.VMEM((tiles, LANES), jnp.float32),
             pltpu.VMEM((components, 2 * LANES), jnp.float32),
-            pltpu.VMEM((components, 2 * LANES), jnp.float32),
             pltpu.VMEM((components, 2 * LANES), jnp.bfloat16),
+            pltpu.VMEM((lift_weight.shape[0], 2 * LANES), jnp.bfloat16),
         ],
-        compiler_params=pltpu.CompilerParams(vmem_limit_bytes=40 << 20),
+        compiler_params=pltpu.CompilerParams(vmem_limit_bytes=24 << 20),
         name="middle",
     )(state, courant, sea_mask, lift_weight, back_weight)
     return lax.all_to_all(final, "cell", split_axis=0, concat_axis=1, tiled=True)
@@ -277,8 +300,8 @@
 def shards(wave_energy, courant, sea_mask, lift_weight, back_weight):
     devices = lax.axis_size("cell")
     groups, cells = wave_energy.shape
-    whole = cells == devices * LANES and groups % ROWS == 0 and groups * ROWS <= ROWS * LANES
-    whole = whole and courant.shape[0] % LANES == 0 and devices > 1
+    whole = cells == devices * LANES and groups % ROWS == 0 and groups <= LANES
+    whole = whole and courant.shape[0] % LANES == 0 and courant.shape[0] <= LANES * LANES // ROWS
     run = tiled_shards if whole else general_shards
     return run(wave_energy, courant, sea_mask, lift_weight, back_weight)
 

time: 145 us -> 59.2 us (0.41)
  Pallas kernels: 93.6 us -> 7.99 us
    pallas_call x1, Pallas kernels: 86.6 us -> 5.67 us  [tiled_shards(): pl.pallas_call(middle_kernel, out_shape=jax.ShapeDtypeStruct((components,...]
    pallas_call x1, Pallas kernels: 7.01 us -> 2.32 us  [tiled_shards(): pl.pallas_call(start_kernel, out_shape=jax.ShapeDtypeStruct((tiles, group...]
where the time goes in v2:
time: 59.2 us; the launch traced here: 58.9 us
  blocking collectives  45.7 us (77%)
  Pallas kernels  7.99 us (13%)
  local copies, waits for them, and re-layouts  5.14 us (9%)
    all_to_all x1, blocking collectives, tiled_shards(): lax.all_to_all(start, 'cell', split_axis=0, concat_axis=0, tiled=True)  25.4 us
    all_to_all x1, blocking collectives, tiled_shards(): lax.all_to_all(final, 'cell', split_axis=0, concat_axis=1, tiled=True)  20.3 us
    pallas_call x1, Pallas kernels, tiled_shards(): pl.pallas_call(middle_kernel, out_shape=jax.ShapeDtypeStruct((components,...  5.67 us
    unnamed x14, local copies, waits for them, and re-layouts  4.28 us
    pallas_call x1, Pallas kernels, tiled_shards(): pl.pallas_call(start_kernel, out_shape=jax.ShapeDtypeStruct((tiles, group...  2.32 us

profile of v2, /device:TPU:0, one launch (start us, length us, event | category | flops | bytes accessed | tf_op | source)
XLA Modules:
  0.0 58.9 jit_solution(9551683092371455176)
XLA Ops:
  0.0 0.0 copy-start
  0.0 0.0 copy-start.2
  0.0 1.2 %copy-done.2 = f32[72,2048]{1,0:T(8,128)S(1)} copy-done((f32[72,2048]{1,0:T(8,128)S(1)}, f32[72,2048]{1,0:T(8,128)}, u32[]{:S(2)}) %copy-start.2) | copy-done | bytes 589848
  1.2 0.0 copy-start.3
  1.2 0.7 %copy-done.3 = f32[1152]{0:T(1024)S(1)} copy-done((f32[1152]{0:T(1024)S(1)}, f32[1152]{0:T(1024)}, u32[]{:S(2)}) %copy-start.3) | copy-done | bytes 4632
  1.9 0.0 copy-start.5
  1.9 0.7 %copy-done.5 = s32[2048]{0:T(1024)S(1)} copy-done((s32[2048]{0:T(1024)S(1)}, s32[2048]{0:T(1024)}, u32[]{:S(2)}) %copy-start.5) | copy-done | bytes 8216
  2.6 0.0 copy-start.4
  2.6 0.0 copy-start.6
  2.6 2.3 %start.1 = f32[16,80,128]{2,1,0:T(8,128)S(1)} custom-call(f32[72,2048]{1,0:T(8,128)S(1)} %copy-done.2, f32[9,128]{1,0:T(8,128)S(1)} %bitcast.10, s32[16,128]{1,0:T(8,128)S(1)} %bitcast.12), custom_call_target="tpu_custom_call" | custom-call | tf_op jit(solution)/shard_map/start/pallas_call | solution.py:274
  4.9 25.4 %all_to_all.24.state_ref = f32[16,80,128]{2,1,0:T(8,128)S(1)} all-to-all(f32[16,80,128]{2,1,0:T(8,128)S(1)} %start.1), channel_id=1, replica_groups=mesh['member'=2,'cell'=16] {'cell'}, dimensions={0} | all-to-all | bytes 1310720 | tf_op jit(solution)/shard_map/all_to_all | solution.py:284
  30.3 0.0 copy-done
  30.3 0.0 copy-done.4
  30.3 0.0 copy-done.6
  30.3 0.0 copy-start.1
  30.4 1.7 %copy-done.1 = bf16[1152,1024]{1,0:T(8,128)(2,1)S(1)} copy-done((bf16[1152,1024]{1,0:T(8,128)(2,1)S(1)}, bf16[1152,1024]{1,0:T(8,128)(2,1)}, u32[]{:S(2)}) %copy-start.1) | copy-done | bytes 2359320
  32.0 5.7 %middle.1 = f32[1152,128]{1,0:T(8,128)S(1)} custom-call(f32[16,80,128]{2,1,0:T(8,128)S(1)} %all_to_all.24.state_ref, f32[9,128]{1,0:T(8,128)S(1)} %bitcast.11, s32[16,128]{1,0:T(8,128)S(1)} %bitcast.13, bf16[1024,1152]{1,0:T(8,128)(2,1)S(1)} %copy-done, bf16[1152,1024]{1,0:T(8,128)(2,1)S(1)} %copy-done.1), custom_call_target="tpu_custom_call" | custom-call | tf_op jit(solution)/shard_map/middle/pallas_call | solution.py:285
  37.7 20.3 %all_to_all.25 = f32[16,72,128]{2,1,0:T(8,128)S(1)} all-to-all(f32[16,72,128]{2,1,0:T(8,128)S(1)} %bitcast.9), channel_id=1, replica_groups=mesh['member'=2,'cell'=16] {'cell'}, dimensions={0} | all-to-all | bytes 1179648 | tf_op jit(solution)/shard_map/all_to_all | solution.py:297
  58.0 0.9 %copy_bitcast_fusion = f32[72,2048]{1,0:T(8,128)} fusion(f32[16,72,128]{2,1,0:T(8,128)S(1)} %all_to_all.25), kind=kLoop, calls=%fused_computation | loop fusion | bytes 1179648 | tf_op jit(solution)/shard_map/all_to_all | solution.py:297
Async XLA Ops:
  0.0 30.3 %copy-start = (bf16[1024,1152]{1,0:T(8,128)(2,1)S(1)}, bf16[1024,1152]{1,0:T(8,128)(2,1)}, u32[]{:S(2)}) copy-start(bf16[1024,1152]{1,0:T(8,128)(2,1)} %lift_ref.1) | copy-start | bytes 7077892
  0.0 1.2 %copy-start.2 = (f32[72,2048]{1,0:T(8,128)S(1)}, f32[72,2048]{1,0:T(8,128)}, u32[]{:S(2)}) copy-start(f32[72,2048]{1,0:T(8,128)} %energy_ref.1) | copy-start | bytes 1769476
  1.2 0.7 %copy-start.3 = (f32[1152]{0:T(1024)S(1)}, f32[1152]{0:T(1024)}, u32[]{:S(2)}) copy-start(f32[1152]{0:T(1024)} %param.6) | copy-start | bytes 13828
  1.9 0.7 %copy-start.5 = (s32[2048]{0:T(1024)S(1)}, s32[2048]{0:T(1024)}, u32[]{:S(2)}) copy-start(s32[2048]{0:T(1024)} %param.7) | copy-start | bytes 24580
  2.6 27.7 %copy-start.4 = (f32[1152]{0:T(1024)S(1)}, f32[1152]{0:T(1024)}, u32[]{:S(2)}) copy-start(f32[1152]{0:T(1024)} %param.6) | copy-start | bytes 13828
  2.6 27.7 %copy-start.6 = (s32[2048]{0:T(1024)S(1)}, s32[2048]{0:T(1024)}, u32[]{:S(2)}) copy-start(s32[2048]{0:T(1024)} %param.7) | copy-start | bytes 24580
  30.3 1.7 %copy-start.1 = (bf16[1152,1024]{1,0:T(8,128)(2,1)S(1)}, bf16[1152,1024]{1,0:T(8,128)(2,1)}, u32[]{:S(2)}) copy-start(bf16[1152,1024]{1,0:T(8,128)(2,1)} %back_ref.1) | copy-start | bytes 7077892

commit v3 on v2

--- a/solution.py
+++ b/solution.py
@@ -148,38 +148,65 @@
     return sea * jnp.where(lane_index(sea.shape) == LANES - 1, below, turned)
 
 
-START_ROWS = 24
-
-
-def start_kernel(energy_ref, courant_ref, sea_ref, out_ref, speeds_ref, faces_ref):
-    groups = energy_ref.shape[0]
+def start_rows(rank, state, speeds_ref, faces_ref, out_ref, halo_ref, first_row, groups):
     tiles = out_ref.shape[0]
-    rank = lax.axis_index("cell")
-    spread_speeds(courant_ref, speeds_ref)
-    faces_ref[...] = face_rows(sea_ref)
-    out_ref[:, groups:, :] = jnp.zeros((tiles, ROWS, LANES), jnp.float32)
+    rows = state[0].shape[0]
+    own = pl.multiple_of(rank * groups + first_row, ROWS)
+    terms = speed_terms(speeds_ref[pl.ds(own, rows), :])
+    opens = [faces_ref[tile : tile + 1, :] for tile in range(tiles)]
+    for turn in range(2):
+        state = tile_substep(state, opens, *terms, False)
     lane = lane_index((ROWS, LANES))
     zero = jnp.zeros((ROWS, LANES), jnp.float32)
-    rows = max(r for r in range(ROWS, START_ROWS + 1, ROWS) if groups % r == 0)
-
-    for base in range(0, groups, rows):
-        own = pl.multiple_of(rank * groups + base, ROWS)
-        terms = speed_terms(speeds_ref[pl.ds(own, rows), :])
-        state = [energy_ref[base : base + rows, pl.ds(tile * LANES, LANES)] for tile in range(tiles)]
-        opens = [faces_ref[tile : tile + 1, :] for tile in range(tiles)]
-        for turn in range(2):
-            state = tile_substep(state, opens, *terms, False)
-        for tile in range(tiles):
-            out_ref[tile, base : base + rows, :] = state[tile]
-        for row in range(base, base + rows, ROWS):
-            part = slice(row - base, row - base + ROWS)
+    for tile in range(tiles):
+        out_ref[tile, :rows, :] = state[tile]
+    for tile in range(tiles):
+        halo = halo_ref[tile]
+        for row in range(first_row, first_row + rows, ROWS):
+            part = slice(row - first_row, row - first_row + ROWS)
             mine = (lane >= row) & (lane < row + ROWS)
-            for tile in range(tiles):
-                right = state[tile + 1][part] if tile + 1 < tiles else zero
-                left = state[tile - 1][part] if tile else zero
-                edges = pltpu.roll(jnp.where(lane < LANES // 2, right, left), row + HALO, 1)
-                halo = out_ref[tile, groups:, :]
-                out_ref[tile, groups:, :] = jnp.where(mine, edges, halo)
+            right = state[tile + 1][part] if tile + 1 < tiles else zero
+            left = state[tile - 1][part] if tile else zero
+            edges = pltpu.roll(jnp.where(lane < LANES // 2, right, left), row + HALO, 1)
+            halo = jnp.where(mine, edges, halo)
+        halo_ref[tile] = halo
+
+
+def start_kernel(
+    energy_hbm, courant_hbm, sea_hbm, out_ref, halo_ref, speeds_ref, faces_ref,
+    energy_ref, courant_ref, sea_ref, sems,
+):
+    groups, rows = energy_hbm.shape[0], energy_ref.shape[0]
+    copies = [
+        pltpu.make_async_copy(courant_hbm, courant_ref, sems.at[0]),
+        pltpu.make_async_copy(sea_hbm, sea_ref, sems.at[1]),
+        pltpu.make_async_copy(energy_hbm.at[pl.ds(0, rows), :], energy_ref, sems.at[2]),
+    ]
+    for copy in copies:
+        copy.start()
+    tiles = out_ref.shape[0]
+    halo_ref[...] = jnp.zeros(halo_ref.shape, jnp.float32)
+    copies[0].wait()
+    spread_speeds(courant_ref, speeds_ref)
+    copies[1].wait()
+    faces_ref[...] = face_rows(sea_ref)
+    copies[2].wait()
+    state = [energy_ref[:, tile * LANES : (tile + 1) * LANES] for tile in range(tiles)]
+    start_rows(lax.axis_index("cell"), state, speeds_ref, faces_ref, out_ref, halo_ref, 0, groups)
+
+
+def second_kernel(energy_hbm, first_halo_ref, speeds_ref, faces_ref, out_ref, energy_ref, sem):
+    groups, rows = energy_hbm.shape[0], energy_ref.shape[0]
+    copy = pltpu.make_async_copy(energy_hbm.at[pl.ds(groups - rows, rows), :], energy_ref, sem)
+    copy.start()
+    out_ref[:, rows:, :] = first_halo_ref[...]
+    tiles = out_ref.shape[0]
+    copy.wait()
+    state = [energy_ref[:, tile * LANES : (tile + 1) * LANES] for tile in range(tiles)]
+    halo_ref = out_ref.at[:, rows:, :]
+    start_rows(
+        lax.axis_index("cell"), state, speeds_ref, faces_ref, out_ref, halo_ref, groups - rows, groups
+    )
 
 
 def row_index(shape):
@@ -199,18 +226,19 @@
 
 
 def middle_kernel(
-    state_ref, courant_ref, sea_ref, lift_ref, back_ref, out_ref,
-    faces_ref, own_ref, half_ref, squared_ref,
+    first_ref, second_ref, courant_ref, faces_ref, lift_ref, back_hbm, out_ref,
+    back_ref, own_ref, half_ref, squared_ref, sem,
 ):
-    sources, rows, _ = state_ref.shape
-    groups = rows - ROWS
+    copy = pltpu.make_async_copy(back_hbm, back_ref, sem)
+    copy.start()
+    sources, split, _ = first_ref.shape
+    groups = split + second_ref.shape[1] - ROWS
     modes = sources * groups
     blocks = modes // LANES
     rank = lax.axis_index("cell")
     tiles = faces_ref.shape[0]
     lane = lane_index((LANES, LANES))
 
-    faces_ref[...] = face_rows(sea_ref)
     own_faces = faces_ref[pl.ds(rank, 1), :]
     after_faces = faces_ref[pl.ds(jnp.minimum(rank + 1, tiles - 1), 1), :]
     before_faces = faces_ref[pl.ds(jnp.maximum(rank - 1, 0), 1), :]
@@ -226,17 +254,21 @@
     opens = jnp.broadcast_to(column, (LANES + 2 * ROWS, LANES))
 
     for source in range(sources):
-        halo = state_ref[source, groups:, :]
+        halo = second_ref[source, groups - split :, :]
         for group in range(groups // ROWS):
             row = source * groups + group * ROWS
-            own = state_ref[source, group * ROWS : (group + 1) * ROWS, :]
-            shift = -group * ROWS % LANES
+            lead = group * ROWS
+            from_first = lead < split
+            ref, at = (first_ref, lead) if from_first else (second_ref, lead - split)
+            own = ref[source, at : at + ROWS, :]
+            shift = -lead % LANES
             own_ref[row : row + ROWS, :LANES] = own
             own_ref[row : row + ROWS, LANES:] = pltpu.roll(halo, shift, 1) if shift else halo
     half_ref[...] = own_ref[...].astype(jnp.bfloat16)
 
     lifted = jnp.dot(lift_ref[...], half_ref[...], preferred_element_type=jnp.float32)
     squared_ref[...] = (lifted * lifted).astype(jnp.bfloat16)
+    copy.wait()
     own_ref[...] += coupling * jnp.dot(
         back_ref[...], squared_ref[...], preferred_element_type=jnp.float32
     )
@@ -271,29 +303,57 @@
     components, tiles = courant.shape[0], cells // LANES
     courant = courant.reshape(components // LANES, LANES)
     sea_mask = sea_mask.reshape(tiles, LANES)
-    start = pl.pallas_call(
+    split = min(-(-groups // (2 * ROWS)) * ROWS + ROWS * (groups % (2 * ROWS) == 0), groups - ROWS)
+    rest = groups - split
+    f32 = jnp.float32
+    hbm = pl.BlockSpec(memory_space=pltpu.HBM)
+    vmem = pl.BlockSpec(memory_space=pltpu.VMEM)
+    first, first_halo, speeds, faces = pl.pallas_call(
         start_kernel,
-        out_shape=jax.ShapeDtypeStruct((tiles, groups + ROWS, LANES), jnp.float32),
+        out_shape=[
+            jax.ShapeDtypeStruct((tiles, split, LANES), f32),
+            jax.ShapeDtypeStruct((tiles, ROWS, LANES), f32),
+            jax.ShapeDtypeStruct((components, LANES), f32),
+            jax.ShapeDtypeStruct((tiles, LANES), f32),
+        ],
+        in_specs=[hbm] * 3,
+        out_specs=[vmem] * 4,
         scratch_shapes=[
-            pltpu.VMEM((components, LANES), jnp.float32),
-            pltpu.VMEM((tiles, LANES), jnp.float32),
+            pltpu.VMEM((split, cells), f32),
+            pltpu.VMEM(courant.shape, f32),
+            pltpu.VMEM(sea_mask.shape, sea_mask.dtype),
+            pltpu.SemaphoreType.DMA((3,)),
         ],
         compiler_params=pltpu.CompilerParams(vmem_limit_bytes=16 << 20),
         name="start",
     )(wave_energy, courant, sea_mask)
-    state = lax.all_to_all(start, "cell", split_axis=0, concat_axis=0, tiled=True)
+    first = lax.all_to_all(first, "cell", split_axis=0, concat_axis=0, tiled=True)
+    second = pl.pallas_call(
+        second_kernel,
+        out_shape=jax.ShapeDtypeStruct((tiles, rest + ROWS, LANES), f32),
+        in_specs=[hbm] + [vmem] * 3,
+        out_specs=vmem,
+        scratch_shapes=[pltpu.VMEM((rest, cells), f32), pltpu.SemaphoreType.DMA],
+        compiler_params=pltpu.CompilerParams(vmem_limit_bytes=16 << 20),
+        cost_estimate=pl.CostEstimate(flops=40 * rest * cells, bytes_accessed=8 * rest * cells, transcendentals=0),
+        name="second",
+    )(wave_energy, first_halo, speeds, faces)
+    second = lax.all_to_all(second, "cell", split_axis=0, concat_axis=0, tiled=True)
     final = pl.pallas_call(
         middle_kernel,
-        out_shape=jax.ShapeDtypeStruct((components, LANES), jnp.float32),
+        out_shape=jax.ShapeDtypeStruct((components, LANES), f32),
+        in_specs=[vmem] * 5 + [hbm],
+        out_specs=vmem,
         scratch_shapes=[
-            pltpu.VMEM((tiles, LANES), jnp.float32),
-            pltpu.VMEM((components, 2 * LANES), jnp.float32),
+            pltpu.VMEM(back_weight.shape, back_weight.dtype),
+            pltpu.VMEM((components, 2 * LANES), f32),
             pltpu.VMEM((components, 2 * LANES), jnp.bfloat16),
             pltpu.VMEM((lift_weight.shape[0], 2 * LANES), jnp.bfloat16),
+            pltpu.SemaphoreType.DMA,
         ],
-        compiler_params=pltpu.CompilerParams(vmem_limit_bytes=24 << 20),
+        compiler_params=pltpu.CompilerParams(vmem_limit_bytes=50 << 20),
         name="middle",
-    )(state, courant, sea_mask, lift_weight, back_weight)
+    )(first, second, courant, faces, lift_weight, back_weight)
     return lax.all_to_all(final, "cell", split_axis=0, concat_axis=1, tiled=True)
 
 

time: 59.2 us -> 65.7 us (1.11)
  blocking collectives: 45.7 us -> 52.7 us
  local copies, waits for them, and re-layouts: 5.14 us -> 3.33 us
  Pallas kernels: 7.99 us -> 9.24 us
    all_to_all x1 -> x2, blocking collectives: 25.4 us -> 32.4 us  [the longest x1 18.3 us: tiled_shards(): lax.all_to_all(second, 'cell', split_axis=0, concat_axis=0, tiled=True)]
    unnamed x14 -> x10, local copies, waits for them, and re-layouts: 4.28 us -> 2.46 us
    pallas_call x1, Pallas kernels: 5.67 us -> 7.06 us  [tiled_shards(): pl.pallas_call(middle_kernel, out_shape=jax.ShapeDtypeStruct((components,...]
    pallas_call x1 -> x2, Pallas kernels: 2.32 us -> 2.18 us  [the longest x1 1.4 us: tiled_shards(): pl.pallas_call(start_kernel, out_shape=[jax.ShapeDtypeStruct((tiles, spli...]
where the time goes in v3:
time: 65.7 us; the launch traced here: 65.3 us
  blocking collectives  52.7 us (80%)
  Pallas kernels  9.24 us (14%)
  local copies, waits for them, and re-layouts  3.33 us (5%)
    all_to_all x1, blocking collectives, tiled_shards(): lax.all_to_all(final, 'cell', split_axis=0, concat_axis=1, tiled=True)  20.3 us
    all_to_all x1, blocking collectives, tiled_shards(): lax.all_to_all(second, 'cell', split_axis=0, concat_axis=0, tiled=True)  18.3 us
    all_to_all x1, blocking collectives, tiled_shards(): lax.all_to_all(first, 'cell', split_axis=0, concat_axis=0, tiled=True)  14.1 us
    pallas_call x1, Pallas kernels, tiled_shards(): pl.pallas_call(middle_kernel, out_shape=jax.ShapeDtypeStruct((components,...  7.06 us
    unnamed x10, local copies, waits for them, and re-layouts  2.46 us
    pallas_call x1, Pallas kernels, tiled_shards(): pl.pallas_call(start_kernel, out_shape=[jax.ShapeDtypeStruct((tiles, spli...  1.4 us

profile of v3, /device:TPU:0, one launch (start us, length us, event | category | flops | bytes accessed | tf_op | source)
XLA Modules:
  0.0 65.3 jit_solution(11299004208018273349)
XLA Ops:
  0.0 0.0 copy-start
  0.0 1.1 %copy-done = f32[72,2048]{1,0:T(8,128)S(1)} copy-done((f32[72,2048]{1,0:T(8,128)S(1)}, f32[72,2048]{1,0:T(8,128)}, u32[]{:S(2)}) %copy-start) | copy-done | bytes 589848
  1.1 0.0 copy-start.2
  1.1 0.7 %copy-done.2 = f32[1152]{0:T(1024)S(1)} copy-done((f32[1152]{0:T(1024)S(1)}, f32[1152]{0:T(1024)}, u32[]{:S(2)}) %copy-start.2) | copy-done | bytes 4632
  1.8 0.0 copy-start.4
  1.8 0.7 %copy-done.4 = s32[2048]{0:T(1024)S(1)} copy-done((s32[2048]{0:T(1024)S(1)}, s32[2048]{0:T(1024)}, u32[]{:S(2)}) %copy-start.4) | copy-done | bytes 8216
  2.5 0.0 copy-start.1
  2.5 0.0 copy-start.3
  2.5 1.4 %start.1 = (f32[16,40,128]{2,1,0:T(8,128)S(1)}, f32[16,8,128]{2,1,0:T(8,128)S(1)}, f32[1152,128]{1,0:T(8,128)S(1)}, f32[16,128]{1,0:T(8,128)S(1)}) custom-call(f32[72,2048]{1,0:T(8,128)S(1)} %copy-done, f32[9,128]{1,0:T(8,128)S(1)} %bitcast.10, s32[16,128]{1,0:T(8,128)S(1)} %bitcast.12), custom_call_target="tpu_custom_call" | custom-call | tf_op jit(solution)/shard_map/start/pallas_call | solution.py:311
  3.9 0.8 %second.1 = f32[16,40,128]{2,1,0:T(8,128)S(1)} custom-call(f32[72,2048]{1,0:T(8,128)S(1)} %copy-done, f32[16,8,128]{2,1,0:T(8,128)S(1)} %get-tuple-element.10.first_halo_ref, f32[1152,128]{1,0:T(8,128)S(1)} %get-tuple-element.11.speeds_ref, f32[16,128]{1,0:T(8,128)S(1)} %get-tuple-element.12.faces_ref), custom_call_target="tpu_custom_call" | custom-call | flops 2621440 | bytes 524288 | tf_op jit(solution)/shard_map/second/pallas_call | solution.py:331
  4.7 18.3 %all_to_all.29.second_ref = f32[16,40,128]{2,1,0:T(8,128)S(1)} all-to-all(f32[16,40,128]{2,1,0:T(8,128)S(1)} %second.1), channel_id=1, replica_groups=mesh['member'=2,'cell'=16] {'cell'}, dimensions={0} | all-to-all | bytes 655360 | tf_op jit(solution)/shard_map/all_to_all | solution.py:341
  22.9 14.1 %all_to_all.30.first_ref = f32[16,40,128]{2,1,0:T(8,128)S(1)} all-to-all(f32[16,40,128]{2,1,0:T(8,128)S(1)} %get-tuple-element.9), channel_id=1, replica_groups=mesh['member'=2,'cell'=16] {'cell'}, dimensions={0} | all-to-all | bytes 655360 | tf_op jit(solution)/shard_map/all_to_all | solution.py:330
  37.0 0.0 copy-done.1
  37.0 0.0 copy-done.3
  37.0 7.1 %middle.1 = f32[1152,128]{1,0:T(8,128)S(1)} custom-call(f32[16,40,128]{2,1,0:T(8,128)S(1)} %all_to_all.30.first_ref, f32[16,40,128]{2,1,0:T(8,128)S(1)} %all_to_all.29.second_ref, f32[9,128]{1,0:T(8,128)S(1)} %bitcast.11, f32[16,128]{1,0:T(8,128)S(1)} %get-tuple-element.12.faces_ref, bf16[1024,1152]{1,0:T(8,128)(2,1)S(1)} %copy-done.1, ...), custom_call_target="tpu_custom_call" | custom-call | tf_op jit(solution)/shard_map/middle/pallas_call | solution.py:342
  44.1 20.3 %all_to_all.31 = f32[16,72,128]{2,1,0:T(8,128)S(1)} all-to-all(f32[16,72,128]{2,1,0:T(8,128)S(1)} %bitcast.9), channel_id=1, replica_groups=mesh['member'=2,'cell'=16] {'cell'}, dimensions={0} | all-to-all | bytes 1179648 | tf_op jit(solution)/shard_map/all_to_all | solution.py:357
  64.4 0.9 %copy_bitcast_fusion = f32[72,2048]{1,0:T(8,128)} fusion(f32[16,72,128]{2,1,0:T(8,128)S(1)} %all_to_all.31), kind=kLoop, calls=%fused_computation | loop fusion | bytes 1179648 | tf_op jit(solution)/shard_map/all_to_all | solution.py:357
Async XLA Ops:
  0.0 1.1 %copy-start = (f32[72,2048]{1,0:T(8,128)S(1)}, f32[72,2048]{1,0:T(8,128)}, u32[]{:S(2)}) copy-start(f32[72,2048]{1,0:T(8,128)} %energy_hbm.3) | copy-start | bytes 1769476
  1.1 0.7 %copy-start.2 = (f32[1152]{0:T(1024)S(1)}, f32[1152]{0:T(1024)}, u32[]{:S(2)}) copy-start(f32[1152]{0:T(1024)} %param.6) | copy-start | bytes 13828
  1.8 0.7 %copy-start.4 = (s32[2048]{0:T(1024)S(1)}, s32[2048]{0:T(1024)}, u32[]{:S(2)}) copy-start(s32[2048]{0:T(1024)} %param.7) | copy-start | bytes 24580
  2.5 34.6 %copy-start.1 = (bf16[1024,1152]{1,0:T(8,128)(2,1)S(1)}, bf16[1024,1152]{1,0:T(8,128)(2,1)}, u32[]{:S(2)}) copy-start(bf16[1024,1152]{1,0:T(8,128)(2,1)} %lift_ref.1) | copy-start | bytes 7077892
  2.5 34.6 %copy-start.3 = (f32[1152]{0:T(1024)S(1)}, f32[1152]{0:T(1024)}, u32[]{:S(2)}) copy-start(f32[1152]{0:T(1024)} %param.6) | copy-start | bytes 13828

commit v4 on v2

--- a/solution.py
+++ b/solution.py
@@ -140,8 +140,7 @@
         )
 
 
-def face_rows(sea_ref):
-    sea = sea_ref[...].astype(jnp.float32)
+def face_rows(sea):
     tiles = sea.shape[0]
     turned = pltpu.roll(sea, LANES - 1, 1)
     below = jnp.concatenate([turned[1:], jnp.zeros((1, LANES), jnp.float32)], axis=0)
@@ -151,35 +150,77 @@
 START_ROWS = 24
 
 
-def start_kernel(energy_ref, courant_ref, sea_ref, out_ref, speeds_ref, faces_ref):
-    groups = energy_ref.shape[0]
+def start_rows(state, speed, faces_ref, out_ref, base, groups):
     tiles = out_ref.shape[0]
-    rank = lax.axis_index("cell")
-    spread_speeds(courant_ref, speeds_ref)
-    faces_ref[...] = face_rows(sea_ref)
-    out_ref[:, groups:, :] = jnp.zeros((tiles, ROWS, LANES), jnp.float32)
+    rows = state[0].shape[0]
+    terms = speed_terms(speed)
+    opens = [faces_ref[tile : tile + 1, :] for tile in range(tiles)]
+    for turn in range(2):
+        state = tile_substep(state, opens, *terms, False)
     lane = lane_index((ROWS, LANES))
     zero = jnp.zeros((ROWS, LANES), jnp.float32)
-    rows = max(r for r in range(ROWS, START_ROWS + 1, ROWS) if groups % r == 0)
-
-    for base in range(0, groups, rows):
-        own = pl.multiple_of(rank * groups + base, ROWS)
-        terms = speed_terms(speeds_ref[pl.ds(own, rows), :])
-        state = [energy_ref[base : base + rows, pl.ds(tile * LANES, LANES)] for tile in range(tiles)]
-        opens = [faces_ref[tile : tile + 1, :] for tile in range(tiles)]
-        for turn in range(2):
-            state = tile_substep(state, opens, *terms, False)
-        for tile in range(tiles):
-            out_ref[tile, base : base + rows, :] = state[tile]
+    for tile in range(tiles):
+        out_ref[tile, base : base + rows, :] = state[tile]
+        halo = out_ref[tile, groups:, :]
         for row in range(base, base + rows, ROWS):
             part = slice(row - base, row - base + ROWS)
             mine = (lane >= row) & (lane < row + ROWS)
-            for tile in range(tiles):
-                right = state[tile + 1][part] if tile + 1 < tiles else zero
-                left = state[tile - 1][part] if tile else zero
-                edges = pltpu.roll(jnp.where(lane < LANES // 2, right, left), row + HALO, 1)
-                halo = out_ref[tile, groups:, :]
-                out_ref[tile, groups:, :] = jnp.where(mine, edges, halo)
+            right = state[tile + 1][part] if tile + 1 < tiles else zero
+            left = state[tile - 1][part] if tile else zero
+            edges = pltpu.roll(jnp.where(lane < LANES // 2, right, left), row + HALO, 1)
+            halo = jnp.where(mine, edges, halo)
+        out_ref[tile, groups:, :] = halo
+
+
+def start_kernel(
+    energy_hbm, courant_hbm, sea_hbm, back_hbm, out_ref, courant_ref, faces_ref, back_ref,
+    energy_ref, sea_ref, speeds_ref, sems, energy_sems,
+):
+    groups = energy_ref.shape[0]
+    tiles = out_ref.shape[0]
+    rows = max(r for r in range(ROWS, START_ROWS + 1, ROWS) if groups % r == 0)
+    small = pltpu.make_async_copy(courant_hbm, courant_ref, sems.at[0])
+    sea = pltpu.make_async_copy(sea_hbm, sea_ref, sems.at[1])
+    weights = pltpu.make_async_copy(back_hbm, back_ref, sems.at[2])
+    state_copies = [
+        pltpu.make_async_copy(
+            energy_hbm.at[pl.ds(base, rows), :], energy_ref.at[pl.ds(base, rows), :], energy_sems.at[step]
+        )
+        for step, base in enumerate(range(0, groups, rows))
+    ]
+    small.start()
+    sea.start()
+    for copy in state_copies:
+        copy.start()
+    weights.start()
+    out_ref[:, groups:, :] = jnp.zeros((tiles, ROWS, LANES), jnp.float32)
+    small.wait()
+    spread_speeds(courant_ref, speeds_ref)
+    sea.wait()
+    faces_ref[...] = face_rows(sea_ref[...].astype(jnp.float32))
+    rank = lax.axis_index("cell")
+    for step, base in enumerate(range(0, groups, rows)):
+        own = pl.multiple_of(rank * groups + base, ROWS)
+        speed = speeds_ref[pl.ds(own, rows), :]
+        state_copies[step].wait()
+        state = [
+            energy_ref[base : base + rows, tile * LANES : (tile + 1) * LANES] for tile in range(tiles)
+        ]
+        start_rows(state, speed, faces_ref, out_ref, base, groups)
+    weights.wait()
+
+
+def final_kernel(blocks_ref, out_hbm, sems):
+    copies = [
+        pltpu.make_async_copy(
+            blocks_ref.at[tile], out_hbm.at[:, pl.ds(tile * LANES, LANES)], sems.at[tile]
+        )
+        for tile in range(blocks_ref.shape[0])
+    ]
+    for copy in copies:
+        copy.start()
+    for copy in copies:
+        copy.wait()
 
 
 def row_index(shape):
@@ -199,8 +240,7 @@
 
 
 def middle_kernel(
-    state_ref, courant_ref, sea_ref, lift_ref, back_ref, out_ref,
-    faces_ref, own_ref, half_ref, squared_ref,
+    state_ref, courant_ref, faces_ref, lift_ref, back_ref, out_ref, own_ref, half_ref, squared_ref
 ):
     sources, rows, _ = state_ref.shape
     groups = rows - ROWS
@@ -208,22 +248,6 @@
     blocks = modes // LANES
     rank = lax.axis_index("cell")
     tiles = faces_ref.shape[0]
-    lane = lane_index((LANES, LANES))
-
-    faces_ref[...] = face_rows(sea_ref)
-    own_faces = faces_ref[pl.ds(rank, 1), :]
-    after_faces = faces_ref[pl.ds(jnp.minimum(rank + 1, tiles - 1), 1), :]
-    before_faces = faces_ref[pl.ds(jnp.maximum(rank - 1, 0), 1), :]
-    after_faces = jnp.where(rank < tiles - 1, after_faces, 0.0)
-    before_faces = jnp.where(rank > 0, before_faces, 0.0)
-    square = jnp.concatenate(
-        [own_faces, before_faces, after_faces, jnp.zeros((LANES - 3, LANES), jnp.float32)], axis=0
-    )
-    turned = jnp.transpose(square)
-    column = jnp.concatenate(
-        [turned[LANES - ROWS :, 1:2], turned[:, 0:1], turned[:ROWS, 2:3]], axis=0
-    )
-    opens = jnp.broadcast_to(column, (LANES + 2 * ROWS, LANES))
 
     for source in range(sources):
         halo = state_ref[source, groups:, :]
@@ -237,32 +261,39 @@
 
     lifted = jnp.dot(lift_ref[...], half_ref[...], preferred_element_type=jnp.float32)
     squared_ref[...] = (lifted * lifted).astype(jnp.bfloat16)
-    own_ref[...] += coupling * jnp.dot(
-        back_ref[...], squared_ref[...], preferred_element_type=jnp.float32
-    )
-
-    merged = jnp.zeros((LANES, LANES), jnp.float32)
-    for block in range(blocks):
-        here = own_ref[block * LANES : (block + 1) * LANES, LANES:]
-        here = pltpu.roll(here, block * ROWS, 1) if block else here
-        merged = jnp.where((lane >= block * ROWS) & (lane < (block + 1) * ROWS), here, merged)
-    halos = jnp.transpose(merged)
+
+    own_faces = faces_ref[pl.ds(rank, 1), :]
+    after_faces = faces_ref[pl.ds(jnp.minimum(rank + 1, tiles - 1), 1), :]
+    before_faces = faces_ref[pl.ds(jnp.maximum(rank - 1, 0), 1), :]
+    after_faces = jnp.where(rank < tiles - 1, after_faces, 0.0)
+    before_faces = jnp.where(rank > 0, before_faces, 0.0)
+    square = jnp.concatenate(
+        [own_faces, before_faces, after_faces, jnp.zeros((LANES - 3, LANES), jnp.float32)], axis=0
+    )
+    turned = jnp.transpose(square)
+    column = jnp.concatenate(
+        [turned[LANES - ROWS :, 1:2], turned[:, 0:1], turned[:ROWS, 2:3]], axis=0
+    )
+    opens = jnp.broadcast_to(column, (LANES + 2 * ROWS, LANES))
+
     for block in range(blocks):
         part = slice(block * LANES, (block + 1) * LANES)
-        halo = halos[block * ROWS : (block + 1) * ROWS]
-        turned = pltpu.roll(halo, HALO, 0)
-        state = jnp.concatenate([turned, jnp.transpose(own_ref[part, :LANES]), turned], axis=0)
+        state = own_ref[part, :] + coupling * jnp.dot(
+            back_ref[part, :], squared_ref[...], preferred_element_type=jnp.float32
+        )
+        halo = pltpu.roll(jnp.transpose(state[:, LANES:])[:ROWS], HALO, 0)
+        state = jnp.concatenate([halo, jnp.transpose(state[:, :LANES]), halo], axis=0)
         terms = speed_terms(courant_ref[block : block + 1, :])
         for turn in range(2):
             state = row_substep(state, opens, *terms)
         advanced = jnp.transpose(state[ROWS : ROWS + LANES])
-        own_ref[part, :LANES] = advanced
+        out_ref[part, :] = advanced
         half_ref[part, :LANES] = advanced.astype(jnp.bfloat16)
 
     lifted = jnp.dot(lift_ref[...], half_ref[:, :LANES], preferred_element_type=jnp.float32)
     squared_ref[:, :LANES] = (lifted * lifted).astype(jnp.bfloat16)
     source = jnp.dot(back_ref[...], squared_ref[:, :LANES], preferred_element_type=jnp.float32)
-    out_ref[...] = own_ref[:, :LANES] + coupling * source
+    out_ref[...] += coupling * source
 
 
 def tiled_shards(wave_energy, courant, sea_mask, lift_weight, back_weight):
@@ -271,30 +302,53 @@
     components, tiles = courant.shape[0], cells // LANES
     courant = courant.reshape(components // LANES, LANES)
     sea_mask = sea_mask.reshape(tiles, LANES)
-    start = pl.pallas_call(
+    f32 = jnp.float32
+    any_space = pl.BlockSpec(memory_space=pl.ANY)
+    vmem = pl.BlockSpec(memory_space=pltpu.VMEM)
+    inputs = (wave_energy, courant, sea_mask, back_weight)
+    start, courant, faces, back_weight = pl.pallas_call(
         start_kernel,
-        out_shape=jax.ShapeDtypeStruct((tiles, groups + ROWS, LANES), jnp.float32),
+        out_shape=[
+            jax.ShapeDtypeStruct((tiles, groups + ROWS, LANES), f32),
+            jax.ShapeDtypeStruct(courant.shape, f32),
+            jax.ShapeDtypeStruct((tiles, LANES), f32),
+            jax.ShapeDtypeStruct(back_weight.shape, back_weight.dtype),
+        ],
+        in_specs=[any_space] * 4,
+        out_specs=[vmem] * 4,
         scratch_shapes=[
-            pltpu.VMEM((components, LANES), jnp.float32),
-            pltpu.VMEM((tiles, LANES), jnp.float32),
+            pltpu.VMEM((groups, cells), f32),
+            pltpu.VMEM(sea_mask.shape, sea_mask.dtype),
+            pltpu.VMEM((components, LANES), f32),
+            pltpu.SemaphoreType.DMA((3,)),
+            pltpu.SemaphoreType.DMA((groups // ROWS,)),
         ],
         compiler_params=pltpu.CompilerParams(vmem_limit_bytes=16 << 20),
         name="start",
-    )(wave_energy, courant, sea_mask)
+    )(*(pltpu.with_memory_space_constraint(x, pltpu.HBM) for x in inputs))
     state = lax.all_to_all(start, "cell", split_axis=0, concat_axis=0, tiled=True)
     final = pl.pallas_call(
         middle_kernel,
-        out_shape=jax.ShapeDtypeStruct((components, LANES), jnp.float32),
+        out_shape=jax.ShapeDtypeStruct((components, LANES), f32),
         scratch_shapes=[
-            pltpu.VMEM((tiles, LANES), jnp.float32),
-            pltpu.VMEM((components, 2 * LANES), jnp.float32),
+            pltpu.VMEM((components, 2 * LANES), f32),
             pltpu.VMEM((components, 2 * LANES), jnp.bfloat16),
             pltpu.VMEM((lift_weight.shape[0], 2 * LANES), jnp.bfloat16),
         ],
         compiler_params=pltpu.CompilerParams(vmem_limit_bytes=24 << 20),
         name="middle",
-    )(state, courant, sea_mask, lift_weight, back_weight)
-    return lax.all_to_all(final, "cell", split_axis=0, concat_axis=1, tiled=True)
+    )(state, courant, faces, lift_weight, back_weight)
+    final = final.reshape(tiles, groups, LANES)
+    final = lax.all_to_all(final, "cell", split_axis=0, concat_axis=0, tiled=True)
+    return pl.pallas_call(
+        final_kernel,
+        out_shape=jax.ShapeDtypeStruct((groups, cells), f32),
+        in_specs=[vmem],
+        out_specs=any_space,
+        scratch_shapes=[pltpu.SemaphoreType.DMA((tiles,))],
+        compiler_params=pltpu.CompilerParams(vmem_limit_bytes=16 << 20),
+        name="final",
+    )(final)
 
 
 def shards(wave_energy, courant, sea_mask, lift_weight, back_weight):

time: 59.2 us -> 55.5 us (0.938)
  local copies, waits for them, and re-layouts: 5.14 us -> 0.01 us
  Pallas kernels: 7.99 us -> 9.56 us
    unnamed x14 -> x2, local copies, waits for them, and re-layouts: 4.28 us -> 0.01 us
    pallas_call x1 -> x2, Pallas kernels: 2.32 us -> 4.46 us  [the longest x1 3.52 us: tiled_shards(): pl.pallas_call(start_kernel, out_shape=[jax.ShapeDtypeStruct((tiles, grou...]
    all_to_all x1 -> x0, local copies, waits for them, and re-layouts: 0.86 us -> none  [tiled_shards(): lax.all_to_all(final, 'cell', split_axis=0, concat_axis=1, tiled=True)]
where the time goes in v4:
time: 55.5 us; the launch traced here: 55.3 us
  blocking collectives  45.7 us (82%)
  Pallas kernels  9.56 us (17%)
    all_to_all x1, blocking collectives, tiled_shards(): lax.all_to_all(start, 'cell', split_axis=0, concat_axis=0, tiled=True)  25.4 us
    all_to_all x1, blocking collectives, tiled_shards(): lax.all_to_all(final, 'cell', split_axis=0, concat_axis=0, tiled=True)  20.3 us
    pallas_call x1, Pallas kernels, tiled_shards(): pl.pallas_call(middle_kernel, out_shape=jax.ShapeDtypeStruct((components,...  5.1 us
    pallas_call x1, Pallas kernels, tiled_shards(): pl.pallas_call(start_kernel, out_shape=[jax.ShapeDtypeStruct((tiles, grou...  3.52 us

profile of v4, /device:TPU:0, one launch (start us, length us, event | category | flops | bytes accessed | tf_op | source)
XLA Modules:
  0.0 55.3 jit_solution(7835298170194555153)
XLA Ops:
  0.0 0.0 copy-start
  0.0 3.5 %start.1 = (f32[16,80,128]{2,1,0:T(8,128)S(1)}, f32[9,128]{1,0:T(8,128)S(1)}, f32[16,128]{1,0:T(8,128)S(1)}, bf16[1152,1024]{1,0:T(8,128)(2,1)S(1)}) custom-call(f32[72,2048]{1,0:T(8,128)} %energy_hbm.1, f32[9,128]{1,0:T(8,128)} %bitcast.4, s32[16,128]{1,0:T(8,128)} %bitcast.5, bf16[1152,1024]{1,0:T(8,128)(2,1)} %back_hbm.1), custom_call_target="tpu_custom_call" | custom-call | tf_op jit(solution)/shard_map/start/pallas_call | solution.py:309
  3.5 25.4 %all_to_all.10.state_ref = f32[16,80,128]{2,1,0:T(8,128)S(1)} all-to-all(f32[16,80,128]{2,1,0:T(8,128)S(1)} %get-tuple-element.9), channel_id=1, replica_groups=mesh['member'=2,'cell'=16] {'cell'}, dimensions={0} | all-to-all | bytes 1310720 | tf_op jit(solution)/shard_map/all_to_all | solution.py:329
  28.9 0.0 copy-done
  28.9 5.1 %middle.1 = f32[1152,128]{1,0:T(8,128)S(1)} custom-call(f32[16,80,128]{2,1,0:T(8,128)S(1)} %all_to_all.10.state_ref, f32[9,128]{1,0:T(8,128)S(1)} %get-tuple-element.10.courant_ref, f32[16,128]{1,0:T(8,128)S(1)} %get-tuple-element.11.faces_ref, bf16[1024,1152]{1,0:T(8,128)(2,1)S(1)} %copy-done, bf16[1152,1024]{1,0:T(8,128)(2,1)S(1)} %get-tuple-element.12.back_ref), custom_call_target="tpu_custom_call" | custom-call | tf_op jit(solution)/shard_map/middle/pallas_call | solution.py:330
  34.0 20.3 %all_to_all.11.blocks_ref = f32[16,72,128]{2,1,0:T(8,128)S(1)} all-to-all(f32[16,72,128]{2,1,0:T(8,128)S(1)} %bitcast.3), channel_id=1, replica_groups=mesh['member'=2,'cell'=16] {'cell'}, dimensions={0} | all-to-all | bytes 1179648 | tf_op jit(solution)/shard_map/all_to_all | solution.py:342
  54.4 0.9 %final.1 = f32[72,2048]{1,0:T(8,128)} custom-call(f32[16,72,128]{2,1,0:T(8,128)S(1)} %all_to_all.11.blocks_ref), custom_call_target="tpu_custom_call" | custom-call | tf_op jit(solution)/shard_map/final/pallas_call | solution.py:343
Async XLA Ops:
  0.0 28.9 %copy-start = (bf16[1024,1152]{1,0:T(8,128)(2,1)S(1)}, bf16[1024,1152]{1,0:T(8,128)(2,1)}, u32[]{:S(2)}) copy-start(bf16[1024,1152]{1,0:T(8,128)(2,1)} %lift_ref.1) | copy-start | bytes 7077892

commit v5 on v4

--- a/solution.py
+++ b/solution.py
@@ -147,79 +147,77 @@
     return sea * jnp.where(lane_index(sea.shape) == LANES - 1, below, turned)
 
 
-START_ROWS = 24
-
-
-def start_rows(state, speed, faces_ref, out_ref, base, groups):
+START_ROWS = 40
+
+
+def start_rows(state, speed, faces_ref, out_ref, edges_ref, base):
     tiles = out_ref.shape[0]
     rows = state[0].shape[0]
     terms = speed_terms(speed)
     opens = [faces_ref[tile : tile + 1, :] for tile in range(tiles)]
     for turn in range(2):
         state = tile_substep(state, opens, *terms, False)
-    lane = lane_index((ROWS, LANES))
-    zero = jnp.zeros((ROWS, LANES), jnp.float32)
+    lane = lane_index((rows, LANES))
+    edges = jnp.zeros((rows, LANES), jnp.float32)
     for tile in range(tiles):
         out_ref[tile, base : base + rows, :] = state[tile]
-        halo = out_ref[tile, groups:, :]
-        for row in range(base, base + rows, ROWS):
-            part = slice(row - base, row - base + ROWS)
-            mine = (lane >= row) & (lane < row + ROWS)
-            right = state[tile + 1][part] if tile + 1 < tiles else zero
-            left = state[tile - 1][part] if tile else zero
-            edges = pltpu.roll(jnp.where(lane < LANES // 2, right, left), row + HALO, 1)
-            halo = jnp.where(mine, edges, halo)
-        out_ref[tile, groups:, :] = halo
+        mine = (lane >= tile * ROWS) & (lane < (tile + 1) * ROWS)
+        edges = jnp.where(mine, pltpu.roll(state[tile], tile * ROWS + HALO, 1), edges)
+    edges_ref[base : base + rows, :] = edges
 
 
 def start_kernel(
-    energy_hbm, courant_hbm, sea_hbm, back_hbm, out_ref, courant_ref, faces_ref, back_ref,
-    energy_ref, sea_ref, speeds_ref, sems, energy_sems,
+    energy_hbm, courant_hbm, sea_hbm, lift_hbm, back_hbm,
+    out_ref, courant_ref, faces_ref, lift_ref, back_ref,
+    energy_ref, sea_ref, speeds_ref, edges_ref, sems, energy_sems,
 ):
     groups = energy_ref.shape[0]
     tiles = out_ref.shape[0]
-    rows = max(r for r in range(ROWS, START_ROWS + 1, ROWS) if groups % r == 0)
+    bases = list(range(0, groups, START_ROWS))
+    sizes = [min(START_ROWS, groups - base) for base in bases]
     small = pltpu.make_async_copy(courant_hbm, courant_ref, sems.at[0])
     sea = pltpu.make_async_copy(sea_hbm, sea_ref, sems.at[1])
-    weights = pltpu.make_async_copy(back_hbm, back_ref, sems.at[2])
+    weights = [
+        pltpu.make_async_copy(lift_hbm, lift_ref, sems.at[2]),
+        pltpu.make_async_copy(back_hbm, back_ref, sems.at[3]),
+    ]
     state_copies = [
         pltpu.make_async_copy(
-            energy_hbm.at[pl.ds(base, rows), :], energy_ref.at[pl.ds(base, rows), :], energy_sems.at[step]
+            energy_hbm.at[pl.ds(base, size), :], energy_ref.at[pl.ds(base, size), :], energy_sems.at[step]
         )
-        for step, base in enumerate(range(0, groups, rows))
+        for step, (base, size) in enumerate(zip(bases, sizes))
     ]
     small.start()
     sea.start()
     for copy in state_copies:
         copy.start()
-    weights.start()
-    out_ref[:, groups:, :] = jnp.zeros((tiles, ROWS, LANES), jnp.float32)
+    edges_ref[...] = jnp.zeros((LANES, LANES), jnp.float32)
     small.wait()
     spread_speeds(courant_ref, speeds_ref)
     sea.wait()
     faces_ref[...] = face_rows(sea_ref[...].astype(jnp.float32))
     rank = lax.axis_index("cell")
-    for step, base in enumerate(range(0, groups, rows)):
+    for copy in state_copies:
+        copy.wait()
+    for copy in weights:
+        copy.start()
+    for base, size in zip(bases, sizes):
         own = pl.multiple_of(rank * groups + base, ROWS)
-        speed = speeds_ref[pl.ds(own, rows), :]
-        state_copies[step].wait()
+        speed = speeds_ref[pl.ds(own, size), :]
         state = [
-            energy_ref[base : base + rows, tile * LANES : (tile + 1) * LANES] for tile in range(tiles)
+            energy_ref[base : base + size, tile * LANES : (tile + 1) * LANES] for tile in range(tiles)
         ]
-        start_rows(state, speed, faces_ref, out_ref, base, groups)
-    weights.wait()
-
-
-def final_kernel(blocks_ref, out_hbm, sems):
-    copies = [
-        pltpu.make_async_copy(
-            blocks_ref.at[tile], out_hbm.at[:, pl.ds(tile * LANES, LANES)], sems.at[tile]
-        )
-        for tile in range(blocks_ref.shape[0])
-    ]
-    for copy in copies:
-        copy.start()
-    for copy in copies:
+        start_rows(state, speed, faces_ref, out_ref, edges_ref, base)
+
+    turned = jnp.transpose(edges_ref[...])
+    edges = [turned[tile * ROWS : (tile + 1) * ROWS] for tile in range(tiles)]
+    zero = jnp.zeros((ROWS, LANES), jnp.float32)
+    last = row_index((ROWS, LANES)) < HALO
+    for tile in range(tiles):
+        before = edges[tile - 1] if tile else zero
+        after = edges[tile + 1] if tile + 1 < tiles else zero
+        out_ref[tile, groups:, :] = pltpu.roll(jnp.where(last, before, after), HALO, 0)
+    for copy in weights:
         copy.wait()
 
 
@@ -239,27 +237,44 @@
     return state - (fluxes - pltpu.roll(fluxes, 1, 0))
 
 
+def dot_rows(values, weights):
+    return lax.dot_general(
+        values, weights, (((1,), (1,)), ((), ())), preferred_element_type=jnp.float32
+    )
+
+
 def middle_kernel(
-    state_ref, courant_ref, faces_ref, lift_ref, back_ref, out_ref, own_ref, half_ref, squared_ref
+    blocks_ref, courant_ref, faces_ref, lift_ref, back_ref, out_ref, state_ref, half_ref, squared_ref
 ):
-    sources, rows, _ = state_ref.shape
+    sources, rows, _ = blocks_ref.shape
     groups = rows - ROWS
     modes = sources * groups
     blocks = modes // LANES
     rank = lax.axis_index("cell")
     tiles = faces_ref.shape[0]
-
+    ring = LANES + ROWS
+    padded = half_ref.shape[0]
+    lane = lane_index((ROWS, LANES))
+
+    halos = [jnp.zeros((ROWS, LANES), jnp.float32)] * (blocks + 1)
     for source in range(sources):
-        halo = state_ref[source, groups:, :]
-        for group in range(groups // ROWS):
-            row = source * groups + group * ROWS
-            own = state_ref[source, group * ROWS : (group + 1) * ROWS, :]
-            shift = -group * ROWS % LANES
-            own_ref[row : row + ROWS, :LANES] = own
-            own_ref[row : row + ROWS, LANES:] = pltpu.roll(halo, shift, 1) if shift else halo
-    half_ref[...] = own_ref[...].astype(jnp.bfloat16)
-
-    lifted = jnp.dot(lift_ref[...], half_ref[...], preferred_element_type=jnp.float32)
+        block, at = divmod(source * groups, LANES)
+        halo = blocks_ref[source, groups:, :]
+        halo = pltpu.roll(halo, at, 1) if at else halo
+        halos[block] = jnp.where(lane >= at, halo, halos[block])
+        halos[block + 1] = halo
+    for block in range(blocks):
+        part = slice(block * LANES, (block + 1) * LANES)
+        pieces = []
+        for row in range(part.start, part.stop, ROWS):
+            source, at = divmod(row, groups)
+            pieces.append(blocks_ref[source, at : at + ROWS, :])
+        state_ref[:LANES, part] = jnp.transpose(jnp.concatenate(pieces, axis=0))
+        state_ref[LANES:ring, part] = halos[block]
+    state_ref[ring:, :] = jnp.zeros((padded - ring, modes), jnp.float32)
+    half_ref[...] = state_ref[...].astype(jnp.bfloat16)
+
+    lifted = dot_rows(half_ref[...], lift_ref[...])
     squared_ref[...] = (lifted * lifted).astype(jnp.bfloat16)
 
     own_faces = faces_ref[pl.ds(rank, 1), :]
@@ -267,33 +282,37 @@
     before_faces = faces_ref[pl.ds(jnp.maximum(rank - 1, 0), 1), :]
     after_faces = jnp.where(rank < tiles - 1, after_faces, 0.0)
     before_faces = jnp.where(rank > 0, before_faces, 0.0)
+    lanes = lane_index((1, LANES))
+    beside_faces = jnp.where(lanes < HALO, after_faces, pltpu.roll(before_faces, ROWS, 1))
     square = jnp.concatenate(
-        [own_faces, before_faces, after_faces, jnp.zeros((LANES - 3, LANES), jnp.float32)], axis=0
+        [own_faces, beside_faces, jnp.zeros((LANES - 2, LANES), jnp.float32)], axis=0
     )
     turned = jnp.transpose(square)
-    column = jnp.concatenate(
-        [turned[LANES - ROWS :, 1:2], turned[:, 0:1], turned[:ROWS, 2:3]], axis=0
-    )
-    opens = jnp.broadcast_to(column, (LANES + 2 * ROWS, LANES))
-
-    for block in range(blocks):
-        part = slice(block * LANES, (block + 1) * LANES)
-        state = own_ref[part, :] + coupling * jnp.dot(
-            back_ref[part, :], squared_ref[...], preferred_element_type=jnp.float32
-        )
-        halo = pltpu.roll(jnp.transpose(state[:, LANES:])[:ROWS], HALO, 0)
-        state = jnp.concatenate([halo, jnp.transpose(state[:, :LANES]), halo], axis=0)
-        terms = speed_terms(courant_ref[block : block + 1, :])
-        for turn in range(2):
-            state = row_substep(state, opens, *terms)
-        advanced = jnp.transpose(state[ROWS : ROWS + LANES])
-        out_ref[part, :] = advanced
-        half_ref[part, :LANES] = advanced.astype(jnp.bfloat16)
-
-    lifted = jnp.dot(lift_ref[...], half_ref[:, :LANES], preferred_element_type=jnp.float32)
-    squared_ref[:, :LANES] = (lifted * lifted).astype(jnp.bfloat16)
-    source = jnp.dot(back_ref[...], squared_ref[:, :LANES], preferred_element_type=jnp.float32)
-    out_ref[...] += coupling * source
+    column = jnp.concatenate([turned[:, 0:1], turned[:ROWS, 1:2]], axis=0)
+    opens = jnp.broadcast_to(column, (ring, LANES))
+
+    chunk = 2 * LANES
+    for base in range(0, modes, chunk):
+        wide = slice(base, min(base + chunk, modes))
+        source = dot_rows(squared_ref[...], back_ref[wide, :])
+        for block in range(wide.start // LANES, wide.stop // LANES):
+            part = slice(block * LANES, (block + 1) * LANES)
+            at = part.start - base
+            state = state_ref[:ring, part] + coupling * source[:ring, at : at + LANES]
+            terms = speed_terms(courant_ref[block : block + 1, :])
+            for turn in range(2):
+                state = row_substep(state, opens, *terms)
+            state_ref[:LANES, part] = state[:LANES]
+            half_ref[:LANES, part] = state[:LANES].astype(jnp.bfloat16)
+
+    lifted = dot_rows(half_ref[:LANES, :], lift_ref[...])
+    squared_ref[:LANES, :] = (lifted * lifted).astype(jnp.bfloat16)
+    for base in range(0, modes, chunk):
+        wide = slice(base, min(base + chunk, modes))
+        state = state_ref[:LANES, wide] + coupling * dot_rows(squared_ref[:LANES, :], back_ref[wide, :])
+        for block in range(wide.start // LANES, wide.stop // LANES):
+            at = block * LANES - base
+            out_ref[block * LANES : (block + 1) * LANES, :] = jnp.transpose(state[:, at : at + LANES])
 
 
 def tiled_shards(wave_energy, courant, sea_mask, lift_weight, back_weight):
@@ -305,23 +324,25 @@
     f32 = jnp.float32
     any_space = pl.BlockSpec(memory_space=pl.ANY)
     vmem = pl.BlockSpec(memory_space=pltpu.VMEM)
-    inputs = (wave_energy, courant, sea_mask, back_weight)
-    start, courant, faces, back_weight = pl.pallas_call(
+    inputs = (wave_energy, courant, sea_mask, lift_weight, back_weight)
+    start, courant, faces, lift_weight, back_weight = pl.pallas_call(
         start_kernel,
         out_shape=[
             jax.ShapeDtypeStruct((tiles, groups + ROWS, LANES), f32),
             jax.ShapeDtypeStruct(courant.shape, f32),
             jax.ShapeDtypeStruct((tiles, LANES), f32),
+            jax.ShapeDtypeStruct(lift_weight.shape, lift_weight.dtype),
             jax.ShapeDtypeStruct(back_weight.shape, back_weight.dtype),
         ],
-        in_specs=[any_space] * 4,
-        out_specs=[vmem] * 4,
+        in_specs=[any_space] * 5,
+        out_specs=[vmem] * 5,
         scratch_shapes=[
             pltpu.VMEM((groups, cells), f32),
             pltpu.VMEM(sea_mask.shape, sea_mask.dtype),
             pltpu.VMEM((components, LANES), f32),
-            pltpu.SemaphoreType.DMA((3,)),
-            pltpu.SemaphoreType.DMA((groups // ROWS,)),
+            pltpu.VMEM((LANES, LANES), f32),
+            pltpu.SemaphoreType.DMA((4,)),
+            pltpu.SemaphoreType.DMA((-(-groups // START_ROWS),)),
         ],
         compiler_params=pltpu.CompilerParams(vmem_limit_bytes=16 << 20),
         name="start",
@@ -331,24 +352,14 @@
         middle_kernel,
         out_shape=jax.ShapeDtypeStruct((components, LANES), f32),
         scratch_shapes=[
-            pltpu.VMEM((components, 2 * LANES), f32),
-            pltpu.VMEM((components, 2 * LANES), jnp.bfloat16),
-            pltpu.VMEM((lift_weight.shape[0], 2 * LANES), jnp.bfloat16),
+            pltpu.VMEM((LANES + 2 * ROWS, components), f32),
+            pltpu.VMEM((LANES + 2 * ROWS, components), jnp.bfloat16),
+            pltpu.VMEM((LANES + 2 * ROWS, lift_weight.shape[0]), jnp.bfloat16),
         ],
         compiler_params=pltpu.CompilerParams(vmem_limit_bytes=24 << 20),
         name="middle",
     )(state, courant, faces, lift_weight, back_weight)
-    final = final.reshape(tiles, groups, LANES)
-    final = lax.all_to_all(final, "cell", split_axis=0, concat_axis=0, tiled=True)
-    return pl.pallas_call(
-        final_kernel,
-        out_shape=jax.ShapeDtypeStruct((groups, cells), f32),
-        in_specs=[vmem],
-        out_specs=any_space,
-        scratch_shapes=[pltpu.SemaphoreType.DMA((tiles,))],
-        compiler_params=pltpu.CompilerParams(vmem_limit_bytes=16 << 20),
-        name="final",
-    )(final)
+    return lax.all_to_all(final, "cell", split_axis=0, concat_axis=1, tiled=True)
 
 
 def shards(wave_energy, courant, sea_mask, lift_weight, back_weight):

time: 55.5 us -> 54.1 us (0.975)
  Pallas kernels: 9.56 us -> 7.27 us
  local copies, waits for them, and re-layouts: 0.01 us -> 0.86 us
    pallas_call x1, Pallas kernels: 5.1 us -> 3.73 us  [tiled_shards(): pl.pallas_call(middle_kernel, out_shape=jax.ShapeDtypeStruct((components,...]
    pallas_call x1 -> x0, Pallas kernels: 0.94 us -> none  [tiled_shards(): pl.pallas_call(final_kernel, out_shape=jax.ShapeDtypeStruct((groups, cell...]
    all_to_all x0 -> x1, local copies, waits for them, and re-layouts: none -> 0.86 us  [tiled_shards(): lax.all_to_all(final, 'cell', split_axis=0, concat_axis=1, tiled=True)]
where the time goes in v5:
time: 54.1 us; the launch traced here: 53.9 us
  blocking collectives  45.7 us (84%)
  Pallas kernels  7.27 us (13%)
  local copies, waits for them, and re-layouts  0.86 us (2%)
    all_to_all x1, blocking collectives, tiled_shards(): lax.all_to_all(start, 'cell', split_axis=0, concat_axis=0, tiled=True)  25.4 us
    all_to_all x1, blocking collectives, tiled_shards(): lax.all_to_all(final, 'cell', split_axis=0, concat_axis=1, tiled=True)  20.3 us
    pallas_call x1, Pallas kernels, tiled_shards(): pl.pallas_call(middle_kernel, out_shape=jax.ShapeDtypeStruct((components,...  3.73 us
    pallas_call x1, Pallas kernels, tiled_shards(): pl.pallas_call(start_kernel, out_shape=[jax.ShapeDtypeStruct((tiles, grou...  3.54 us

profile of v5, /device:TPU:0, one launch (start us, length us, event | category | flops | bytes accessed | tf_op | source)
XLA Modules:
  0.0 53.9 jit_solution(459796547710695109)
XLA Ops:
  0.0 3.5 %start.1 = (f32[16,80,128]{2,1,0:T(8,128)S(1)}, f32[9,128]{1,0:T(8,128)S(1)}, f32[16,128]{1,0:T(8,128)S(1)}, bf16[1024,1152]{1,0:T(8,128)(2,1)S(1)}, bf16[1152,1024]{1,0:T(8,128)(2,1)S(1)}) custom-call(f32[72,2048]{1,0:T(8,128)} %energy_hbm.1, f32[9,128]{1,0:T(8,128)} %bitcast.10, s32[16,128]{1,0:T(8,128)} %bitcast.11, bf16[1024,1152]{1,0:T(8,128)(2,1)} %lift_hbm.1, ...), custom_call_target="tpu_custom_call" | custom-call | tf_op jit(solution)/shard_map/start/pallas_call | solution.py:328
  3.5 25.4 %all_to_all.24.blocks_ref = f32[16,80,128]{2,1,0:T(8,128)S(1)} all-to-all(f32[16,80,128]{2,1,0:T(8,128)S(1)} %get-tuple-element.10), channel_id=1, replica_groups=mesh['member'=2,'cell'=16] {'cell'}, dimensions={0} | all-to-all | bytes 1310720 | tf_op jit(solution)/shard_map/all_to_all | solution.py:350
  28.9 3.7 %middle.1 = f32[1152,128]{1,0:T(8,128)S(1)} custom-call(f32[16,80,128]{2,1,0:T(8,128)S(1)} %all_to_all.24.blocks_ref, f32[9,128]{1,0:T(8,128)S(1)} %get-tuple-element.11.courant_ref, f32[16,128]{1,0:T(8,128)S(1)} %get-tuple-element.12.faces_ref, bf16[1024,1152]{1,0:T(8,128)(2,1)S(1)} %get-tuple-element.13.lift_ref, ...), custom_call_target="tpu_custom_call" | custom-call | tf_op jit(solution)/shard_map/middle/pallas_call | solution.py:351
  32.7 20.3 %all_to_all.25 = f32[16,72,128]{2,1,0:T(8,128)S(1)} all-to-all(f32[16,72,128]{2,1,0:T(8,128)S(1)} %bitcast.9), channel_id=1, replica_groups=mesh['member'=2,'cell'=16] {'cell'}, dimensions={0} | all-to-all | bytes 1179648 | tf_op jit(solution)/shard_map/all_to_all | solution.py:362
  53.0 0.9 %copy_bitcast_fusion = f32[72,2048]{1,0:T(8,128)} fusion(f32[16,72,128]{2,1,0:T(8,128)S(1)} %all_to_all.25), kind=kLoop, calls=%fused_computation | loop fusion | bytes 1179648 | tf_op jit(solution)/shard_map/all_to_all | solution.py:362

commit v6 on v5

--- a/solution.py
+++ b/solution.py
@@ -1,3 +1,5 @@
+import functools
+
 import jax
 import jax.numpy as jnp
 from jax import lax
@@ -167,9 +169,9 @@
 
 
 def start_kernel(
-    energy_hbm, courant_hbm, sea_hbm, lift_hbm, back_hbm,
-    out_ref, courant_ref, faces_ref, lift_ref, back_ref,
-    energy_ref, sea_ref, speeds_ref, edges_ref, sems, energy_sems,
+    energy_hbm, courant_hbm, sea_hbm, back_hbm,
+    out_ref, edges_out_ref, courant_ref, faces_ref, back_ref,
+    energy_ref, sea_ref, speeds_ref, edges_ref, sems, energy_sems, back_sems,
 ):
     groups = energy_ref.shape[0]
     tiles = out_ref.shape[0]
@@ -177,9 +179,13 @@
     sizes = [min(START_ROWS, groups - base) for base in bases]
     small = pltpu.make_async_copy(courant_hbm, courant_ref, sems.at[0])
     sea = pltpu.make_async_copy(sea_hbm, sea_ref, sems.at[1])
+    pieces = back_sems.shape[0]
+    piece = back_hbm.shape[0] // pieces
     weights = [
-        pltpu.make_async_copy(lift_hbm, lift_ref, sems.at[2]),
-        pltpu.make_async_copy(back_hbm, back_ref, sems.at[3]),
+        pltpu.make_async_copy(
+            back_hbm.at[pl.ds(at * piece, piece), :], back_ref.at[pl.ds(at * piece, piece), :], back_sems.at[at]
+        )
+        for at in range(pieces)
     ]
     state_copies = [
         pltpu.make_async_copy(
@@ -190,6 +196,8 @@
     small.start()
     sea.start()
     for copy in state_copies:
+        copy.start()
+    for copy in weights:
         copy.start()
     edges_ref[...] = jnp.zeros((LANES, LANES), jnp.float32)
     small.wait()
@@ -197,11 +205,8 @@
     sea.wait()
     faces_ref[...] = face_rows(sea_ref[...].astype(jnp.float32))
     rank = lax.axis_index("cell")
-    for copy in state_copies:
+    for copy, base, size in zip(state_copies, bases, sizes):
         copy.wait()
-    for copy in weights:
-        copy.start()
-    for base, size in zip(bases, sizes):
         own = pl.multiple_of(rank * groups + base, ROWS)
         speed = speeds_ref[pl.ds(own, size), :]
         state = [
@@ -209,14 +214,7 @@
         ]
         start_rows(state, speed, faces_ref, out_ref, edges_ref, base)
 
-    turned = jnp.transpose(edges_ref[...])
-    edges = [turned[tile * ROWS : (tile + 1) * ROWS] for tile in range(tiles)]
-    zero = jnp.zeros((ROWS, LANES), jnp.float32)
-    last = row_index((ROWS, LANES)) < HALO
-    for tile in range(tiles):
-        before = edges[tile - 1] if tile else zero
-        after = edges[tile + 1] if tile + 1 < tiles else zero
-        out_ref[tile, groups:, :] = pltpu.roll(jnp.where(last, before, after), HALO, 0)
+    edges_out_ref[...] = jnp.transpose(edges_ref[...])
     for copy in weights:
         copy.wait()
 
@@ -244,10 +242,10 @@
 
 
 def middle_kernel(
-    blocks_ref, courant_ref, faces_ref, lift_ref, back_ref, out_ref, state_ref, half_ref, squared_ref
+    blocks_ref, edges_hbm, courant_ref, faces_ref, lift_ref, back_ref, out_ref, extra_ref,
+    state_ref, half_ref, squared_ref, edges_ref, sem,
 ):
-    sources, rows, _ = blocks_ref.shape
-    groups = rows - ROWS
+    sources, groups, _ = blocks_ref.shape
     modes = sources * groups
     blocks = modes // LANES
     rank = lax.axis_index("cell")
@@ -255,14 +253,12 @@
     ring = LANES + ROWS
     padded = half_ref.shape[0]
     lane = lane_index((ROWS, LANES))
-
-    halos = [jnp.zeros((ROWS, LANES), jnp.float32)] * (blocks + 1)
-    for source in range(sources):
-        block, at = divmod(source * groups, LANES)
-        halo = blocks_ref[source, groups:, :]
-        halo = pltpu.roll(halo, at, 1) if at else halo
-        halos[block] = jnp.where(lane >= at, halo, halos[block])
-        halos[block + 1] = halo
+    first = jnp.clip(rank - 1, 0, tiles - 3)
+    copy = pltpu.make_async_copy(
+        edges_hbm.at[:, pl.ds(pl.multiple_of(first * ROWS, ROWS), 3 * ROWS), :], edges_ref, sem
+    )
+    copy.start()
+
     for block in range(blocks):
         part = slice(block * LANES, (block + 1) * LANES)
         pieces = []
@@ -270,8 +266,25 @@
             source, at = divmod(row, groups)
             pieces.append(blocks_ref[source, at : at + ROWS, :])
         state_ref[:LANES, part] = jnp.transpose(jnp.concatenate(pieces, axis=0))
-        state_ref[LANES:ring, part] = halos[block]
     state_ref[ring:, :] = jnp.zeros((padded - ring, modes), jnp.float32)
+    copy.wait()
+    before_at = pl.multiple_of((jnp.maximum(rank - 1, 0) - first) * ROWS, ROWS)
+    after_at = pl.multiple_of((jnp.minimum(rank + 1, tiles - 1) - first) * ROWS, ROWS)
+    last = row_index((ROWS, LANES)) < HALO
+    from_before = last & (rank > 0)
+    from_after = jnp.logical_not(last) & (rank < tiles - 1)
+    halos = [jnp.zeros((ROWS, LANES), jnp.float32)] * (blocks + 1)
+    for source in range(sources):
+        block, at = divmod(source * groups, LANES)
+        before = edges_ref[source, pl.ds(before_at, ROWS), :]
+        after = edges_ref[source, pl.ds(after_at, ROWS), :]
+        halo = jnp.where(from_before, before, jnp.where(from_after, after, 0.0))
+        halo = pltpu.roll(halo, at, 1) if at else halo
+        halos[block] = jnp.where(lane >= at, halo, halos[block])
+        halos[block + 1] = halo
+    for block in range(blocks):
+        part = slice(block * LANES, (block + 1) * LANES)
+        state_ref[LANES:ring, part] = pltpu.roll(halos[block], HALO, 0)
     half_ref[...] = state_ref[...].astype(jnp.bfloat16)
 
     lifted = dot_rows(half_ref[...], lift_ref[...])
@@ -292,6 +305,7 @@
     opens = jnp.broadcast_to(column, (ring, LANES))
 
     chunk = 2 * LANES
+    kept = out_ref.shape[1]
     for base in range(0, modes, chunk):
         wide = slice(base, min(base + chunk, modes))
         source = dot_rows(squared_ref[...], back_ref[wide, :])
@@ -312,61 +326,117 @@
         state = state_ref[:LANES, wide] + coupling * dot_rows(squared_ref[:LANES, :], back_ref[wide, :])
         for block in range(wide.start // LANES, wide.stop // LANES):
             at = block * LANES - base
-            out_ref[block * LANES : (block + 1) * LANES, :] = jnp.transpose(state[:, at : at + LANES])
+            turned = jnp.transpose(state[:, at : at + LANES])
+            for row in range(0, LANES, ROWS):
+                target, place = divmod(block * LANES + row, groups)
+                values = turned[row : row + ROWS]
+                if place < kept:
+                    out_ref[target, place : place + ROWS, :] = values
+                else:
+                    place += target * (groups - kept) - kept
+                    extra_ref[place : place + ROWS, :] = values
+
+
+def final_kernel(blocks_ref, extra_hbm, out_hbm, sems, extra_sems):
+    tiles, kept, _ = blocks_ref.shape
+    extra = out_hbm.shape[0] - kept
+    at = pl.multiple_of(lax.axis_index("cell") * extra, ROWS)
+    copies = []
+    for tile in range(tiles):
+        cells = pl.ds(tile * LANES, LANES)
+        copies.append(
+            pltpu.make_async_copy(
+                extra_hbm.at[tile, pl.ds(at, extra), :], out_hbm.at[pl.ds(kept, extra), cells], extra_sems.at[tile]
+            )
+        )
+        copies.append(
+            pltpu.make_async_copy(
+                blocks_ref.at[tile], out_hbm.at[pl.ds(0, kept), cells], sems.at[tile]
+            )
+        )
+    for copy in copies:
+        copy.start()
+    for copy in copies:
+        copy.wait()
+
+
+GATHERED = 8
 
 
 def tiled_shards(wave_energy, courant, sea_mask, lift_weight, back_weight):
-    devices = lax.axis_size("cell")
     groups, cells = wave_energy.shape
     components, tiles = courant.shape[0], cells // LANES
+    kept = groups - GATHERED
     courant = courant.reshape(components // LANES, LANES)
     sea_mask = sea_mask.reshape(tiles, LANES)
     f32 = jnp.float32
     any_space = pl.BlockSpec(memory_space=pl.ANY)
     vmem = pl.BlockSpec(memory_space=pltpu.VMEM)
-    inputs = (wave_energy, courant, sea_mask, lift_weight, back_weight)
-    start, courant, faces, lift_weight, back_weight = pl.pallas_call(
+    dma = pltpu.SemaphoreType.DMA
+    in_hbm = functools.partial(pltpu.with_memory_space_constraint, memory_space=pltpu.HBM)
+    inputs = (wave_energy, courant, sea_mask, back_weight)
+    start, edges, courant, faces, back_weight = pl.pallas_call(
         start_kernel,
         out_shape=[
-            jax.ShapeDtypeStruct((tiles, groups + ROWS, LANES), f32),
+            jax.ShapeDtypeStruct((tiles, groups, LANES), f32),
+            jax.ShapeDtypeStruct((LANES, LANES), f32),
             jax.ShapeDtypeStruct(courant.shape, f32),
             jax.ShapeDtypeStruct((tiles, LANES), f32),
-            jax.ShapeDtypeStruct(lift_weight.shape, lift_weight.dtype),
             jax.ShapeDtypeStruct(back_weight.shape, back_weight.dtype),
         ],
-        in_specs=[any_space] * 5,
+        in_specs=[any_space] * 4,
         out_specs=[vmem] * 5,
         scratch_shapes=[
             pltpu.VMEM((groups, cells), f32),
             pltpu.VMEM(sea_mask.shape, sea_mask.dtype),
             pltpu.VMEM((components, LANES), f32),
             pltpu.VMEM((LANES, LANES), f32),
-            pltpu.SemaphoreType.DMA((4,)),
-            pltpu.SemaphoreType.DMA((-(-groups // START_ROWS),)),
+            dma((2,)),
+            dma((-(-groups // START_ROWS),)),
+            dma((4 if back_weight.shape[0] % LANES == 0 else 1,)),
         ],
         compiler_params=pltpu.CompilerParams(vmem_limit_bytes=16 << 20),
         name="start",
-    )(*(pltpu.with_memory_space_constraint(x, pltpu.HBM) for x in inputs))
+    )(*map(in_hbm, inputs))
+    edges = lax.all_gather(edges, "cell", axis=0, tiled=True).reshape(tiles, LANES, LANES)
     state = lax.all_to_all(start, "cell", split_axis=0, concat_axis=0, tiled=True)
-    final = pl.pallas_call(
+    padded = LANES + 2 * ROWS
+    final, extra = pl.pallas_call(
         middle_kernel,
-        out_shape=jax.ShapeDtypeStruct((components, LANES), f32),
+        out_shape=[
+            jax.ShapeDtypeStruct((tiles, kept, LANES), f32),
+            jax.ShapeDtypeStruct((tiles * GATHERED, LANES), f32),
+        ],
+        in_specs=[vmem, any_space] + [vmem] * 4,
+        out_specs=[vmem] * 2,
         scratch_shapes=[
-            pltpu.VMEM((LANES + 2 * ROWS, components), f32),
-            pltpu.VMEM((LANES + 2 * ROWS, components), jnp.bfloat16),
-            pltpu.VMEM((LANES + 2 * ROWS, lift_weight.shape[0]), jnp.bfloat16),
+            pltpu.VMEM((padded, components), f32),
+            pltpu.VMEM((padded, components), jnp.bfloat16),
+            pltpu.VMEM((padded, lift_weight.shape[0]), jnp.bfloat16),
+            pltpu.VMEM((tiles, 3 * ROWS, LANES), f32),
+            dma,
         ],
         compiler_params=pltpu.CompilerParams(vmem_limit_bytes=24 << 20),
         name="middle",
-    )(state, courant, faces, lift_weight, back_weight)
-    return lax.all_to_all(final, "cell", split_axis=0, concat_axis=1, tiled=True)
+    )(state, in_hbm(edges), courant, faces, lift_weight, back_weight)
+    extra = lax.all_gather(extra, "cell", axis=0, tiled=True).reshape(tiles, tiles * GATHERED, LANES)
+    final = lax.all_to_all(final, "cell", split_axis=0, concat_axis=0, tiled=True)
+    return pl.pallas_call(
+        final_kernel,
+        out_shape=jax.ShapeDtypeStruct((groups, cells), f32),
+        in_specs=[vmem, any_space],
+        out_specs=any_space,
+        scratch_shapes=[dma((tiles,)), dma((tiles,))],
+        compiler_params=pltpu.CompilerParams(vmem_limit_bytes=16 << 20),
+        name="final",
+    )(final, in_hbm(extra))
 
 
 def shards(wave_energy, courant, sea_mask, lift_weight, back_weight):
     devices = lax.axis_size("cell")
     groups, cells = wave_energy.shape
-    whole = cells == devices * LANES and groups % ROWS == 0 and groups <= LANES
-    whole = whole and courant.shape[0] % LANES == 0 and courant.shape[0] <= LANES * LANES // ROWS
+    whole = cells == devices * LANES and groups % ROWS == 0 and GATHERED < groups <= LANES
+    whole = whole and 3 <= devices <= LANES // ROWS and courant.shape[0] % LANES == 0 and courant.shape[0] <= LANES * LANES // ROWS
     run = tiled_shards if whole else general_shards
     return run(wave_energy, courant, sea_mask, lift_weight, back_weight)
 

time: 54.1 us -> 111 us (2.05)
  waiting for transfers between devices: 0 us -> 35.6 us
  between operations: 0.01 us -> 13.4 us
  Pallas kernels: 7.27 us -> 12.8 us
  local copies, waits for them, and re-layouts: 0.86 us -> 3.07 us
    all_gather x0 -> x2, waiting for transfers between devices: none -> 35.6 us  [the longest x1 19.5 us: tiled_shards(): lax.all_gather(extra, 'cell', axis=0, tiled=True)]
    pallas_call x1 -> x2, Pallas kernels: 3.73 us -> 8.83 us  [the longest x1 5.45 us: tiled_shards(): pl.pallas_call(middle_kernel, out_shape=[jax.ShapeDtypeStruct((tiles, kep...]
    unnamed x0 -> x6, local copies, waits for them, and re-layouts: none -> 3.07 us
    all_to_all x1, blocking collectives: 25.4 us -> 26.6 us  [tiled_shards(): lax.all_to_all(start, 'cell', split_axis=0, concat_axis=0, tiled=True)]
  transfers between devices with their start and end apart: 0 -> 2, of which waited for: 0 -> 2; matrix products, arithmetic and copies ran while one was open for 0% -> 0% of each run, Pallas kernels for 0% -> 0%
where the time goes in v6:
time: 111 us
  blocking collectives  45.9 us (41%)
  waiting for transfers between devices  35.6 us (32%)
  between operations  13.4 us (12%)
  Pallas kernels  12.8 us (12%)
  local copies, waits for them, and re-layouts  3.07 us (3%)
    all_to_all x1, blocking collectives, tiled_shards(): lax.all_to_all(start, 'cell', split_axis=0, concat_axis=0, tiled=True)  26.6 us
    all_gather x1, waiting for transfers between devices, tiled_shards(): lax.all_gather(extra, 'cell', axis=0, tiled=True)  19.5 us
    all_to_all x1, blocking collectives, tiled_shards(): lax.all_to_all(final, 'cell', split_axis=0, concat_axis=0, tiled=True)  19.3 us
    all_gather x1, waiting for transfers between devices, tiled_shards(): lax.all_gather(edges, 'cell', axis=0, tiled=True)  16 us
    pallas_call x1, Pallas kernels, tiled_shards(): pl.pallas_call(middle_kernel, out_shape=[jax.ShapeDtypeStruct((tiles, kep...  5.45 us
    pallas_call x1, Pallas kernels, tiled_shards(): pl.pallas_call(start_kernel, out_shape=[jax.ShapeDtypeStruct((tiles, grou...  3.96 us
    pallas_call x1, Pallas kernels, tiled_shards(): pl.pallas_call(final_kernel, out_shape=jax.ShapeDtypeStruct((groups, cell...  3.37 us
    unnamed x6, local copies, waits for them, and re-layouts  3.07 us
  transfers between devices with their start and end apart: 2, of which 2 were waited for; matrix products, arithmetic and copies ran while one was open for 0% of the time, Pallas kernels for 0%

profile of v6, /device:TPU:0, one launch (start us, length us, event | category | flops | bytes accessed | tf_op | source)
XLA Modules:
  0.0 110.8 jit_solution(3730351130276443594)
XLA Ops:
  6.5 0.0 copy-start
  6.5 0.0 all-gather.3.cloned.1.call-start
  6.5 4.0 %start.1 = (f32[16,72,128]{2,1,0:T(8,128)S(1)}, f32[128,128]{1,0:T(8,128)}, f32[9,128]{1,0:T(8,128)S(1)}, f32[16,128]{1,0:T(8,128)S(1)}, bf16[1152,1024]{1,0:T(8,128)(2,1)S(1)}) custom-call(f32[72,2048]{1,0:T(8,128)} %energy_hbm.1, f32[9,128]{1,0:T(8,128)} %bitcast.6, s32[16,128]{1,0:T(8,128)} %bitcast.7, bf16[1152,1024]{1,0:T(8,128)(2,1)} %back_hbm.1), custom_call_target="tpu_custom_call" | custom-call | tf_op jit(solution)/shard_map/start/pallas_call | solution.py:378
  10.5 0.0 copy-start.1
  10.5 1.4 %copy-done.1 = bf16[1152,1024]{1,0:T(8,128)(2,1)} copy-done((bf16[1152,1024]{1,0:T(8,128)(2,1)}, bf16[1152,1024]{1,0:T(8,128)(2,1)S(1)}, u32[]{:S(2)}) %copy-start.1) | copy-done | bytes 2359320
  11.9 0.0 all-gather.3.cloned.1.call-update
  11.9 0.0 all-gather.5.cloned.1.call-start
  12.0 26.6 %all_to_all.10.blocks_ref = f32[16,72,128]{2,1,0:T(8,128)S(1)} all-to-all(f32[16,72,128]{2,1,0:T(8,128)S(1)} %get-tuple-element.12), channel_id=1, replica_groups=mesh['member'=2,'cell'=16] {'cell'}, dimensions={0} | all-to-all | bytes 1179648 | tf_op jit(solution)/shard_map/all_to_all | solution.py:402
  38.6 16.0 %all-gather.3.cloned.1.call-done = f32[2048,128]{1,0:T(8,128)} async-done(((f32[128,128]{1,0:T(8,128)}), f32[2048,128]{1,0:T(8,128)}) %all-gather.3.cloned.1.call-update) | async-done | bytes 1048592 | tf_op jit(solution)/shard_map/all_gather | solution.py:401
  54.6 0.0 copy-done
  54.6 0.0 copy-start.2
  54.6 1.7 %copy-done.2 = bf16[1152,1024]{1,0:T(8,128)(2,1)S(1)} copy-done((bf16[1152,1024]{1,0:T(8,128)(2,1)S(1)}, bf16[1152,1024]{1,0:T(8,128)(2,1)}, u32[]{:S(2)}) %copy-start.2) | copy-done | bytes 2359320
  56.3 5.5 %middle.1 = (f32[16,64,128]{2,1,0:T(8,128)S(1)}, f32[128,128]{1,0:T(8,128)}) custom-call(f32[16,72,128]{2,1,0:T(8,128)S(1)} %all_to_all.10.blocks_ref, f32[16,128,128]{2,1,0:T(8,128)} %bitcast.4, f32[9,128]{1,0:T(8,128)S(1)} %get-tuple-element.14.courant_ref, f32[16,128]{1,0:T(8,128)S(1)} %get-tuple-element.15.faces_ref, bf16[1024,1152]{1,0:T(8,128)(2,1)S(1)} %copy-done, ...), custom_call_target="tpu_custom_call" | custom-call | tf_op jit(solution)/shard_map/middle/pallas_call | solution.py:404
  61.7 0.0 all-gather.5.cloned.1.call-update
  61.8 19.3 %all_to_all.11.blocks_ref = f32[16,64,128]{2,1,0:T(8,128)S(1)} all-to-all(f32[16,64,128]{2,1,0:T(8,128)S(1)} %get-tuple-element.17), channel_id=1, replica_groups=mesh['member'=2,'cell'=16] {'cell'}, dimensions={0} | all-to-all | bytes 1048576 | tf_op jit(solution)/shard_map/all_to_all | solution.py:423
  81.0 19.5 %all-gather.5.cloned.1.call-done = f32[2048,128]{1,0:T(8,128)} async-done(((f32[128,128]{1,0:T(8,128)}), f32[2048,128]{1,0:T(8,128)}) %all-gather.5.cloned.1.call-update) | async-done | bytes 1048592 | tf_op jit(solution)/shard_map/all_gather | solution.py:422
  100.6 3.4 %final.1 = f32[72,2048]{1,0:T(8,128)} custom-call(f32[16,64,128]{2,1,0:T(8,128)S(1)} %all_to_all.11.blocks_ref, f32[16,128,128]{2,1,0:T(8,128)} %bitcast.5), custom_call_target="tpu_custom_call" | custom-call | tf_op jit(solution)/shard_map/final/pallas_call | solution.py:424
Async XLA Ops:
  6.5 48.1 %copy-start = (bf16[1024,1152]{1,0:T(8,128)(2,1)S(1)}, bf16[1024,1152]{1,0:T(8,128)(2,1)}, u32[]{:S(2)}) copy-start(bf16[1024,1152]{1,0:T(8,128)(2,1)} %lift_ref.1) | copy-start | bytes 7077892
  6.5 48.1 %all-gather.3.cloned.1.call-start = ((), (), s32[]{:S(2)}) async-start(), calls=%async_computation.2 | async-start | bytes 1114112 | tf_op jit(solution)/shard_map/all_gather | solution.py:401
  10.5 1.4 %copy-start.1 = (bf16[1152,1024]{1,0:T(8,128)(2,1)}, bf16[1152,1024]{1,0:T(8,128)(2,1)S(1)}, u32[]{:S(2)}) copy-start(bf16[1152,1024]{1,0:T(8,128)(2,1)S(1)} %get-tuple-element.16.back_ref) | copy-start | bytes 7077892
  11.9 88.6 %all-gather.5.cloned.1.call-start = ((), (), s32[]{:S(2)}) async-start(), calls=%async_computation.3 | async-start | bytes 1114112 | tf_op jit(solution)/shard_map/all_gather | solution.py:422
  54.6 1.7 %copy-start.2 = (bf16[1152,1024]{1,0:T(8,128)(2,1)S(1)}, bf16[1152,1024]{1,0:T(8,128)(2,1)}, u32[]{:S(2)}) copy-start(bf16[1152,1024]{1,0:T(8,128)(2,1)} %copy-done.1) | copy-start | bytes 7077892
Sparse Core Ops, SparseCore 0:
  12.1 42.4 all-gather.2
  61.9 38.6 all-gather.4

commit v7 on v5

--- a/solution.py
+++ b/solution.py
@@ -167,8 +167,7 @@
 
 
 def start_kernel(
-    energy_hbm, courant_hbm, sea_hbm, lift_hbm, back_hbm,
-    out_ref, courant_ref, faces_ref, lift_ref, back_ref,
+    energy_hbm, courant_hbm, sea_hbm, out_ref, courant_ref, faces_ref,
     energy_ref, sea_ref, speeds_ref, edges_ref, sems, energy_sems,
 ):
     groups = energy_ref.shape[0]
@@ -177,10 +176,6 @@
     sizes = [min(START_ROWS, groups - base) for base in bases]
     small = pltpu.make_async_copy(courant_hbm, courant_ref, sems.at[0])
     sea = pltpu.make_async_copy(sea_hbm, sea_ref, sems.at[1])
-    weights = [
-        pltpu.make_async_copy(lift_hbm, lift_ref, sems.at[2]),
-        pltpu.make_async_copy(back_hbm, back_ref, sems.at[3]),
-    ]
     state_copies = [
         pltpu.make_async_copy(
             energy_hbm.at[pl.ds(base, size), :], energy_ref.at[pl.ds(base, size), :], energy_sems.at[step]
@@ -197,11 +192,8 @@
     sea.wait()
     faces_ref[...] = face_rows(sea_ref[...].astype(jnp.float32))
     rank = lax.axis_index("cell")
-    for copy in state_copies:
+    for copy, base, size in zip(state_copies, bases, sizes):
         copy.wait()
-    for copy in weights:
-        copy.start()
-    for base, size in zip(bases, sizes):
         own = pl.multiple_of(rank * groups + base, ROWS)
         speed = speeds_ref[pl.ds(own, size), :]
         state = [
@@ -217,8 +209,6 @@
         before = edges[tile - 1] if tile else zero
         after = edges[tile + 1] if tile + 1 < tiles else zero
         out_ref[tile, groups:, :] = pltpu.roll(jnp.where(last, before, after), HALO, 0)
-    for copy in weights:
-        copy.wait()
 
 
 def row_index(shape):
@@ -324,27 +314,26 @@
     f32 = jnp.float32
     any_space = pl.BlockSpec(memory_space=pl.ANY)
     vmem = pl.BlockSpec(memory_space=pltpu.VMEM)
-    inputs = (wave_energy, courant, sea_mask, lift_weight, back_weight)
-    start, courant, faces, lift_weight, back_weight = pl.pallas_call(
+    inputs = (wave_energy, courant, sea_mask)
+    start, courant, faces = pl.pallas_call(
         start_kernel,
         out_shape=[
             jax.ShapeDtypeStruct((tiles, groups + ROWS, LANES), f32),
             jax.ShapeDtypeStruct(courant.shape, f32),
             jax.ShapeDtypeStruct((tiles, LANES), f32),
-            jax.ShapeDtypeStruct(lift_weight.shape, lift_weight.dtype),
-            jax.ShapeDtypeStruct(back_weight.shape, back_weight.dtype),
         ],
-        in_specs=[any_space] * 5,
-        out_specs=[vmem] * 5,
+        in_specs=[any_space] * 3,
+        out_specs=[vmem] * 3,
         scratch_shapes=[
             pltpu.VMEM((groups, cells), f32),
             pltpu.VMEM(sea_mask.shape, sea_mask.dtype),
             pltpu.VMEM((components, LANES), f32),
             pltpu.VMEM((LANES, LANES), f32),
-            pltpu.SemaphoreType.DMA((4,)),
+            pltpu.SemaphoreType.DMA((2,)),
             pltpu.SemaphoreType.DMA((-(-groups // START_ROWS),)),
         ],
         compiler_params=pltpu.CompilerParams(vmem_limit_bytes=16 << 20),
+        cost_estimate=pl.CostEstimate(flops=1000000000, bytes_accessed=3 * 4 * groups * cells, transcendentals=0),
         name="start",
     )(*(pltpu.with_memory_space_constraint(x, pltpu.HBM) for x in inputs))
     state = lax.all_to_all(start, "cell", split_axis=0, concat_axis=0, tiled=True)

time: 54.1 us -> 53.5 us (0.989)
  Pallas kernels: 7.27 us -> 6.67 us
    pallas_call x1, Pallas kernels: 3.54 us -> 2.94 us  [tiled_shards(): pl.pallas_call(start_kernel, out_shape=[jax.ShapeDtypeStruct((tiles, grou...]
where the time goes in v7:
time: 53.5 us; the launch traced here: 53.3 us
  blocking collectives  45.7 us (85%)
  Pallas kernels  6.67 us (12%)
  local copies, waits for them, and re-layouts  0.87 us (2%)
    all_to_all x1, blocking collectives, tiled_shards(): lax.all_to_all(start, 'cell', split_axis=0, concat_axis=0, tiled=True)  25.4 us
    all_to_all x1, blocking collectives, tiled_shards(): lax.all_to_all(final, 'cell', split_axis=0, concat_axis=1, tiled=True)  20.3 us
    pallas_call x1, Pallas kernels, tiled_shards(): pl.pallas_call(middle_kernel, out_shape=jax.ShapeDtypeStruct((components,...  3.73 us
    pallas_call x1, Pallas kernels, tiled_shards(): pl.pallas_call(start_kernel, out_shape=[jax.ShapeDtypeStruct((tiles, grou...  2.94 us

profile of v7, /device:TPU:0, one launch (start us, length us, event | category | flops | bytes accessed | tf_op | source)
XLA Modules:
  0.0 53.3 jit_solution(628955696394273389)
XLA Ops:
  0.0 0.0 copy-start
  0.0 0.0 copy-start.1
  0.0 2.9 %start.1 = (f32[16,80,128]{2,1,0:T(8,128)S(1)}, f32[9,128]{1,0:T(8,128)S(1)}, f32[16,128]{1,0:T(8,128)S(1)}) custom-call(f32[72,2048]{1,0:T(8,128)} %energy_hbm.1, f32[9,128]{1,0:T(8,128)} %bitcast.10, s32[16,128]{1,0:T(8,128)} %bitcast.11), custom_call_target="tpu_custom_call" | custom-call | flops 1000000000 | bytes 1769472 | tf_op jit(solution)/shard_map/start/pallas_call | solution.py:318
  2.9 25.4 %all_to_all.24.blocks_ref = f32[16,80,128]{2,1,0:T(8,128)S(1)} all-to-all(f32[16,80,128]{2,1,0:T(8,128)S(1)} %get-tuple-element.8), channel_id=1, replica_groups=mesh['member'=2,'cell'=16] {'cell'}, dimensions={0} | all-to-all | bytes 1310720 | tf_op jit(solution)/shard_map/all_to_all | solution.py:339
  28.3 0.0 copy-done
  28.3 0.0 copy-done.1
  28.3 3.7 %middle.1 = f32[1152,128]{1,0:T(8,128)S(1)} custom-call(f32[16,80,128]{2,1,0:T(8,128)S(1)} %all_to_all.24.blocks_ref, f32[9,128]{1,0:T(8,128)S(1)} %get-tuple-element.9.courant_ref, f32[16,128]{1,0:T(8,128)S(1)} %get-tuple-element.10.faces_ref, bf16[1024,1152]{1,0:T(8,128)(2,1)S(1)} %copy-done, bf16[1152,1024]{1,0:T(8,128)(2,1)S(1)} %copy-done.1), custom_call_target="tpu_custom_call" | custom-call | tf_op jit(solution)/shard_map/middle/pallas_call | solution.py:340
  32.1 20.3 %all_to_all.25 = f32[16,72,128]{2,1,0:T(8,128)S(1)} all-to-all(f32[16,72,128]{2,1,0:T(8,128)S(1)} %bitcast.9), channel_id=1, replica_groups=mesh['member'=2,'cell'=16] {'cell'}, dimensions={0} | all-to-all | bytes 1179648 | tf_op jit(solution)/shard_map/all_to_all | solution.py:351
  52.4 0.9 %copy_bitcast_fusion = f32[72,2048]{1,0:T(8,128)} fusion(f32[16,72,128]{2,1,0:T(8,128)S(1)} %all_to_all.25), kind=kLoop, calls=%fused_computation | loop fusion | bytes 1179648 | tf_op jit(solution)/shard_map/all_to_all | solution.py:351
Async XLA Ops:
  0.0 28.3 %copy-start = (bf16[1024,1152]{1,0:T(8,128)(2,1)S(1)}, bf16[1024,1152]{1,0:T(8,128)(2,1)}, u32[]{:S(2)}) copy-start(bf16[1024,1152]{1,0:T(8,128)(2,1)} %lift_ref.1) | copy-start | bytes 7077892
  0.0 28.3 %copy-start.1 = (bf16[1152,1024]{1,0:T(8,128)(2,1)S(1)}, bf16[1152,1024]{1,0:T(8,128)(2,1)}, u32[]{:S(2)}) copy-start(bf16[1152,1024]{1,0:T(8,128)(2,1)} %back_ref.1) | copy-start | bytes 7077892

commit v8 on v7

--- a/solution.py
+++ b/solution.py
@@ -150,6 +150,18 @@
 START_ROWS = 40
 
 
+def places(devices):
+    half = devices // 2
+    return [2 * i if i < half else 2 * (i - half) + 1 for i in range(2 * half)]
+
+
+def exchange(blocks):
+    devices = lax.axis_size("cell")
+    place = places(devices)
+    order = sorted(range(devices), key=lambda device: place[device])
+    return lax.all_to_all(blocks, "cell", split_axis=0, concat_axis=0, axis_index_groups=[order], tiled=True)
+
+
 def start_rows(state, speed, faces_ref, out_ref, edges_ref, base):
     tiles = out_ref.shape[0]
     rows = state[0].shape[0]
@@ -159,8 +171,9 @@
         state = tile_substep(state, opens, *terms, False)
     lane = lane_index((rows, LANES))
     edges = jnp.zeros((rows, LANES), jnp.float32)
+    place = places(tiles)
     for tile in range(tiles):
-        out_ref[tile, base : base + rows, :] = state[tile]
+        out_ref[place[tile], base : base + rows, :] = state[tile]
         mine = (lane >= tile * ROWS) & (lane < (tile + 1) * ROWS)
         edges = jnp.where(mine, pltpu.roll(state[tile], tile * ROWS + HALO, 1), edges)
     edges_ref[base : base + rows, :] = edges
@@ -205,10 +218,11 @@
     edges = [turned[tile * ROWS : (tile + 1) * ROWS] for tile in range(tiles)]
     zero = jnp.zeros((ROWS, LANES), jnp.float32)
     last = row_index((ROWS, LANES)) < HALO
+    place = places(tiles)
     for tile in range(tiles):
         before = edges[tile - 1] if tile else zero
         after = edges[tile + 1] if tile + 1 < tiles else zero
-        out_ref[tile, groups:, :] = pltpu.roll(jnp.where(last, before, after), HALO, 0)
+        out_ref[place[tile], groups:, :] = pltpu.roll(jnp.where(last, before, after), HALO, 0)
 
 
 def row_index(shape):
@@ -245,11 +259,12 @@
     ring = LANES + ROWS
     padded = half_ref.shape[0]
     lane = lane_index((ROWS, LANES))
+    place = places(sources)
 
     halos = [jnp.zeros((ROWS, LANES), jnp.float32)] * (blocks + 1)
     for source in range(sources):
         block, at = divmod(source * groups, LANES)
-        halo = blocks_ref[source, groups:, :]
+        halo = blocks_ref[place[source], groups:, :]
         halo = pltpu.roll(halo, at, 1) if at else halo
         halos[block] = jnp.where(lane >= at, halo, halos[block])
         halos[block + 1] = halo
@@ -258,7 +273,7 @@
         pieces = []
         for row in range(part.start, part.stop, ROWS):
             source, at = divmod(row, groups)
-            pieces.append(blocks_ref[source, at : at + ROWS, :])
+            pieces.append(blocks_ref[place[source], at : at + ROWS, :])
         state_ref[:LANES, part] = jnp.transpose(jnp.concatenate(pieces, axis=0))
         state_ref[LANES:ring, part] = halos[block]
     state_ref[ring:, :] = jnp.zeros((padded - ring, modes), jnp.float32)
@@ -302,7 +317,25 @@
         state = state_ref[:LANES, wide] + coupling * dot_rows(squared_ref[:LANES, :], back_ref[wide, :])
         for block in range(wide.start // LANES, wide.stop // LANES):
             at = block * LANES - base
-            out_ref[block * LANES : (block + 1) * LANES, :] = jnp.transpose(state[:, at : at + LANES])
+            turned = jnp.transpose(state[:, at : at + LANES])
+            for row in range(0, LANES, ROWS):
+                target, to = divmod(block * LANES + row, groups)
+                out_ref[place[target], to : to + ROWS, :] = turned[row : row + ROWS]
+
+
+def final_kernel(blocks_ref, out_hbm, sems):
+    tiles = blocks_ref.shape[0]
+    place = places(tiles)
+    copies = [
+        pltpu.make_async_copy(
+            blocks_ref.at[place[tile]], out_hbm.at[:, pl.ds(tile * LANES, LANES)], sems.at[tile]
+        )
+        for tile in range(tiles)
+    ]
+    for copy in copies:
+        copy.start()
+    for copy in copies:
+        copy.wait()
 
 
 def tiled_shards(wave_energy, courant, sea_mask, lift_weight, back_weight):
@@ -336,10 +369,10 @@
         cost_estimate=pl.CostEstimate(flops=1000000000, bytes_accessed=3 * 4 * groups * cells, transcendentals=0),
         name="start",
     )(*(pltpu.with_memory_space_constraint(x, pltpu.HBM) for x in inputs))
-    state = lax.all_to_all(start, "cell", split_axis=0, concat_axis=0, tiled=True)
+    state = exchange(start)
     final = pl.pallas_call(
         middle_kernel,
-        out_shape=jax.ShapeDtypeStruct((components, LANES), f32),
+        out_shape=jax.ShapeDtypeStruct((tiles, groups, LANES), f32),
         scratch_shapes=[
             pltpu.VMEM((LANES + 2 * ROWS, components), f32),
             pltpu.VMEM((LANES + 2 * ROWS, components), jnp.bfloat16),
@@ -348,14 +381,22 @@
         compiler_params=pltpu.CompilerParams(vmem_limit_bytes=24 << 20),
         name="middle",
     )(state, courant, faces, lift_weight, back_weight)
-    return lax.all_to_all(final, "cell", split_axis=0, concat_axis=1, tiled=True)
+    return pl.pallas_call(
+        final_kernel,
+        out_shape=jax.ShapeDtypeStruct((groups, cells), f32),
+        in_specs=[vmem],
+        out_specs=any_space,
+        scratch_shapes=[pltpu.SemaphoreType.DMA((tiles,))],
+        compiler_params=pltpu.CompilerParams(vmem_limit_bytes=16 << 20),
+        name="final",
+    )(exchange(final))
 
 
 def shards(wave_energy, courant, sea_mask, lift_weight, back_weight):
     devices = lax.axis_size("cell")
     groups, cells = wave_energy.shape
     whole = cells == devices * LANES and groups % ROWS == 0 and groups <= LANES
-    whole = whole and courant.shape[0] % LANES == 0 and courant.shape[0] <= LANES * LANES // ROWS
+    whole = whole and devices % 2 == 0 and courant.shape[0] % LANES == 0 and courant.shape[0] <= LANES * LANES // ROWS
     run = tiled_shards if whole else general_shards
     return run(wave_energy, courant, sea_mask, lift_weight, back_weight)
 

time: 53.5 us -> 54 us (level)
  Pallas kernels: 6.67 us -> 7.6 us
  local copies, waits for them, and re-layouts: 0.87 us -> 0.01 us
    pallas_call x1 -> x2, Pallas kernels: 3.73 us -> 4.67 us  [the longest x1 3.73 us: tiled_shards(): pl.pallas_call(middle_kernel, out_shape=jax.ShapeDtypeStruct((tiles, grou...]
    all_to_all x1 -> x0, local copies, waits for them, and re-layouts: 0.86 us -> none  [tiled_shards(): lax.all_to_all(final, 'cell', split_axis=0, concat_axis=1, tiled=True)]
where the time goes in v8:
time: 54 us; the launch traced here: 53.8 us
  blocking collectives  46.2 us (86%)
  Pallas kernels  7.6 us (14%)
    all_to_all x2, blocking collectives, exchange(): lax.all_to_all(blocks, 'cell', split_axis=0, concat_axis=0, axis_index_gr...  46.2 us
    pallas_call x1, Pallas kernels, tiled_shards(): pl.pallas_call(middle_kernel, out_shape=jax.ShapeDtypeStruct((tiles, grou...  3.73 us
    pallas_call x1, Pallas kernels, tiled_shards(): pl.pallas_call(start_kernel, out_shape=[jax.ShapeDtypeStruct((tiles, grou...  2.94 us

profile of v8, /device:TPU:0, one launch (start us, length us, event | category | flops | bytes accessed | tf_op | source)
XLA Modules:
  0.0 53.8 jit_solution(9501443160041107102)
XLA Ops:
  0.0 0.0 copy-start
  0.0 0.0 copy-start.1
  0.0 2.9 %start.1 = (f32[16,80,128]{2,1,0:T(8,128)S(1)}, f32[9,128]{1,0:T(8,128)S(1)}, f32[16,128]{1,0:T(8,128)S(1)}) custom-call(f32[72,2048]{1,0:T(8,128)} %energy_hbm.1, f32[9,128]{1,0:T(8,128)} %bitcast.2, s32[16,128]{1,0:T(8,128)} %bitcast.3), custom_call_target="tpu_custom_call" | custom-call | flops 1000000000 | bytes 1769472 | tf_op jit(solution)/shard_map/start/pallas_call | solution.py:351
  2.9 26.0 %all_to_all.10.blocks_ref = f32[16,80,128]{2,1,0:T(8,128)S(1)} all-to-all(f32[16,80,128]{2,1,0:T(8,128)S(1)} %get-tuple-element.8), channel_id=1, replica_groups={{0,8,1,9,2,10,3,11,4,12,5,13,6,14,7,15},{16,24,17,25,18,26,19,27,20,28,..., dimensions={0} | all-to-all | bytes 1310720 | tf_op jit(solution)/shard_map/all_to_all | solution.py:162
  28.9 0.0 copy-done
  28.9 0.0 copy-done.1
  28.9 3.7 %middle.1 = f32[16,72,128]{2,1,0:T(8,128)S(1)} custom-call(f32[16,80,128]{2,1,0:T(8,128)S(1)} %all_to_all.10.blocks_ref, f32[9,128]{1,0:T(8,128)S(1)} %get-tuple-element.9.courant_ref, f32[16,128]{1,0:T(8,128)S(1)} %get-tuple-element.10.faces_ref, bf16[1024,1152]{1,0:T(8,128)(2,1)S(1)} %copy-done, bf16[1152,1024]{1,0:T(8,128)(2,1)S(1)} %copy-done.1), custom_call_target="tpu_custom_call" | custom-call | tf_op jit(solution)/shard_map/middle/pallas_call | solution.py:373
  32.6 20.2 %all_to_all.11.blocks_ref = f32[16,72,128]{2,1,0:T(8,128)S(1)} all-to-all(f32[16,72,128]{2,1,0:T(8,128)S(1)} %middle.1), channel_id=1, replica_groups={{0,8,1,9,2,10,3,11,4,12,5,13,6,14,7,15},{16,24,17,25,18,26,19,27,20,28,..., dimensions={0} | all-to-all | bytes 1179648 | tf_op jit(solution)/shard_map/all_to_all | solution.py:162
  52.8 0.9 %final.1 = f32[72,2048]{1,0:T(8,128)} custom-call(f32[16,72,128]{2,1,0:T(8,128)S(1)} %all_to_all.11.blocks_ref), custom_call_target="tpu_custom_call" | custom-call | tf_op jit(solution)/shard_map/final/pallas_call | solution.py:384
Async XLA Ops:
  0.0 28.9 %copy-start = (bf16[1024,1152]{1,0:T(8,128)(2,1)S(1)}, bf16[1024,1152]{1,0:T(8,128)(2,1)}, u32[]{:S(2)}) copy-start(bf16[1024,1152]{1,0:T(8,128)(2,1)} %lift_ref.1) | copy-start | bytes 7077892
  0.0 28.9 %copy-start.1 = (bf16[1152,1024]{1,0:T(8,128)(2,1)S(1)}, bf16[1152,1024]{1,0:T(8,128)(2,1)}, u32[]{:S(2)}) copy-start(bf16[1152,1024]{1,0:T(8,128)(2,1)} %back_ref.1) | copy-start | bytes 7077892

commit v9 on v7

--- a/solution.py
+++ b/solution.py
@@ -147,10 +147,7 @@
     return sea * jnp.where(lane_index(sea.shape) == LANES - 1, below, turned)
 
 
-START_ROWS = 40
-
-
-def start_rows(state, speed, faces_ref, out_ref, edges_ref, base):
+def start_rows(state, speed, faces_ref, out_ref, edges_ref):
     tiles = out_ref.shape[0]
     rows = state[0].shape[0]
     terms = speed_terms(speed)
@@ -160,10 +157,10 @@
     lane = lane_index((rows, LANES))
     edges = jnp.zeros((rows, LANES), jnp.float32)
     for tile in range(tiles):
-        out_ref[tile, base : base + rows, :] = state[tile]
+        out_ref[tile, :rows, :] = state[tile]
         mine = (lane >= tile * ROWS) & (lane < (tile + 1) * ROWS)
         edges = jnp.where(mine, pltpu.roll(state[tile], tile * ROWS + HALO, 1), edges)
-    edges_ref[base : base + rows, :] = edges
+    edges_ref[:rows, :] = edges
 
 
 def start_kernel(
@@ -172,15 +169,13 @@
 ):
     groups = energy_ref.shape[0]
     tiles = out_ref.shape[0]
-    bases = list(range(0, groups, START_ROWS))
-    sizes = [min(START_ROWS, groups - base) for base in bases]
     small = pltpu.make_async_copy(courant_hbm, courant_ref, sems.at[0])
     sea = pltpu.make_async_copy(sea_hbm, sea_ref, sems.at[1])
     state_copies = [
         pltpu.make_async_copy(
-            energy_hbm.at[pl.ds(base, size), :], energy_ref.at[pl.ds(base, size), :], energy_sems.at[step]
-        )
-        for step, (base, size) in enumerate(zip(bases, sizes))
+            energy_hbm.at[pl.ds(step * ROWS, ROWS), :], energy_ref.at[pl.ds(step * ROWS, ROWS), :], energy_sems.at[step]
+        )
+        for step in range(groups // ROWS)
     ]
     small.start()
     sea.start()
@@ -192,14 +187,11 @@
     sea.wait()
     faces_ref[...] = face_rows(sea_ref[...].astype(jnp.float32))
     rank = lax.axis_index("cell")
-    for copy, base, size in zip(state_copies, bases, sizes):
+    speed = speeds_ref[pl.ds(pl.multiple_of(rank * groups, ROWS), groups), :]
+    for copy in state_copies:
         copy.wait()
-        own = pl.multiple_of(rank * groups + base, ROWS)
-        speed = speeds_ref[pl.ds(own, size), :]
-        state = [
-            energy_ref[base : base + size, tile * LANES : (tile + 1) * LANES] for tile in range(tiles)
-        ]
-        start_rows(state, speed, faces_ref, out_ref, edges_ref, base)
+    state = [energy_ref[:, tile * LANES : (tile + 1) * LANES] for tile in range(tiles)]
+    start_rows(state, speed, faces_ref, out_ref, edges_ref)
 
     turned = jnp.transpose(edges_ref[...])
     edges = [turned[tile * ROWS : (tile + 1) * ROWS] for tile in range(tiles)]
@@ -279,24 +271,27 @@
     )
     turned = jnp.transpose(square)
     column = jnp.concatenate([turned[:, 0:1], turned[:ROWS, 1:2]], axis=0)
-    opens = jnp.broadcast_to(column, (ring, LANES))
-
-    chunk = 2 * LANES
-    for base in range(0, modes, chunk):
-        wide = slice(base, min(base + chunk, modes))
+    chunk = 4 * LANES
+    bases = list(range(0, modes, chunk))
+    if len(bases) > 1 and modes - bases[-1] < chunk // 2:
+        bases.pop()
+    for base, stop in zip(bases, bases[1:] + [modes]):
+        wide = slice(base, stop)
         source = dot_rows(squared_ref[...], back_ref[wide, :])
-        for block in range(wide.start // LANES, wide.stop // LANES):
-            part = slice(block * LANES, (block + 1) * LANES)
-            at = part.start - base
-            state = state_ref[:ring, part] + coupling * source[:ring, at : at + LANES]
-            terms = speed_terms(courant_ref[block : block + 1, :])
-            for turn in range(2):
-                state = row_substep(state, opens, *terms)
-            state_ref[:LANES, part] = state[:LANES]
-            half_ref[:LANES, part] = state[:LANES].astype(jnp.bfloat16)
+        state = state_ref[:ring, wide] + coupling * source[:ring]
+        speed = jnp.concatenate(
+            [courant_ref[block : block + 1, :] for block in range(base // LANES, stop // LANES)], axis=1
+        )
+        terms = speed_terms(speed)
+        opens = jnp.broadcast_to(column, state.shape)
+        for turn in range(2):
+            state = row_substep(state, opens, *terms)
+        state_ref[:LANES, wide] = state[:LANES]
+        half_ref[:LANES, wide] = state[:LANES].astype(jnp.bfloat16)
 
     lifted = dot_rows(half_ref[:LANES, :], lift_ref[...])
     squared_ref[:LANES, :] = (lifted * lifted).astype(jnp.bfloat16)
+    chunk = 2 * LANES
     for base in range(0, modes, chunk):
         wide = slice(base, min(base + chunk, modes))
         state = state_ref[:LANES, wide] + coupling * dot_rows(squared_ref[:LANES, :], back_ref[wide, :])
@@ -330,7 +325,7 @@
             pltpu.VMEM((components, LANES), f32),
             pltpu.VMEM((LANES, LANES), f32),
             pltpu.SemaphoreType.DMA((2,)),
-            pltpu.SemaphoreType.DMA((-(-groups // START_ROWS),)),
+            pltpu.SemaphoreType.DMA((groups // ROWS,)),
         ],
         compiler_params=pltpu.CompilerParams(vmem_limit_bytes=16 << 20),
         cost_estimate=pl.CostEstimate(flops=1000000000, bytes_accessed=3 * 4 * groups * cells, transcendentals=0),

time: 53.5 us -> 53.7 us (level)
  no operation moved by 1% of the time
where the time goes in v9:
time: 53.7 us; the launch traced here: 53.5 us
  blocking collectives  45.7 us (85%)
  Pallas kernels  6.82 us (13%)
  local copies, waits for them, and re-layouts  0.87 us (2%)
    all_to_all x1, blocking collectives, tiled_shards(): lax.all_to_all(start, 'cell', split_axis=0, concat_axis=0, tiled=True)  25.4 us
    all_to_all x1, blocking collectives, tiled_shards(): lax.all_to_all(final, 'cell', split_axis=0, concat_axis=1, tiled=True)  20.4 us
    pallas_call x1, Pallas kernels, tiled_shards(): pl.pallas_call(middle_kernel, out_shape=jax.ShapeDtypeStruct((components,...  3.7 us
    pallas_call x1, Pallas kernels, tiled_shards(): pl.pallas_call(start_kernel, out_shape=[jax.ShapeDtypeStruct((tiles, grou...  3.12 us

profile of v9, /device:TPU:0, one launch (start us, length us, event | category | flops | bytes accessed | tf_op | source)
XLA Modules:
  0.0 53.5 jit_solution(1759706566838244630)
XLA Ops:
  0.0 0.0 copy-start
  0.0 0.0 copy-start.1
  0.0 3.1 %start.1 = (f32[16,80,128]{2,1,0:T(8,128)S(1)}, f32[9,128]{1,0:T(8,128)S(1)}, f32[16,128]{1,0:T(8,128)S(1)}) custom-call(f32[72,2048]{1,0:T(8,128)} %energy_hbm.1, f32[9,128]{1,0:T(8,128)} %bitcast.10, s32[16,128]{1,0:T(8,128)} %bitcast.11), custom_call_target="tpu_custom_call" | custom-call | flops 1000000000 | bytes 1769472 | tf_op jit(solution)/shard_map/start/pallas_call | solution.py:313
  3.1 25.4 %all_to_all.24.blocks_ref = f32[16,80,128]{2,1,0:T(8,128)S(1)} all-to-all(f32[16,80,128]{2,1,0:T(8,128)S(1)} %get-tuple-element.8), channel_id=1, replica_groups=mesh['member'=2,'cell'=16] {'cell'}, dimensions={0} | all-to-all | bytes 1310720 | tf_op jit(solution)/shard_map/all_to_all | solution.py:334
  28.5 0.0 copy-done
  28.5 0.0 copy-done.1
  28.5 3.7 %middle.1 = f32[1152,128]{1,0:T(8,128)S(1)} custom-call(f32[16,80,128]{2,1,0:T(8,128)S(1)} %all_to_all.24.blocks_ref, f32[9,128]{1,0:T(8,128)S(1)} %get-tuple-element.9.courant_ref, f32[16,128]{1,0:T(8,128)S(1)} %get-tuple-element.10.faces_ref, bf16[1024,1152]{1,0:T(8,128)(2,1)S(1)} %copy-done, bf16[1152,1024]{1,0:T(8,128)(2,1)S(1)} %copy-done.1), custom_call_target="tpu_custom_call" | custom-call | tf_op jit(solution)/shard_map/middle/pallas_call | solution.py:335
  32.2 20.4 %all_to_all.25 = f32[16,72,128]{2,1,0:T(8,128)S(1)} all-to-all(f32[16,72,128]{2,1,0:T(8,128)S(1)} %bitcast.9), channel_id=1, replica_groups=mesh['member'=2,'cell'=16] {'cell'}, dimensions={0} | all-to-all | bytes 1179648 | tf_op jit(solution)/shard_map/all_to_all | solution.py:346
  52.6 0.9 %copy_bitcast_fusion = f32[72,2048]{1,0:T(8,128)} fusion(f32[16,72,128]{2,1,0:T(8,128)S(1)} %all_to_all.25), kind=kLoop, calls=%fused_computation | loop fusion | bytes 1179648 | tf_op jit(solution)/shard_map/all_to_all | solution.py:346
Async XLA Ops:
  0.0 28.5 %copy-start = (bf16[1024,1152]{1,0:T(8,128)(2,1)S(1)}, bf16[1024,1152]{1,0:T(8,128)(2,1)}, u32[]{:S(2)}) copy-start(bf16[1024,1152]{1,0:T(8,128)(2,1)} %lift_ref.1) | copy-start | bytes 7077892
  0.0 28.5 %copy-start.1 = (bf16[1152,1024]{1,0:T(8,128)(2,1)S(1)}, bf16[1152,1024]{1,0:T(8,128)(2,1)}, u32[]{:S(2)}) copy-start(bf16[1152,1024]{1,0:T(8,128)(2,1)} %back_ref.1) | copy-start | bytes 7077892

commit v10 on v7

--- a/solution.py
+++ b/solution.py
@@ -215,16 +215,23 @@
     return lax.broadcasted_iota(jnp.int32, shape, 0)
 
 
-def row_substep(state, opens, speed, slope_speed, forward):
-    rows = state.shape[0]
-    steps = pltpu.roll(state, rows - 1, 0) - state
-    left_steps = pltpu.roll(steps, 1, 0)
-    slopes = jnp.maximum(
-        jnp.minimum(steps, left_steps), jnp.minimum(jnp.maximum(steps, left_steps), 0.0)
-    )
-    amounts = speed * state + slope_speed * slopes
-    fluxes = opens * jnp.where(forward, amounts, pltpu.roll(amounts, rows - 1, 0))
-    return state - (fluxes - pltpu.roll(fluxes, 1, 0))
+def ring_substep(state, opens, speed, slope_speed, forward):
+    def following(values):
+        return values[1:] + [pltpu.roll(values[0], ROWS - 1, 0)]
+
+    def preceding(values):
+        return [pltpu.roll(values[-1], 1, 0)] + values[:-1]
+
+    steps = [b - a for a, b in zip(state, following(state))]
+    slopes = [
+        jnp.maximum(jnp.minimum(a, b), jnp.minimum(jnp.maximum(a, b), 0.0))
+        for a, b in zip(steps, preceding(steps))
+    ]
+    amounts = [speed * u + slope_speed * s for u, s in zip(state, slopes)]
+    fluxes = [
+        face * jnp.where(forward, a, b) for face, a, b in zip(opens, amounts, following(amounts))
+    ]
+    return [u - (f - g) for u, f, g in zip(state, fluxes, preceding(fluxes))]
 
 
 def dot_rows(values, weights):
@@ -234,7 +241,7 @@
 
 
 def middle_kernel(
-    blocks_ref, courant_ref, faces_ref, lift_ref, back_ref, out_ref, state_ref, half_ref, squared_ref
+    blocks_ref, courant_ref, faces_ref, lift_ref, back_ref, out_ref, ring_ref, opens_ref, half_ref, squared_ref
 ):
     sources, rows, _ = blocks_ref.shape
     groups = rows - ROWS
@@ -259,10 +266,12 @@
         for row in range(part.start, part.stop, ROWS):
             source, at = divmod(row, groups)
             pieces.append(blocks_ref[source, at : at + ROWS, :])
-        state_ref[:LANES, part] = jnp.transpose(jnp.concatenate(pieces, axis=0))
-        state_ref[LANES:ring, part] = halos[block]
-    state_ref[ring:, :] = jnp.zeros((padded - ring, modes), jnp.float32)
-    half_ref[...] = state_ref[...].astype(jnp.bfloat16)
+        own = jnp.transpose(jnp.concatenate(pieces, axis=0))
+        ring_ref[block, :LANES, :] = own
+        ring_ref[block, LANES:, :] = halos[block]
+        half_ref[:LANES, part] = own.astype(jnp.bfloat16)
+        beside = jnp.concatenate([halos[block], jnp.zeros((padded - ring, LANES), jnp.float32)], axis=0)
+        half_ref[LANES:, part] = beside.astype(jnp.bfloat16)
 
     lifted = dot_rows(half_ref[...], lift_ref[...])
     squared_ref[...] = (lifted * lifted).astype(jnp.bfloat16)
@@ -279,7 +288,10 @@
     )
     turned = jnp.transpose(square)
     column = jnp.concatenate([turned[:, 0:1], turned[:ROWS, 1:2]], axis=0)
-    opens = jnp.broadcast_to(column, (ring, LANES))
+    opens_ref[...] = jnp.broadcast_to(column, (ring, LANES))
+    stride = ring // ROWS
+    strided = [pl.ds(at, ROWS, stride=stride) for at in range(stride)]
+    opens = [opens_ref[rows, :] for rows in strided]
 
     chunk = 2 * LANES
     for base in range(0, modes, chunk):
@@ -288,21 +300,24 @@
         for block in range(wide.start // LANES, wide.stop // LANES):
             part = slice(block * LANES, (block + 1) * LANES)
             at = part.start - base
-            state = state_ref[:ring, part] + coupling * source[:ring, at : at + LANES]
-            terms = speed_terms(courant_ref[block : block + 1, :])
+            ring_ref[block] += coupling * source[:ring, at : at + LANES]
+            terms = speed_terms(jnp.broadcast_to(courant_ref[block : block + 1, :], (ROWS, LANES)))
+            state = [ring_ref[block, rows, :] for rows in strided]
             for turn in range(2):
-                state = row_substep(state, opens, *terms)
-            state_ref[:LANES, part] = state[:LANES]
-            half_ref[:LANES, part] = state[:LANES].astype(jnp.bfloat16)
+                state = ring_substep(state, opens, *terms)
+            for rows, values in zip(strided, state):
+                ring_ref[block, rows, :] = values
+            half_ref[:LANES, part] = ring_ref[block, :LANES, :].astype(jnp.bfloat16)
 
     lifted = dot_rows(half_ref[:LANES, :], lift_ref[...])
     squared_ref[:LANES, :] = (lifted * lifted).astype(jnp.bfloat16)
     for base in range(0, modes, chunk):
         wide = slice(base, min(base + chunk, modes))
-        state = state_ref[:LANES, wide] + coupling * dot_rows(squared_ref[:LANES, :], back_ref[wide, :])
+        source = coupling * dot_rows(squared_ref[:LANES, :], back_ref[wide, :])
         for block in range(wide.start // LANES, wide.stop // LANES):
             at = block * LANES - base
-            out_ref[block * LANES : (block + 1) * LANES, :] = jnp.transpose(state[:, at : at + LANES])
+            state = ring_ref[block, :LANES, :] + source[:, at : at + LANES]
+            out_ref[block * LANES : (block + 1) * LANES, :] = jnp.transpose(state)
 
 
 def tiled_shards(wave_energy, courant, sea_mask, lift_weight, back_weight):
@@ -341,7 +356,8 @@
         middle_kernel,
         out_shape=jax.ShapeDtypeStruct((components, LANES), f32),
         scratch_shapes=[
-            pltpu.VMEM((LANES + 2 * ROWS, components), f32),
+            pltpu.VMEM((components // LANES, LANES + ROWS, LANES), f32),
+            pltpu.VMEM((LANES + ROWS, LANES), f32),
             pltpu.VMEM((LANES + 2 * ROWS, components), jnp.bfloat16),
             pltpu.VMEM((LANES + 2 * ROWS, lift_weight.shape[0]), jnp.bfloat16),
         ],

time: 53.5 us -> 53.4 us (level)
  no operation moved by 1% of the time
where the time goes in v10:
time: 53.4 us; the launch traced here: 53.2 us
  blocking collectives  45.7 us (86%)
  Pallas kernels  6.59 us (12%)
  local copies, waits for them, and re-layouts  0.87 us (2%)
    all_to_all x1, blocking collectives, tiled_shards(): lax.all_to_all(start, 'cell', split_axis=0, concat_axis=0, tiled=True)  25.4 us
    all_to_all x1, blocking collectives, tiled_shards(): lax.all_to_all(final, 'cell', split_axis=0, concat_axis=1, tiled=True)  20.4 us
    pallas_call x1, Pallas kernels, tiled_shards(): pl.pallas_call(middle_kernel, out_shape=jax.ShapeDtypeStruct((components,...  3.65 us
    pallas_call x1, Pallas kernels, tiled_shards(): pl.pallas_call(start_kernel, out_shape=[jax.ShapeDtypeStruct((tiles, grou...  2.94 us

profile of v10, /device:TPU:0, one launch (start us, length us, event | category | flops | bytes accessed | tf_op | source)
XLA Modules:
  0.0 53.2 jit_solution(7066428804469303087)
XLA Ops:
  0.0 0.0 copy-start
  0.0 0.0 copy-start.1
  0.0 2.9 %start.1 = (f32[16,80,128]{2,1,0:T(8,128)S(1)}, f32[9,128]{1,0:T(8,128)S(1)}, f32[16,128]{1,0:T(8,128)S(1)}) custom-call(f32[72,2048]{1,0:T(8,128)} %energy_hbm.1, f32[9,128]{1,0:T(8,128)} %bitcast.10, s32[16,128]{1,0:T(8,128)} %bitcast.11), custom_call_target="tpu_custom_call" | custom-call | flops 1000000000 | bytes 1769472 | tf_op jit(solution)/shard_map/start/pallas_call | solution.py:333
  2.9 25.4 %all_to_all.24.blocks_ref = f32[16,80,128]{2,1,0:T(8,128)S(1)} all-to-all(f32[16,80,128]{2,1,0:T(8,128)S(1)} %get-tuple-element.8), channel_id=1, replica_groups=mesh['member'=2,'cell'=16] {'cell'}, dimensions={0} | all-to-all | bytes 1310720 | tf_op jit(solution)/shard_map/all_to_all | solution.py:354
  28.3 0.0 copy-done
  28.3 0.0 copy-done.1
  28.3 3.7 %middle.1 = f32[1152,128]{1,0:T(8,128)S(1)} custom-call(f32[16,80,128]{2,1,0:T(8,128)S(1)} %all_to_all.24.blocks_ref, f32[9,128]{1,0:T(8,128)S(1)} %get-tuple-element.9.courant_ref, f32[16,128]{1,0:T(8,128)S(1)} %get-tuple-element.10.faces_ref, bf16[1024,1152]{1,0:T(8,128)(2,1)S(1)} %copy-done, bf16[1152,1024]{1,0:T(8,128)(2,1)S(1)} %copy-done.1), custom_call_target="tpu_custom_call" | custom-call | tf_op jit(solution)/shard_map/middle/pallas_call | solution.py:355
  32.0 20.4 %all_to_all.25 = f32[16,72,128]{2,1,0:T(8,128)S(1)} all-to-all(f32[16,72,128]{2,1,0:T(8,128)S(1)} %bitcast.9), channel_id=1, replica_groups=mesh['member'=2,'cell'=16] {'cell'}, dimensions={0} | all-to-all | bytes 1179648 | tf_op jit(solution)/shard_map/all_to_all | solution.py:367
  52.4 0.9 %copy_bitcast_fusion = f32[72,2048]{1,0:T(8,128)} fusion(f32[16,72,128]{2,1,0:T(8,128)S(1)} %all_to_all.25), kind=kLoop, calls=%fused_computation | loop fusion | bytes 1179648 | tf_op jit(solution)/shard_map/all_to_all | solution.py:367
Async XLA Ops:
  0.0 28.3 %copy-start = (bf16[1024,1152]{1,0:T(8,128)(2,1)S(1)}, bf16[1024,1152]{1,0:T(8,128)(2,1)}, u32[]{:S(2)}) copy-start(bf16[1024,1152]{1,0:T(8,128)(2,1)} %lift_ref.1) | copy-start | bytes 7077892
  0.0 28.3 %copy-start.1 = (bf16[1152,1024]{1,0:T(8,128)(2,1)S(1)}, bf16[1152,1024]{1,0:T(8,128)(2,1)}, u32[]{:S(2)}) copy-start(bf16[1152,1024]{1,0:T(8,128)(2,1)} %back_ref.1) | copy-start | bytes 7077892

commit v11 on v10

--- a/solution.py
+++ b/solution.py
@@ -260,6 +260,9 @@
         halo = pltpu.roll(halo, at, 1) if at else halo
         halos[block] = jnp.where(lane >= at, halo, halos[block])
         halos[block + 1] = halo
+    chunk = 2 * LANES
+    wides = [slice(base, min(base + chunk, modes)) for base in range(0, modes, chunk)]
+    lifted = None
     for block in range(blocks):
         part = slice(block * LANES, (block + 1) * LANES)
         pieces = []
@@ -272,8 +275,10 @@
         half_ref[:LANES, part] = own.astype(jnp.bfloat16)
         beside = jnp.concatenate([halos[block], jnp.zeros((padded - ring, LANES), jnp.float32)], axis=0)
         half_ref[LANES:, part] = beside.astype(jnp.bfloat16)
-
-    lifted = dot_rows(half_ref[...], lift_ref[...])
+        for wide in wides:
+            if wide.stop == part.stop:
+                term = dot_rows(half_ref[:, wide], lift_ref[:, wide])
+                lifted = term if lifted is None else lifted + term
     squared_ref[...] = (lifted * lifted).astype(jnp.bfloat16)
 
     own_faces = faces_ref[pl.ds(rank, 1), :]
@@ -293,13 +298,12 @@
     strided = [pl.ds(at, ROWS, stride=stride) for at in range(stride)]
     opens = [opens_ref[rows, :] for rows in strided]
 
-    chunk = 2 * LANES
-    for base in range(0, modes, chunk):
-        wide = slice(base, min(base + chunk, modes))
+    lifted = None
+    for wide in wides:
         source = dot_rows(squared_ref[...], back_ref[wide, :])
         for block in range(wide.start // LANES, wide.stop // LANES):
             part = slice(block * LANES, (block + 1) * LANES)
-            at = part.start - base
+            at = part.start - wide.start
             ring_ref[block] += coupling * source[:ring, at : at + LANES]
             terms = speed_terms(jnp.broadcast_to(courant_ref[block : block + 1, :], (ROWS, LANES)))
             state = [ring_ref[block, rows, :] for rows in strided]
@@ -308,14 +312,14 @@
             for rows, values in zip(strided, state):
                 ring_ref[block, rows, :] = values
             half_ref[:LANES, part] = ring_ref[block, :LANES, :].astype(jnp.bfloat16)
-
-    lifted = dot_rows(half_ref[:LANES, :], lift_ref[...])
+        term = dot_rows(half_ref[:LANES, wide], lift_ref[:, wide])
+        lifted = term if lifted is None else lifted + term
+
     squared_ref[:LANES, :] = (lifted * lifted).astype(jnp.bfloat16)
-    for base in range(0, modes, chunk):
-        wide = slice(base, min(base + chunk, modes))
+    for wide in wides:
         source = coupling * dot_rows(squared_ref[:LANES, :], back_ref[wide, :])
         for block in range(wide.start // LANES, wide.stop // LANES):
-            at = block * LANES - base
+            at = block * LANES - wide.start
             state = ring_ref[block, :LANES, :] + source[:, at : at + LANES]
             out_ref[block * LANES : (block + 1) * LANES, :] = jnp.transpose(state)
 

time: 53.4 us -> 54.3 us (1.017)
  Pallas kernels: 6.59 us -> 7.49 us
    pallas_call x1, Pallas kernels: 3.65 us -> 4.55 us  [tiled_shards(): pl.pallas_call(middle_kernel, out_shape=jax.ShapeDtypeStruct((components,...]
where the time goes in v11:
time: 54.3 us; the launch traced here: 54.1 us
  blocking collectives  45.7 us (84%)
  Pallas kernels  7.49 us (14%)
  local copies, waits for them, and re-layouts  0.87 us (2%)
    all_to_all x1, blocking collectives, tiled_shards(): lax.all_to_all(start, 'cell', split_axis=0, concat_axis=0, tiled=True)  25.4 us
    all_to_all x1, blocking collectives, tiled_shards(): lax.all_to_all(final, 'cell', split_axis=0, concat_axis=1, tiled=True)  20.4 us
    pallas_call x1, Pallas kernels, tiled_shards(): pl.pallas_call(middle_kernel, out_shape=jax.ShapeDtypeStruct((components,...  4.55 us
    pallas_call x1, Pallas kernels, tiled_shards(): pl.pallas_call(start_kernel, out_shape=[jax.ShapeDtypeStruct((tiles, grou...  2.94 us

profile of v11, /device:TPU:0, one launch (start us, length us, event | category | flops | bytes accessed | tf_op | source)
XLA Modules:
  0.0 54.1 jit_solution(3269533753146238991)
XLA Ops:
  0.0 0.0 copy-start
  0.0 0.0 copy-start.1
  0.0 2.9 %start.1 = (f32[16,80,128]{2,1,0:T(8,128)S(1)}, f32[9,128]{1,0:T(8,128)S(1)}, f32[16,128]{1,0:T(8,128)S(1)}) custom-call(f32[72,2048]{1,0:T(8,128)} %energy_hbm.1, f32[9,128]{1,0:T(8,128)} %bitcast.10, s32[16,128]{1,0:T(8,128)} %bitcast.11), custom_call_target="tpu_custom_call" | custom-call | flops 1000000000 | bytes 1769472 | tf_op jit(solution)/shard_map/start/pallas_call | solution.py:337
  2.9 25.4 %all_to_all.24.blocks_ref = f32[16,80,128]{2,1,0:T(8,128)S(1)} all-to-all(f32[16,80,128]{2,1,0:T(8,128)S(1)} %get-tuple-element.8), channel_id=1, replica_groups=mesh['member'=2,'cell'=16] {'cell'}, dimensions={0} | all-to-all | bytes 1310720 | tf_op jit(solution)/shard_map/all_to_all | solution.py:358
  28.3 0.0 copy-done
  28.3 0.0 copy-done.1
  28.3 4.6 %middle.1 = f32[1152,128]{1,0:T(8,128)S(1)} custom-call(f32[16,80,128]{2,1,0:T(8,128)S(1)} %all_to_all.24.blocks_ref, f32[9,128]{1,0:T(8,128)S(1)} %get-tuple-element.9.courant_ref, f32[16,128]{1,0:T(8,128)S(1)} %get-tuple-element.10.faces_ref, bf16[1024,1152]{1,0:T(8,128)(2,1)S(1)} %copy-done, bf16[1152,1024]{1,0:T(8,128)(2,1)S(1)} %copy-done.1), custom_call_target="tpu_custom_call" | custom-call | tf_op jit(solution)/shard_map/middle/pallas_call | solution.py:359
  32.9 20.4 %all_to_all.25 = f32[16,72,128]{2,1,0:T(8,128)S(1)} all-to-all(f32[16,72,128]{2,1,0:T(8,128)S(1)} %bitcast.9), channel_id=1, replica_groups=mesh['member'=2,'cell'=16] {'cell'}, dimensions={0} | all-to-all | bytes 1179648 | tf_op jit(solution)/shard_map/all_to_all | solution.py:371
  53.3 0.9 %copy_bitcast_fusion = f32[72,2048]{1,0:T(8,128)} fusion(f32[16,72,128]{2,1,0:T(8,128)S(1)} %all_to_all.25), kind=kLoop, calls=%fused_computation | loop fusion | bytes 1179648 | tf_op jit(solution)/shard_map/all_to_all | solution.py:371
Async XLA Ops:
  0.0 28.3 %copy-start = (bf16[1024,1152]{1,0:T(8,128)(2,1)S(1)}, bf16[1024,1152]{1,0:T(8,128)(2,1)}, u32[]{:S(2)}) copy-start(bf16[1024,1152]{1,0:T(8,128)(2,1)} %lift_ref.1) | copy-start | bytes 7077892
  0.0 28.3 %copy-start.1 = (bf16[1152,1024]{1,0:T(8,128)(2,1)S(1)}, bf16[1152,1024]{1,0:T(8,128)(2,1)}, u32[]{:S(2)}) copy-start(bf16[1152,1024]{1,0:T(8,128)(2,1)} %back_ref.1) | copy-start | bytes 7077892

commit v12 on v10

--- a/solution.py
+++ b/solution.py
@@ -234,10 +234,8 @@
     return [u - (f - g) for u, f, g in zip(state, fluxes, preceding(fluxes))]
 
 
-def dot_rows(values, weights):
-    return lax.dot_general(
-        values, weights, (((1,), (1,)), ((), ())), preferred_element_type=jnp.float32
-    )
+def dot(values, weights):
+    return jnp.dot(values, weights, preferred_element_type=jnp.float32)
 
 
 def middle_kernel(
@@ -273,7 +271,7 @@
         beside = jnp.concatenate([halos[block], jnp.zeros((padded - ring, LANES), jnp.float32)], axis=0)
         half_ref[LANES:, part] = beside.astype(jnp.bfloat16)
 
-    lifted = dot_rows(half_ref[...], lift_ref[...])
+    lifted = dot(half_ref[...], lift_ref[...])
     squared_ref[...] = (lifted * lifted).astype(jnp.bfloat16)
 
     own_faces = faces_ref[pl.ds(rank, 1), :]
@@ -296,7 +294,7 @@
     chunk = 2 * LANES
     for base in range(0, modes, chunk):
         wide = slice(base, min(base + chunk, modes))
-        source = dot_rows(squared_ref[...], back_ref[wide, :])
+        source = dot(squared_ref[...], back_ref[:, wide])
         for block in range(wide.start // LANES, wide.stop // LANES):
             part = slice(block * LANES, (block + 1) * LANES)
             at = part.start - base
@@ -309,11 +307,11 @@
                 ring_ref[block, rows, :] = values
             half_ref[:LANES, part] = ring_ref[block, :LANES, :].astype(jnp.bfloat16)
 
-    lifted = dot_rows(half_ref[:LANES, :], lift_ref[...])
+    lifted = dot(half_ref[:LANES, :], lift_ref[...])
     squared_ref[:LANES, :] = (lifted * lifted).astype(jnp.bfloat16)
     for base in range(0, modes, chunk):
         wide = slice(base, min(base + chunk, modes))
-        source = coupling * dot_rows(squared_ref[:LANES, :], back_ref[wide, :])
+        source = coupling * dot(squared_ref[:LANES, :], back_ref[:, wide])
         for block in range(wide.start // LANES, wide.stop // LANES):
             at = block * LANES - base
             state = ring_ref[block, :LANES, :] + source[:, at : at + LANES]
@@ -363,7 +361,7 @@
         ],
         compiler_params=pltpu.CompilerParams(vmem_limit_bytes=24 << 20),
         name="middle",
-    )(state, courant, faces, lift_weight, back_weight)
+    )(state, courant, faces, lift_weight.T, back_weight.T)
     return lax.all_to_all(final, "cell", split_axis=0, concat_axis=1, tiled=True)
 
 

time: 53.4 us -> 54.9 us (1.028)
  blocking collectives: 45.7 us -> 21.9 us
  waiting for transfers between devices: 0 us -> 9.38 us
  local copies, waits for them, and re-layouts: 0.87 us -> 9.74 us
  starting transfers between devices: 0 us -> 7.37 us
    all_to_all x1 -> x0, blocking collectives: 25.4 us -> none  [tiled_shards(): lax.all_to_all(start, 'cell', split_axis=0, concat_axis=0, tiled=True)]
    all_to_all x0 -> x1, waiting for transfers between devices: none -> 9.38 us  [tiled_shards(): lax.all_to_all(start, 'cell', split_axis=0, concat_axis=0, tiled=True)]
    unnamed x4, local copies, waits for them, and re-layouts: 0.01 us -> 8.88 us
    all_to_all x0 -> x1, starting transfers between devices: none -> 7.37 us  [tiled_shards(): lax.all_to_all(start, 'cell', split_axis=0, concat_axis=0, tiled=True)]
    all_to_all x1, blocking collectives: 20.4 us -> 21.9 us  [tiled_shards(): lax.all_to_all(final, 'cell', split_axis=0, concat_axis=1, tiled=True)]
    pallas_call x1, Pallas kernels: 3.65 us -> 2.51 us  [tiled_shards(): pl.pallas_call(middle_kernel, out_shape=jax.ShapeDtypeStruct((components,...]
    pallas_call x1, Pallas kernels: 2.94 us -> 3.63 us  [tiled_shards(): pl.pallas_call(start_kernel, out_shape=[jax.ShapeDtypeStruct((tiles, grou...]
  transfers between devices with their start and end apart: 0 -> 1, of which waited for: 0 -> 1; matrix products, arithmetic and copies ran while one was open for 0% -> 13% of each run, Pallas kernels for 0% -> 0%
where the time goes in v12:
time: 54.9 us; the launch traced here: 54.5 us
  blocking collectives  21.9 us (40%)
  local copies, waits for them, and re-layouts  9.74 us (18%)
  waiting for transfers between devices  9.38 us (17%)
  starting transfers between devices  7.37 us (13%)
  Pallas kernels  6.14 us (11%)
    all_to_all x1, blocking collectives, tiled_shards(): lax.all_to_all(final, 'cell', split_axis=0, concat_axis=1, tiled=True)  21.9 us
    all_to_all x1, waiting for transfers between devices, tiled_shards(): lax.all_to_all(start, 'cell', split_axis=0, concat_axis=0, tiled=True)  9.38 us
    unnamed x4, local copies, waits for them, and re-layouts  8.88 us
    all_to_all x1, starting transfers between devices, tiled_shards(): lax.all_to_all(start, 'cell', split_axis=0, concat_axis=0, tiled=True)  7.37 us
    pallas_call x1, Pallas kernels, tiled_shards(): pl.pallas_call(start_kernel, out_shape=[jax.ShapeDtypeStruct((tiles, grou...  3.63 us
    pallas_call x1, Pallas kernels, tiled_shards(): pl.pallas_call(middle_kernel, out_shape=jax.ShapeDtypeStruct((components,...  2.51 us
  transfers between devices with their start and end apart: 1, of which 1 were waited for; matrix products, arithmetic and copies ran while one was open for 13% of the time, Pallas kernels for 0%

profile of v12, /device:TPU:0, one launch (start us, length us, event | category | flops | bytes accessed | tf_op | source)
XLA Modules:
  0.0 54.5 jit_solution(2002057699582813991)
XLA Ops:
  0.0 3.6 %start.1 = (f32[16,80,128]{2,1,0:T(8,128)}, f32[9,128]{1,0:T(8,128)S(1)}, f32[16,128]{1,0:T(8,128)S(1)}) custom-call(f32[72,2048]{1,0:T(8,128)} %energy_hbm.1, f32[9,128]{1,0:T(8,128)} %bitcast.14, s32[16,128]{1,0:T(8,128)} %bitcast.15), custom_call_target="tpu_custom_call" | custom-call | flops 1000000000 | bytes 1769472 | tf_op jit(solution)/shard_map/start/pallas_call | solution.py:331
  3.6 7.4 %all-to-all-start = ((f32[16,80,128]{2,1,0:T(8,128)}), f32[16,80,128]{2,1,0:T(8,128)S(1)}, u32[]{:S(2)}, u32[]{:S(2)}) async-start(f32[16,80,128]{2,1,0:T(8,128)} %get-tuple-element.8), calls=%async_computation | async-start | bytes 1310720 | tf_op jit(solution)/shard_map/all_to_all | solution.py:352
  11.0 2.8 %copy.6 = bf16[1024,1152]{0,1:T(8,128)(2,1)S(1)} copy(bf16[1024,1152]{1,0:T(8,128)(2,1)} %param.8) | data formatting | bytes 4718592 | tf_op args[3]
  13.9 4.4 %copy.7 = bf16[1152,1024]{0,1:T(8,128)(2,1)} copy(bf16[1152,1024]{1,0:T(8,128)(2,1)} %param.9) | data formatting | bytes 4718592 | tf_op args[4]
  18.2 9.4 %all-to-all-done.blocks_ref = f32[16,80,128]{2,1,0:T(8,128)S(1)} async-done(((f32[16,80,128]{2,1,0:T(8,128)}), f32[16,80,128]{2,1,0:T(8,128)S(1)}, u32[]{:S(2)}, u32[]{:S(2)}) %all-to-all-start) | async-done | bytes 655392 | tf_op jit(solution)/shard_map/all_to_all | solution.py:352
  27.6 0.0 copy-start
  27.6 1.7 %copy-done = bf16[1152,1024]{0,1:T(8,128)(2,1)S(1)} copy-done((bf16[1152,1024]{0,1:T(8,128)(2,1)S(1)}, bf16[1152,1024]{0,1:T(8,128)(2,1)}, u32[]{:S(2)}) %copy-start) | copy-done | bytes 2359320
  29.3 2.5 %middle.1 = f32[1152,128]{1,0:T(8,128)S(1)} custom-call(f32[16,80,128]{2,1,0:T(8,128)S(1)} %all-to-all-done.blocks_ref, f32[9,128]{1,0:T(8,128)S(1)} %get-tuple-element.9.courant_ref, f32[16,128]{1,0:T(8,128)S(1)} %get-tuple-element.10.faces_ref, bf16[1152,1024]{1,0:T(8,128)(2,1)S(1)} %bitcast.11, bf16[1024,1152]{1,0:T(8,128)(2,1)S(1)} %bitcast.12), custom_call_target="tpu_custom_call" | custom-call | tf_op jit(solution)/shard_map/middle/pallas_call | solution.py:353
  31.8 21.9 %all_to_all.24 = f32[16,72,128]{2,1,0:T(8,128)S(1)} all-to-all(f32[16,72,128]{2,1,0:T(8,128)S(1)} %bitcast.13), channel_id=1, replica_groups=mesh['member'=2,'cell'=16] {'cell'}, dimensions={0} | all-to-all | bytes 1179648 | tf_op jit(solution)/shard_map/all_to_all | solution.py:365
  53.6 0.9 %copy_bitcast_fusion = f32[72,2048]{1,0:T(8,128)} fusion(f32[16,72,128]{2,1,0:T(8,128)S(1)} %all_to_all.24), kind=kLoop, calls=%fused_computation | loop fusion | bytes 1179648 | tf_op jit(solution)/shard_map/all_to_all | solution.py:365
Async XLA Ops:
  3.6 24.0 %all-to-all-start = ((f32[16,80,128]{2,1,0:T(8,128)}), f32[16,80,128]{2,1,0:T(8,128)S(1)}, u32[]{:S(2)}, u32[]{:S(2)}) async-start(f32[16,80,128]{2,1,0:T(8,128)} %get-tuple-element.8), calls=%async_computation | async-start | bytes 1310720 | tf_op jit(solution)/shard_map/all_to_all | solution.py:352
  27.6 1.7 %copy-start = (bf16[1152,1024]{0,1:T(8,128)(2,1)S(1)}, bf16[1152,1024]{0,1:T(8,128)(2,1)}, u32[]{:S(2)}) copy-start(bf16[1152,1024]{0,1:T(8,128)(2,1)} %copy.7) | copy-start | bytes 7077892

commit v13 on v12

--- a/solution.py
+++ b/solution.py
@@ -1,3 +1,5 @@
+import functools
+
 import jax
 import jax.numpy as jnp
 from jax import lax
@@ -234,6 +236,22 @@
     return [u - (f - g) for u, f, g in zip(state, fluxes, preceding(fluxes))]
 
 
+def turn_kernel(lift_hbm, back_hbm, lift_out_ref, back_out_ref, lift_ref, back_ref, sems):
+    jobs = []
+    for which, (source, held, target) in enumerate(
+        ((lift_hbm, lift_ref, lift_out_ref), (back_hbm, back_ref, back_out_ref))
+    ):
+        for step in range(source.shape[0] // LANES):
+            rows = pl.ds(step * LANES, LANES)
+            copy = pltpu.make_async_copy(source.at[rows, :], held.at[rows, :], sems.at[which, step])
+            jobs.append((copy, held, target, step * LANES))
+    for copy, *_ in jobs:
+        copy.start()
+    for copy, held, target, at in jobs:
+        copy.wait()
+        target[:, at : at + LANES] = jnp.transpose(held[at : at + LANES, :])
+
+
 def dot(values, weights):
     return jnp.dot(values, weights, preferred_element_type=jnp.float32)
 
@@ -327,11 +345,12 @@
     f32 = jnp.float32
     any_space = pl.BlockSpec(memory_space=pl.ANY)
     vmem = pl.BlockSpec(memory_space=pltpu.VMEM)
+    in_hbm = functools.partial(pltpu.with_memory_space_constraint, memory_space=pltpu.HBM)
     inputs = (wave_energy, courant, sea_mask)
     start, courant, faces = pl.pallas_call(
         start_kernel,
         out_shape=[
-            jax.ShapeDtypeStruct((tiles, groups + ROWS, LANES), f32),
+            pltpu.VMEM((tiles, groups + ROWS, LANES), f32),
             jax.ShapeDtypeStruct(courant.shape, f32),
             jax.ShapeDtypeStruct((tiles, LANES), f32),
         ],
@@ -348,7 +367,25 @@
         compiler_params=pltpu.CompilerParams(vmem_limit_bytes=16 << 20),
         cost_estimate=pl.CostEstimate(flops=1000000000, bytes_accessed=3 * 4 * groups * cells, transcendentals=0),
         name="start",
-    )(*(pltpu.with_memory_space_constraint(x, pltpu.HBM) for x in inputs))
+    )(*map(in_hbm, inputs))
+    modes = lift_weight.shape[0]
+    bf16 = jnp.bfloat16
+    lift_turned, back_turned = pl.pallas_call(
+        turn_kernel,
+        out_shape=[pltpu.VMEM((components, modes), bf16), pltpu.VMEM((modes, components), bf16)],
+        in_specs=[any_space] * 2,
+        out_specs=[vmem] * 2,
+        scratch_shapes=[
+            pltpu.VMEM((modes, components), bf16),
+            pltpu.VMEM((components, modes), bf16),
+            pltpu.SemaphoreType.DMA((2, max(modes, components) // LANES)),
+        ],
+        compiler_params=pltpu.CompilerParams(vmem_limit_bytes=16 << 20),
+        cost_estimate=pl.CostEstimate(
+            flops=0, bytes_accessed=8 * modes * components, transcendentals=0
+        ),
+        name="turn",
+    )(in_hbm(lift_weight), in_hbm(back_weight))
     state = lax.all_to_all(start, "cell", split_axis=0, concat_axis=0, tiled=True)
     final = pl.pallas_call(
         middle_kernel,
@@ -361,7 +398,7 @@
         ],
         compiler_params=pltpu.CompilerParams(vmem_limit_bytes=24 << 20),
         name="middle",
-    )(state, courant, faces, lift_weight.T, back_weight.T)
+    )(state, courant, faces, lift_turned, back_turned)
     return lax.all_to_all(final, "cell", split_axis=0, concat_axis=1, tiled=True)
 
 
@@ -369,7 +406,7 @@
     devices = lax.axis_size("cell")
     groups, cells = wave_energy.shape
     whole = cells == devices * LANES and groups % ROWS == 0 and groups <= LANES
-    whole = whole and courant.shape[0] % LANES == 0 and courant.shape[0] <= LANES * LANES // ROWS
+    whole = whole and courant.shape[0] % LANES == 0 and lift_weight.shape[0] % LANES == 0 and courant.shape[0] <= LANES * LANES // ROWS
     run = tiled_shards if whole else general_shards
     return run(wave_energy, courant, sea_mask, lift_weight, back_weight)
 

time: 54.9 us -> 54.8 us (level)
  local copies, waits for them, and re-layouts: 9.74 us -> 3.93 us
  Pallas kernels: 6.14 us -> 9.59 us
  waiting for transfers between devices: 9.38 us -> 11.7 us
    unnamed x4, local copies, waits for them, and re-layouts: 8.88 us -> 3.07 us
    pallas_call x1 -> x2, Pallas kernels: 3.63 us -> 7.08 us  [the longest x1 3.63 us: tiled_shards(): pl.pallas_call(start_kernel, out_shape=[pltpu.VMEM((tiles, groups + ROWS,...]
    all_to_all x1, waiting for transfers between devices: 9.38 us -> 11.7 us  [tiled_shards(): lax.all_to_all(start, 'cell', split_axis=0, concat_axis=0, tiled=True)]
  transfers between devices with their start and end apart: 1 -> 1, of which waited for: 1 -> 1; matrix products, arithmetic and copies ran while one was open for 13% -> 0% of each run, Pallas kernels for 0% -> 6%
where the time goes in v13:
time: 54.8 us; the launch traced here: 54.5 us
  blocking collectives  21.9 us (40%)
  waiting for transfers between devices  11.7 us (21%)
  Pallas kernels  9.59 us (18%)
  starting transfers between devices  7.37 us (13%)
  local copies, waits for them, and re-layouts  3.93 us (7%)
    all_to_all x1, blocking collectives, tiled_shards(): lax.all_to_all(final, 'cell', split_axis=0, concat_axis=1, tiled=True)  21.9 us
    all_to_all x1, waiting for transfers between devices, tiled_shards(): lax.all_to_all(start, 'cell', split_axis=0, concat_axis=0, tiled=True)  11.7 us
    all_to_all x1, starting transfers between devices, tiled_shards(): lax.all_to_all(start, 'cell', split_axis=0, concat_axis=0, tiled=True)  7.37 us
    pallas_call x1, Pallas kernels, tiled_shards(): pl.pallas_call(start_kernel, out_shape=[pltpu.VMEM((tiles, groups + ROWS,...  3.63 us
    pallas_call x1, Pallas kernels, tiled_shards(): pl.pallas_call(turn_kernel, out_shape=[pltpu.VMEM((components, modes), bf...  3.45 us
    unnamed x4, local copies, waits for them, and re-layouts  3.07 us
    pallas_call x1, Pallas kernels, tiled_shards(): pl.pallas_call(middle_kernel, out_shape=jax.ShapeDtypeStruct((components,...  2.51 us
  transfers between devices with their start and end apart: 1, of which 1 were waited for; matrix products, arithmetic and copies ran while one was open for 0% of the time, Pallas kernels for 6%

profile of v13, /device:TPU:0, one launch (start us, length us, event | category | flops | bytes accessed | tf_op | source)
XLA Modules:
  0.0 54.5 jit_solution(6307874098253244070)
XLA Ops:
  0.0 3.6 %start.1 = (f32[16,80,128]{2,1,0:T(8,128)}, f32[9,128]{1,0:T(8,128)S(1)}, f32[16,128]{1,0:T(8,128)S(1)}) custom-call(f32[72,2048]{1,0:T(8,128)} %energy_hbm.1, f32[9,128]{1,0:T(8,128)} %bitcast.10, s32[16,128]{1,0:T(8,128)} %bitcast.11), custom_call_target="tpu_custom_call" | custom-call | flops 1000000000 | bytes 1769472 | tf_op jit(solution)/shard_map/start/pallas_call | solution.py:350
  3.6 7.4 %all-to-all-start = ((f32[16,80,128]{2,1,0:T(8,128)}), f32[16,80,128]{2,1,0:T(8,128)S(1)}, u32[]{:S(2)}, u32[]{:S(2)}) async-start(f32[16,80,128]{2,1,0:T(8,128)} %get-tuple-element.10), calls=%async_computation | async-start | bytes 1310720 | tf_op jit(solution)/shard_map/all_to_all | solution.py:389
  11.0 3.4 %turn.1 = (bf16[1152,1024]{1,0:T(8,128)(2,1)S(1)}, bf16[1024,1152]{1,0:T(8,128)(2,1)S(1)}) custom-call(bf16[1024,1152]{1,0:T(8,128)(2,1)} %lift_hbm.1, bf16[1152,1024]{1,0:T(8,128)(2,1)} %back_hbm.1), custom_call_target="tpu_custom_call" | custom-call | bytes 9437184 | tf_op jit(solution)/shard_map/turn/pallas_call | solution.py:373
  14.5 0.0 copy-start
  14.5 1.4 %copy-done = bf16[1024,1152]{1,0:T(8,128)(2,1)} copy-done((bf16[1024,1152]{1,0:T(8,128)(2,1)}, bf16[1024,1152]{1,0:T(8,128)(2,1)S(1)}, u32[]{:S(2)}) %copy-start) | copy-done | bytes 2359320
  15.9 11.7 %all-to-all-done.blocks_ref = f32[16,80,128]{2,1,0:T(8,128)S(1)} async-done(((f32[16,80,128]{2,1,0:T(8,128)}), f32[16,80,128]{2,1,0:T(8,128)S(1)}, u32[]{:S(2)}, u32[]{:S(2)}) %all-to-all-start) | async-done | bytes 655392 | tf_op jit(solution)/shard_map/all_to_all | solution.py:389
  27.6 0.0 copy-start.1
  27.6 1.7 %copy-done.1 = bf16[1024,1152]{1,0:T(8,128)(2,1)S(1)} copy-done((bf16[1024,1152]{1,0:T(8,128)(2,1)S(1)}, bf16[1024,1152]{1,0:T(8,128)(2,1)}, u32[]{:S(2)}) %copy-start.1) | copy-done | bytes 2359320
  29.3 2.5 %middle.1 = f32[1152,128]{1,0:T(8,128)S(1)} custom-call(f32[16,80,128]{2,1,0:T(8,128)S(1)} %all-to-all-done.blocks_ref, f32[9,128]{1,0:T(8,128)S(1)} %get-tuple-element.11.courant_ref, f32[16,128]{1,0:T(8,128)S(1)} %get-tuple-element.12.faces_ref, bf16[1152,1024]{1,0:T(8,128)(2,1)S(1)} %get-tuple-element.13.lift_ref, bf16[1024,1152]{1,0:T(8,128)(2,1)S(1)} %copy-done.1), custom_call_target="tpu_custom_call" | custom-call | tf_op jit(solution)/shard_map/middle/pallas_call | solution.py:390
  31.8 21.9 %all_to_all.24 = f32[16,72,128]{2,1,0:T(8,128)S(1)} all-to-all(f32[16,72,128]{2,1,0:T(8,128)S(1)} %bitcast.9), channel_id=1, replica_groups=mesh['member'=2,'cell'=16] {'cell'}, dimensions={0} | all-to-all | bytes 1179648 | tf_op jit(solution)/shard_map/all_to_all | solution.py:402
  53.7 0.9 %copy_bitcast_fusion = f32[72,2048]{1,0:T(8,128)} fusion(f32[16,72,128]{2,1,0:T(8,128)S(1)} %all_to_all.24), kind=kLoop, calls=%fused_computation | loop fusion | bytes 1179648 | tf_op jit(solution)/shard_map/all_to_all | solution.py:402
Async XLA Ops:
  3.6 24.0 %all-to-all-start = ((f32[16,80,128]{2,1,0:T(8,128)}), f32[16,80,128]{2,1,0:T(8,128)S(1)}, u32[]{:S(2)}, u32[]{:S(2)}) async-start(f32[16,80,128]{2,1,0:T(8,128)} %get-tuple-element.10), calls=%async_computation | async-start | bytes 1310720 | tf_op jit(solution)/shard_map/all_to_all | solution.py:389
  14.5 1.4 %copy-start = (bf16[1024,1152]{1,0:T(8,128)(2,1)}, bf16[1024,1152]{1,0:T(8,128)(2,1)S(1)}, u32[]{:S(2)}) copy-start(bf16[1024,1152]{1,0:T(8,128)(2,1)S(1)} %get-tuple-element.14.back_ref) | copy-start | bytes 7077892
  27.6 1.7 %copy-start.1 = (bf16[1024,1152]{1,0:T(8,128)(2,1)S(1)}, bf16[1024,1152]{1,0:T(8,128)(2,1)}, u32[]{:S(2)}) copy-start(bf16[1024,1152]{1,0:T(8,128)(2,1)} %copy-done) | copy-start | bytes 7077892

commit v14 on v10

--- a/solution.py
+++ b/solution.py
@@ -241,7 +241,8 @@
 
 
 def middle_kernel(
-    blocks_ref, courant_ref, faces_ref, lift_ref, back_ref, out_ref, ring_ref, opens_ref, half_ref, squared_ref
+    blocks_ref, courant_ref, faces_ref, lift_ref, back_ref, out_ref,
+    ring_ref, opens_ref, half_ref, squared_ref, last_ref, last_squared_ref,
 ):
     sources, rows, _ = blocks_ref.shape
     groups = rows - ROWS
@@ -307,17 +308,15 @@
                 state = ring_substep(state, opens, *terms)
             for rows, values in zip(strided, state):
                 ring_ref[block, rows, :] = values
-            half_ref[:LANES, part] = ring_ref[block, :LANES, :].astype(jnp.bfloat16)
-
-    lifted = dot_rows(half_ref[:LANES, :], lift_ref[...])
-    squared_ref[:LANES, :] = (lifted * lifted).astype(jnp.bfloat16)
-    for base in range(0, modes, chunk):
-        wide = slice(base, min(base + chunk, modes))
-        source = coupling * dot_rows(squared_ref[:LANES, :], back_ref[wide, :])
-        for block in range(wide.start // LANES, wide.stop // LANES):
-            at = block * LANES - base
-            state = ring_ref[block, :LANES, :] + source[:, at : at + LANES]
-            out_ref[block * LANES : (block + 1) * LANES, :] = jnp.transpose(state)
+            advanced = jnp.transpose(ring_ref[block, :LANES, :])
+            out_ref[part, :] = advanced
+            last_ref[part, :] = advanced.astype(jnp.bfloat16)
+
+    lifted = jnp.dot(lift_ref[...], last_ref[...], preferred_element_type=jnp.float32)
+    last_squared_ref[...] = (lifted * lifted).astype(jnp.bfloat16)
+    out_ref[...] += coupling * jnp.dot(
+        back_ref[...], last_squared_ref[...], preferred_element_type=jnp.float32
+    )
 
 
 def tiled_shards(wave_energy, courant, sea_mask, lift_weight, back_weight):
@@ -360,6 +359,8 @@
             pltpu.VMEM((LANES + ROWS, LANES), f32),
             pltpu.VMEM((LANES + 2 * ROWS, components), jnp.bfloat16),
             pltpu.VMEM((LANES + 2 * ROWS, lift_weight.shape[0]), jnp.bfloat16),
+            pltpu.VMEM((components, LANES), jnp.bfloat16),
+            pltpu.VMEM((lift_weight.shape[0], LANES), jnp.bfloat16),
         ],
         compiler_params=pltpu.CompilerParams(vmem_limit_bytes=24 << 20),
         name="middle",

time: 53.4 us -> 54 us (1.011)
  Pallas kernels: 6.59 us -> 7.15 us
    pallas_call x1, Pallas kernels: 3.65 us -> 4.21 us  [tiled_shards(): pl.pallas_call(middle_kernel, out_shape=jax.ShapeDtypeStruct((components,...]
where the time goes in v14:
time: 54 us; the launch traced here: 53.8 us
  blocking collectives  45.7 us (85%)
  Pallas kernels  7.15 us (13%)
  local copies, waits for them, and re-layouts  0.87 us (2%)
    all_to_all x1, blocking collectives, tiled_shards(): lax.all_to_all(start, 'cell', split_axis=0, concat_axis=0, tiled=True)  25.4 us
    all_to_all x1, blocking collectives, tiled_shards(): lax.all_to_all(final, 'cell', split_axis=0, concat_axis=1, tiled=True)  20.3 us
    pallas_call x1, Pallas kernels, tiled_shards(): pl.pallas_call(middle_kernel, out_shape=jax.ShapeDtypeStruct((components,...  4.21 us
    pallas_call x1, Pallas kernels, tiled_shards(): pl.pallas_call(start_kernel, out_shape=[jax.ShapeDtypeStruct((tiles, grou...  2.94 us

profile of v14, /device:TPU:0, one launch (start us, length us, event | category | flops | bytes accessed | tf_op | source)
XLA Modules:
  0.0 53.8 jit_solution(4647895308310970488)
XLA Ops:
  0.0 0.0 copy-start
  0.0 0.0 copy-start.1
  0.0 2.9 %start.1 = (f32[16,80,128]{2,1,0:T(8,128)S(1)}, f32[9,128]{1,0:T(8,128)S(1)}, f32[16,128]{1,0:T(8,128)S(1)}) custom-call(f32[72,2048]{1,0:T(8,128)} %energy_hbm.1, f32[9,128]{1,0:T(8,128)} %bitcast.10, s32[16,128]{1,0:T(8,128)} %bitcast.11), custom_call_target="tpu_custom_call" | custom-call | flops 1000000000 | bytes 1769472 | tf_op jit(solution)/shard_map/start/pallas_call | solution.py:332
  2.9 25.4 %all_to_all.24.blocks_ref = f32[16,80,128]{2,1,0:T(8,128)S(1)} all-to-all(f32[16,80,128]{2,1,0:T(8,128)S(1)} %get-tuple-element.8), channel_id=1, replica_groups=mesh['member'=2,'cell'=16] {'cell'}, dimensions={0} | all-to-all | bytes 1310720 | tf_op jit(solution)/shard_map/all_to_all | solution.py:353
  28.3 0.0 copy-done
  28.3 0.0 copy-done.1
  28.3 4.2 %middle.1 = f32[1152,128]{1,0:T(8,128)S(1)} custom-call(f32[16,80,128]{2,1,0:T(8,128)S(1)} %all_to_all.24.blocks_ref, f32[9,128]{1,0:T(8,128)S(1)} %get-tuple-element.9.courant_ref, f32[16,128]{1,0:T(8,128)S(1)} %get-tuple-element.10.faces_ref, bf16[1024,1152]{1,0:T(8,128)(2,1)S(1)} %copy-done, bf16[1152,1024]{1,0:T(8,128)(2,1)S(1)} %copy-done.1), custom_call_target="tpu_custom_call" | custom-call | tf_op jit(solution)/shard_map/middle/pallas_call | solution.py:354
  32.6 20.3 %all_to_all.25 = f32[16,72,128]{2,1,0:T(8,128)S(1)} all-to-all(f32[16,72,128]{2,1,0:T(8,128)S(1)} %bitcast.9), channel_id=1, replica_groups=mesh['member'=2,'cell'=16] {'cell'}, dimensions={0} | all-to-all | bytes 1179648 | tf_op jit(solution)/shard_map/all_to_all | solution.py:368
  52.9 0.9 %copy_bitcast_fusion = f32[72,2048]{1,0:T(8,128)} fusion(f32[16,72,128]{2,1,0:T(8,128)S(1)} %all_to_all.25), kind=kLoop, calls=%fused_computation | loop fusion | bytes 1179648 | tf_op jit(solution)/shard_map/all_to_all | solution.py:368
Async XLA Ops:
  0.0 28.3 %copy-start = (bf16[1024,1152]{1,0:T(8,128)(2,1)S(1)}, bf16[1024,1152]{1,0:T(8,128)(2,1)}, u32[]{:S(2)}) copy-start(bf16[1024,1152]{1,0:T(8,128)(2,1)} %lift_ref.1) | copy-start | bytes 7077892
  0.0 28.3 %copy-start.1 = (bf16[1152,1024]{1,0:T(8,128)(2,1)S(1)}, bf16[1152,1024]{1,0:T(8,128)(2,1)}, u32[]{:S(2)}) copy-start(bf16[1152,1024]{1,0:T(8,128)(2,1)} %back_ref.1) | copy-start | bytes 7077892

commit v15 on v10

--- a/solution.py
+++ b/solution.py
@@ -128,16 +128,14 @@
     return speed, 0.5 * size * (1.0 - size), speed >= 0.0
 
 
-def spread_speeds(courant_ref, speeds_ref):
-    parts = courant_ref.shape[0]
-    square = jnp.concatenate(
-        [courant_ref[...], jnp.zeros((LANES - parts, LANES), jnp.float32)], axis=0
-    )
-    turned = jnp.transpose(square)
-    for part in range(parts):
-        speeds_ref[pl.ds(part * LANES, LANES), :] = jnp.broadcast_to(
-            turned[:, part : part + 1], (LANES, LANES)
-        )
+def own_speeds(courant_ref, first):
+    part, at = first // LANES, first % LANES
+    this = courant_ref[pl.ds(part, 1), :]
+    following = courant_ref[pl.ds(jnp.minimum(part + 1, courant_ref.shape[0] - 1), 1), :]
+    back = (LANES - at) % LANES
+    this, following = pltpu.roll(this, back, 1), pltpu.roll(following, back, 1)
+    row = jnp.where(lane_index((1, LANES)) < LANES - at, this, following)
+    return jnp.transpose(jnp.broadcast_to(row, (LANES, LANES)))
 
 
 def face_rows(sea):
@@ -168,7 +166,7 @@
 
 def start_kernel(
     energy_hbm, courant_hbm, sea_hbm, out_ref, courant_ref, faces_ref,
-    energy_ref, sea_ref, speeds_ref, edges_ref, sems, energy_sems,
+    energy_ref, sea_ref, edges_ref, sems, energy_sems,
 ):
     groups = energy_ref.shape[0]
     tiles = out_ref.shape[0]
@@ -178,24 +176,23 @@
     sea = pltpu.make_async_copy(sea_hbm, sea_ref, sems.at[1])
     state_copies = [
         pltpu.make_async_copy(
-            energy_hbm.at[pl.ds(base, size), :], energy_ref.at[pl.ds(base, size), :], energy_sems.at[step]
+            energy_hbm.at[pl.ds(step * ROWS, ROWS), :], energy_ref.at[pl.ds(step * ROWS, ROWS), :], energy_sems.at[step]
         )
-        for step, (base, size) in enumerate(zip(bases, sizes))
-    ]
+        for step in range(groups // ROWS)
+    ]
+    for copy in state_copies:
+        copy.start()
     small.start()
     sea.start()
-    for copy in state_copies:
-        copy.start()
     edges_ref[...] = jnp.zeros((LANES, LANES), jnp.float32)
     small.wait()
-    spread_speeds(courant_ref, speeds_ref)
+    speeds = own_speeds(courant_ref, lax.axis_index("cell") * groups)
     sea.wait()
     faces_ref[...] = face_rows(sea_ref[...].astype(jnp.float32))
-    rank = lax.axis_index("cell")
-    for copy, base, size in zip(state_copies, bases, sizes):
-        copy.wait()
-        own = pl.multiple_of(rank * groups + base, ROWS)
-        speed = speeds_ref[pl.ds(own, size), :]
+    for base, size in zip(bases, sizes):
+        for copy in state_copies[base // ROWS : (base + size) // ROWS]:
+            copy.wait()
+        speed = speeds[base : base + size]
         state = [
             energy_ref[base : base + size, tile * LANES : (tile + 1) * LANES] for tile in range(tiles)
         ]
@@ -342,10 +339,9 @@
         scratch_shapes=[
             pltpu.VMEM((groups, cells), f32),
             pltpu.VMEM(sea_mask.shape, sea_mask.dtype),
-            pltpu.VMEM((components, LANES), f32),
             pltpu.VMEM((LANES, LANES), f32),
             pltpu.SemaphoreType.DMA((2,)),
-            pltpu.SemaphoreType.DMA((-(-groups // START_ROWS),)),
+            pltpu.SemaphoreType.DMA((groups // ROWS,)),
         ],
         compiler_params=pltpu.CompilerParams(vmem_limit_bytes=16 << 20),
         cost_estimate=pl.CostEstimate(flops=1000000000, bytes_accessed=3 * 4 * groups * cells, transcendentals=0),

time: 53.4 us -> 53.6 us (level)
  no operation moved by 1% of the time
where the time goes in v15:
time: 53.6 us; the launch traced here: 53.4 us
  blocking collectives  45.7 us (85%)
  Pallas kernels  6.73 us (13%)
  local copies, waits for them, and re-layouts  0.87 us (2%)
    all_to_all x1, blocking collectives, tiled_shards(): lax.all_to_all(start, 'cell', split_axis=0, concat_axis=0, tiled=True)  25.4 us
    all_to_all x1, blocking collectives, tiled_shards(): lax.all_to_all(final, 'cell', split_axis=0, concat_axis=1, tiled=True)  20.3 us
    pallas_call x1, Pallas kernels, tiled_shards(): pl.pallas_call(middle_kernel, out_shape=jax.ShapeDtypeStruct((components,...  3.66 us
    pallas_call x1, Pallas kernels, tiled_shards(): pl.pallas_call(start_kernel, out_shape=[jax.ShapeDtypeStruct((tiles, grou...  3.07 us

profile of v15, /device:TPU:0, one launch (start us, length us, event | category | flops | bytes accessed | tf_op | source)
XLA Modules:
  0.0 53.4 jit_solution(15080255531772456929)
XLA Ops:
  0.0 0.0 copy-start
  0.0 0.0 copy-start.1
  0.0 3.1 %start.1 = (f32[16,80,128]{2,1,0:T(8,128)S(1)}, f32[9,128]{1,0:T(8,128)S(1)}, f32[16,128]{1,0:T(8,128)S(1)}) custom-call(f32[72,2048]{1,0:T(8,128)} %energy_hbm.1, f32[9,128]{1,0:T(8,128)} %bitcast.10, s32[16,128]{1,0:T(8,128)} %bitcast.11), custom_call_target="tpu_custom_call" | custom-call | flops 1000000000 | bytes 1769472 | tf_op jit(solution)/shard_map/start/pallas_call | solution.py:330
  3.1 25.4 %all_to_all.24.blocks_ref = f32[16,80,128]{2,1,0:T(8,128)S(1)} all-to-all(f32[16,80,128]{2,1,0:T(8,128)S(1)} %get-tuple-element.8), channel_id=1, replica_groups=mesh['member'=2,'cell'=16] {'cell'}, dimensions={0} | all-to-all | bytes 1310720 | tf_op jit(solution)/shard_map/all_to_all | solution.py:350
  28.5 0.0 copy-done
  28.5 0.0 copy-done.1
  28.5 3.7 %middle.1 = f32[1152,128]{1,0:T(8,128)S(1)} custom-call(f32[16,80,128]{2,1,0:T(8,128)S(1)} %all_to_all.24.blocks_ref, f32[9,128]{1,0:T(8,128)S(1)} %get-tuple-element.9.courant_ref, f32[16,128]{1,0:T(8,128)S(1)} %get-tuple-element.10.faces_ref, bf16[1024,1152]{1,0:T(8,128)(2,1)S(1)} %copy-done, bf16[1152,1024]{1,0:T(8,128)(2,1)S(1)} %copy-done.1), custom_call_target="tpu_custom_call" | custom-call | tf_op jit(solution)/shard_map/middle/pallas_call | solution.py:351
  32.1 20.3 %all_to_all.25 = f32[16,72,128]{2,1,0:T(8,128)S(1)} all-to-all(f32[16,72,128]{2,1,0:T(8,128)S(1)} %bitcast.9), channel_id=1, replica_groups=mesh['member'=2,'cell'=16] {'cell'}, dimensions={0} | all-to-all | bytes 1179648 | tf_op jit(solution)/shard_map/all_to_all | solution.py:363
  52.5 0.9 %copy_bitcast_fusion = f32[72,2048]{1,0:T(8,128)} fusion(f32[16,72,128]{2,1,0:T(8,128)S(1)} %all_to_all.25), kind=kLoop, calls=%fused_computation | loop fusion | bytes 1179648 | tf_op jit(solution)/shard_map/all_to_all | solution.py:363
Async XLA Ops:
  0.0 28.5 %copy-start = (bf16[1024,1152]{1,0:T(8,128)(2,1)S(1)}, bf16[1024,1152]{1,0:T(8,128)(2,1)}, u32[]{:S(2)}) copy-start(bf16[1024,1152]{1,0:T(8,128)(2,1)} %lift_ref.1) | copy-start | bytes 7077892
  0.0 28.5 %copy-start.1 = (bf16[1152,1024]{1,0:T(8,128)(2,1)S(1)}, bf16[1152,1024]{1,0:T(8,128)(2,1)}, u32[]{:S(2)}) copy-start(bf16[1152,1024]{1,0:T(8,128)(2,1)} %back_ref.1) | copy-start | bytes 7077892

commit v16 on v10

--- a/solution.py
+++ b/solution.py
@@ -273,8 +273,12 @@
         beside = jnp.concatenate([halos[block], jnp.zeros((padded - ring, LANES), jnp.float32)], axis=0)
         half_ref[LANES:, part] = beside.astype(jnp.bfloat16)
 
-    lifted = dot_rows(half_ref[...], lift_ref[...])
-    squared_ref[...] = (lifted * lifted).astype(jnp.bfloat16)
+    chunk = 2 * LANES
+    width = lift_ref.shape[0]
+    lifts = [slice(base, min(base + chunk, width)) for base in range(0, width, chunk)]
+    for wide in lifts:
+        lifted = dot_rows(half_ref[...], lift_ref[wide, :])
+        squared_ref[:, wide] = (lifted * lifted).astype(jnp.bfloat16)
 
     own_faces = faces_ref[pl.ds(rank, 1), :]
     after_faces = faces_ref[pl.ds(jnp.minimum(rank + 1, tiles - 1), 1), :]
@@ -293,7 +297,6 @@
     strided = [pl.ds(at, ROWS, stride=stride) for at in range(stride)]
     opens = [opens_ref[rows, :] for rows in strided]
 
-    chunk = 2 * LANES
     for base in range(0, modes, chunk):
         wide = slice(base, min(base + chunk, modes))
         source = dot_rows(squared_ref[...], back_ref[wide, :])
@@ -309,8 +312,9 @@
                 ring_ref[block, rows, :] = values
             half_ref[:LANES, part] = ring_ref[block, :LANES, :].astype(jnp.bfloat16)
 
-    lifted = dot_rows(half_ref[:LANES, :], lift_ref[...])
-    squared_ref[:LANES, :] = (lifted * lifted).astype(jnp.bfloat16)
+    for wide in lifts:
+        lifted = dot_rows(half_ref[:LANES, :], lift_ref[wide, :])
+        squared_ref[:LANES, wide] = (lifted * lifted).astype(jnp.bfloat16)
     for base in range(0, modes, chunk):
         wide = slice(base, min(base + chunk, modes))
         source = coupling * dot_rows(squared_ref[:LANES, :], back_ref[wide, :])

time: 53.4 us -> 53.4 us (level)
  no operation moved by 1% of the time
where the time goes in v16:
time: 53.4 us; the launch traced here: 53.2 us
  blocking collectives  45.7 us (86%)
  Pallas kernels  6.59 us (12%)
  local copies, waits for them, and re-layouts  0.87 us (2%)
    all_to_all x1, blocking collectives, tiled_shards(): lax.all_to_all(start, 'cell', split_axis=0, concat_axis=0, tiled=True)  25.4 us
    all_to_all x1, blocking collectives, tiled_shards(): lax.all_to_all(final, 'cell', split_axis=0, concat_axis=1, tiled=True)  20.3 us
    pallas_call x1, Pallas kernels, tiled_shards(): pl.pallas_call(middle_kernel, out_shape=jax.ShapeDtypeStruct((components,...  3.65 us
    pallas_call x1, Pallas kernels, tiled_shards(): pl.pallas_call(start_kernel, out_shape=[jax.ShapeDtypeStruct((tiles, grou...  2.94 us

profile of v16, /device:TPU:0, one launch (start us, length us, event | category | flops | bytes accessed | tf_op | source)
XLA Modules:
  0.0 53.2 jit_solution(10170950005167190444)
XLA Ops:
  0.0 0.0 copy-start
  0.0 0.0 copy-start.1
  0.0 2.9 %start.1 = (f32[16,80,128]{2,1,0:T(8,128)S(1)}, f32[9,128]{1,0:T(8,128)S(1)}, f32[16,128]{1,0:T(8,128)S(1)}) custom-call(f32[72,2048]{1,0:T(8,128)} %energy_hbm.1, f32[9,128]{1,0:T(8,128)} %bitcast.10, s32[16,128]{1,0:T(8,128)} %bitcast.11), custom_call_target="tpu_custom_call" | custom-call | flops 1000000000 | bytes 1769472 | tf_op jit(solution)/shard_map/start/pallas_call | solution.py:337
  2.9 25.4 %all_to_all.24.blocks_ref = f32[16,80,128]{2,1,0:T(8,128)S(1)} all-to-all(f32[16,80,128]{2,1,0:T(8,128)S(1)} %get-tuple-element.8), channel_id=1, replica_groups=mesh['member'=2,'cell'=16] {'cell'}, dimensions={0} | all-to-all | bytes 1310720 | tf_op jit(solution)/shard_map/all_to_all | solution.py:358
  28.3 0.0 copy-done
  28.3 0.0 copy-done.1
  28.3 3.7 %middle.1 = f32[1152,128]{1,0:T(8,128)S(1)} custom-call(f32[16,80,128]{2,1,0:T(8,128)S(1)} %all_to_all.24.blocks_ref, f32[9,128]{1,0:T(8,128)S(1)} %get-tuple-element.9.courant_ref, f32[16,128]{1,0:T(8,128)S(1)} %get-tuple-element.10.faces_ref, bf16[1024,1152]{1,0:T(8,128)(2,1)S(1)} %copy-done, bf16[1152,1024]{1,0:T(8,128)(2,1)S(1)} %copy-done.1), custom_call_target="tpu_custom_call" | custom-call | tf_op jit(solution)/shard_map/middle/pallas_call | solution.py:359
  32.0 20.3 %all_to_all.25 = f32[16,72,128]{2,1,0:T(8,128)S(1)} all-to-all(f32[16,72,128]{2,1,0:T(8,128)S(1)} %bitcast.9), channel_id=1, replica_groups=mesh['member'=2,'cell'=16] {'cell'}, dimensions={0} | all-to-all | bytes 1179648 | tf_op jit(solution)/shard_map/all_to_all | solution.py:371
  52.3 0.9 %copy_bitcast_fusion = f32[72,2048]{1,0:T(8,128)} fusion(f32[16,72,128]{2,1,0:T(8,128)S(1)} %all_to_all.25), kind=kLoop, calls=%fused_computation | loop fusion | bytes 1179648 | tf_op jit(solution)/shard_map/all_to_all | solution.py:371
Async XLA Ops:
  0.0 28.3 %copy-start = (bf16[1024,1152]{1,0:T(8,128)(2,1)S(1)}, bf16[1024,1152]{1,0:T(8,128)(2,1)}, u32[]{:S(2)}) copy-start(bf16[1024,1152]{1,0:T(8,128)(2,1)} %lift_ref.1) | copy-start | bytes 7077892
  0.0 28.3 %copy-start.1 = (bf16[1152,1024]{1,0:T(8,128)(2,1)S(1)}, bf16[1152,1024]{1,0:T(8,128)(2,1)}, u32[]{:S(2)}) copy-start(bf16[1152,1024]{1,0:T(8,128)(2,1)} %back_ref.1) | copy-start | bytes 7077892

commit v17 on v14

--- a/solution.py
+++ b/solution.py
@@ -274,8 +274,12 @@
         beside = jnp.concatenate([halos[block], jnp.zeros((padded - ring, LANES), jnp.float32)], axis=0)
         half_ref[LANES:, part] = beside.astype(jnp.bfloat16)
 
-    lifted = dot_rows(half_ref[...], lift_ref[...])
-    squared_ref[...] = (lifted * lifted).astype(jnp.bfloat16)
+    chunk = 2 * LANES
+    width = lift_ref.shape[0]
+    lifts = [slice(base, min(base + chunk, width)) for base in range(0, width, chunk)]
+    for wide in lifts:
+        lifted = dot_rows(half_ref[...], lift_ref[wide, :])
+        squared_ref[:, wide] = (lifted * lifted).astype(jnp.bfloat16)
 
     own_faces = faces_ref[pl.ds(rank, 1), :]
     after_faces = faces_ref[pl.ds(jnp.minimum(rank + 1, tiles - 1), 1), :]
@@ -294,7 +298,6 @@
     strided = [pl.ds(at, ROWS, stride=stride) for at in range(stride)]
     opens = [opens_ref[rows, :] for rows in strided]
 
-    chunk = 2 * LANES
     for base in range(0, modes, chunk):
         wide = slice(base, min(base + chunk, modes))
         source = dot_rows(squared_ref[...], back_ref[wide, :])
@@ -312,11 +315,14 @@
             out_ref[part, :] = advanced
             last_ref[part, :] = advanced.astype(jnp.bfloat16)
 
-    lifted = jnp.dot(lift_ref[...], last_ref[...], preferred_element_type=jnp.float32)
-    last_squared_ref[...] = (lifted * lifted).astype(jnp.bfloat16)
-    out_ref[...] += coupling * jnp.dot(
-        back_ref[...], last_squared_ref[...], preferred_element_type=jnp.float32
-    )
+    for rows in lifts:
+        lifted = jnp.dot(lift_ref[rows, :], last_ref[...], preferred_element_type=jnp.float32)
+        last_squared_ref[rows, :] = (lifted * lifted).astype(jnp.bfloat16)
+    for base in range(0, modes, chunk):
+        rows = slice(base, min(base + chunk, modes))
+        out_ref[rows, :] += coupling * jnp.dot(
+            back_ref[rows, :], last_squared_ref[...], preferred_element_type=jnp.float32
+        )
 
 
 def tiled_shards(wave_energy, courant, sea_mask, lift_weight, back_weight):

time: 54 us -> 53.5 us (level)
  no operation moved by 1% of the time
where the time goes in v17:
time: 53.5 us; the launch traced here: 53.3 us
  blocking collectives  45.7 us (85%)
  Pallas kernels  6.69 us (13%)
  local copies, waits for them, and re-layouts  0.87 us (2%)
    all_to_all x1, blocking collectives, tiled_shards(): lax.all_to_all(start, 'cell', split_axis=0, concat_axis=0, tiled=True)  25.4 us
    all_to_all x1, blocking collectives, tiled_shards(): lax.all_to_all(final, 'cell', split_axis=0, concat_axis=1, tiled=True)  20.4 us
    pallas_call x1, Pallas kernels, tiled_shards(): pl.pallas_call(middle_kernel, out_shape=jax.ShapeDtypeStruct((components,...  3.76 us
    pallas_call x1, Pallas kernels, tiled_shards(): pl.pallas_call(start_kernel, out_shape=[jax.ShapeDtypeStruct((tiles, grou...  2.94 us

profile of v17, /device:TPU:0, one launch (start us, length us, event | category | flops | bytes accessed | tf_op | source)
XLA Modules:
  0.0 53.3 jit_solution(9426623993654957198)
XLA Ops:
  0.0 0.0 copy-start
  0.0 0.0 copy-start.1
  0.0 2.9 %start.1 = (f32[16,80,128]{2,1,0:T(8,128)S(1)}, f32[9,128]{1,0:T(8,128)S(1)}, f32[16,128]{1,0:T(8,128)S(1)}) custom-call(f32[72,2048]{1,0:T(8,128)} %energy_hbm.1, f32[9,128]{1,0:T(8,128)} %bitcast.10, s32[16,128]{1,0:T(8,128)} %bitcast.11), custom_call_target="tpu_custom_call" | custom-call | flops 1000000000 | bytes 1769472 | tf_op jit(solution)/shard_map/start/pallas_call | solution.py:338
  2.9 25.4 %all_to_all.24.blocks_ref = f32[16,80,128]{2,1,0:T(8,128)S(1)} all-to-all(f32[16,80,128]{2,1,0:T(8,128)S(1)} %get-tuple-element.8), channel_id=1, replica_groups=mesh['member'=2,'cell'=16] {'cell'}, dimensions={0} | all-to-all | bytes 1310720 | tf_op jit(solution)/shard_map/all_to_all | solution.py:359
  28.3 0.0 copy-done
  28.3 0.0 copy-done.1
  28.3 3.8 %middle.1 = f32[1152,128]{1,0:T(8,128)S(1)} custom-call(f32[16,80,128]{2,1,0:T(8,128)S(1)} %all_to_all.24.blocks_ref, f32[9,128]{1,0:T(8,128)S(1)} %get-tuple-element.9.courant_ref, f32[16,128]{1,0:T(8,128)S(1)} %get-tuple-element.10.faces_ref, bf16[1024,1152]{1,0:T(8,128)(2,1)S(1)} %copy-done, bf16[1152,1024]{1,0:T(8,128)(2,1)S(1)} %copy-done.1), custom_call_target="tpu_custom_call" | custom-call | tf_op jit(solution)/shard_map/middle/pallas_call | solution.py:360
  32.1 20.4 %all_to_all.25 = f32[16,72,128]{2,1,0:T(8,128)S(1)} all-to-all(f32[16,72,128]{2,1,0:T(8,128)S(1)} %bitcast.9), channel_id=1, replica_groups=mesh['member'=2,'cell'=16] {'cell'}, dimensions={0} | all-to-all | bytes 1179648 | tf_op jit(solution)/shard_map/all_to_all | solution.py:374
  52.5 0.9 %copy_bitcast_fusion = f32[72,2048]{1,0:T(8,128)} fusion(f32[16,72,128]{2,1,0:T(8,128)S(1)} %all_to_all.25), kind=kLoop, calls=%fused_computation | loop fusion | bytes 1179648 | tf_op jit(solution)/shard_map/all_to_all | solution.py:374
Async XLA Ops:
  0.0 28.3 %copy-start = (bf16[1024,1152]{1,0:T(8,128)(2,1)S(1)}, bf16[1024,1152]{1,0:T(8,128)(2,1)}, u32[]{:S(2)}) copy-start(bf16[1024,1152]{1,0:T(8,128)(2,1)} %lift_ref.1) | copy-start | bytes 7077892
  0.0 28.3 %copy-start.1 = (bf16[1152,1024]{1,0:T(8,128)(2,1)S(1)}, bf16[1152,1024]{1,0:T(8,128)(2,1)}, u32[]{:S(2)}) copy-start(bf16[1152,1024]{1,0:T(8,128)(2,1)} %back_ref.1) | copy-start | bytes 7077892

commit v18 on v17

--- a/solution.py
+++ b/solution.py
@@ -238,6 +238,11 @@
     return lax.dot_general(
         values, weights, (((1,), (1,)), ((), ())), preferred_element_type=jnp.float32
     )
+
+
+def halves(length):
+    middle = length // 2 // (2 * ROWS) * (2 * ROWS)
+    return [slice(0, middle), slice(middle, length)]
 
 
 def middle_kernel(
@@ -315,11 +320,10 @@
             out_ref[part, :] = advanced
             last_ref[part, :] = advanced.astype(jnp.bfloat16)
 
-    for rows in lifts:
+    for rows in halves(width):
         lifted = jnp.dot(lift_ref[rows, :], last_ref[...], preferred_element_type=jnp.float32)
         last_squared_ref[rows, :] = (lifted * lifted).astype(jnp.bfloat16)
-    for base in range(0, modes, chunk):
-        rows = slice(base, min(base + chunk, modes))
+    for rows in halves(modes):
         out_ref[rows, :] += coupling * jnp.dot(
             back_ref[rows, :], last_squared_ref[...], preferred_element_type=jnp.float32
         )

time: 53.5 us -> 53.5 us (level)
  no operation moved by 1% of the time
where the time goes in v18:
time: 53.5 us; the launch traced here: 53.3 us
  blocking collectives  45.7 us (85%)
  Pallas kernels  6.67 us (12%)
  local copies, waits for them, and re-layouts  0.87 us (2%)
    all_to_all x1, blocking collectives, tiled_shards(): lax.all_to_all(start, 'cell', split_axis=0, concat_axis=0, tiled=True)  25.4 us
    all_to_all x1, blocking collectives, tiled_shards(): lax.all_to_all(final, 'cell', split_axis=0, concat_axis=1, tiled=True)  20.4 us
    pallas_call x1, Pallas kernels, tiled_shards(): pl.pallas_call(middle_kernel, out_shape=jax.ShapeDtypeStruct((components,...  3.74 us
    pallas_call x1, Pallas kernels, tiled_shards(): pl.pallas_call(start_kernel, out_shape=[jax.ShapeDtypeStruct((tiles, grou...  2.94 us

profile of v18, /device:TPU:0, one launch (start us, length us, event | category | flops | bytes accessed | tf_op | source)
XLA Modules:
  0.0 53.3 jit_solution(5614037344227652879)
XLA Ops:
  0.0 0.0 copy-start
  0.0 0.0 copy-start.1
  0.0 2.9 %start.1 = (f32[16,80,128]{2,1,0:T(8,128)S(1)}, f32[9,128]{1,0:T(8,128)S(1)}, f32[16,128]{1,0:T(8,128)S(1)}) custom-call(f32[72,2048]{1,0:T(8,128)} %energy_hbm.1, f32[9,128]{1,0:T(8,128)} %bitcast.10, s32[16,128]{1,0:T(8,128)} %bitcast.11), custom_call_target="tpu_custom_call" | custom-call | flops 1000000000 | bytes 1769472 | tf_op jit(solution)/shard_map/start/pallas_call | solution.py:342
  2.9 25.4 %all_to_all.24.blocks_ref = f32[16,80,128]{2,1,0:T(8,128)S(1)} all-to-all(f32[16,80,128]{2,1,0:T(8,128)S(1)} %get-tuple-element.8), channel_id=1, replica_groups=mesh['member'=2,'cell'=16] {'cell'}, dimensions={0} | all-to-all | bytes 1310720 | tf_op jit(solution)/shard_map/all_to_all | solution.py:363
  28.3 0.0 copy-done
  28.3 0.0 copy-done.1
  28.3 3.7 %middle.1 = f32[1152,128]{1,0:T(8,128)S(1)} custom-call(f32[16,80,128]{2,1,0:T(8,128)S(1)} %all_to_all.24.blocks_ref, f32[9,128]{1,0:T(8,128)S(1)} %get-tuple-element.9.courant_ref, f32[16,128]{1,0:T(8,128)S(1)} %get-tuple-element.10.faces_ref, bf16[1024,1152]{1,0:T(8,128)(2,1)S(1)} %copy-done, bf16[1152,1024]{1,0:T(8,128)(2,1)S(1)} %copy-done.1), custom_call_target="tpu_custom_call" | custom-call | tf_op jit(solution)/shard_map/middle/pallas_call | solution.py:364
  32.1 20.4 %all_to_all.25 = f32[16,72,128]{2,1,0:T(8,128)S(1)} all-to-all(f32[16,72,128]{2,1,0:T(8,128)S(1)} %bitcast.9), channel_id=1, replica_groups=mesh['member'=2,'cell'=16] {'cell'}, dimensions={0} | all-to-all | bytes 1179648 | tf_op jit(solution)/shard_map/all_to_all | solution.py:378
  52.4 0.9 %copy_bitcast_fusion = f32[72,2048]{1,0:T(8,128)} fusion(f32[16,72,128]{2,1,0:T(8,128)S(1)} %all_to_all.25), kind=kLoop, calls=%fused_computation | loop fusion | bytes 1179648 | tf_op jit(solution)/shard_map/all_to_all | solution.py:378
Async XLA Ops:
  0.0 28.3 %copy-start = (bf16[1024,1152]{1,0:T(8,128)(2,1)S(1)}, bf16[1024,1152]{1,0:T(8,128)(2,1)}, u32[]{:S(2)}) copy-start(bf16[1024,1152]{1,0:T(8,128)(2,1)} %lift_ref.1) | copy-start | bytes 7077892
  0.0 28.3 %copy-start.1 = (bf16[1152,1024]{1,0:T(8,128)(2,1)S(1)}, bf16[1152,1024]{1,0:T(8,128)(2,1)}, u32[]{:S(2)}) copy-start(bf16[1152,1024]{1,0:T(8,128)(2,1)} %back_ref.1) | copy-start | bytes 7077892

commit v19 on v16

--- a/solution.py
+++ b/solution.py
@@ -168,7 +168,7 @@
 
 def start_kernel(
     energy_hbm, courant_hbm, sea_hbm, out_ref, courant_ref, faces_ref,
-    energy_ref, sea_ref, speeds_ref, edges_ref, sems, energy_sems,
+    energy_ref, sea_ref, speeds_ref, edges_ref, sems,
 ):
     groups = energy_ref.shape[0]
     tiles = out_ref.shape[0]
@@ -176,24 +176,18 @@
     sizes = [min(START_ROWS, groups - base) for base in bases]
     small = pltpu.make_async_copy(courant_hbm, courant_ref, sems.at[0])
     sea = pltpu.make_async_copy(sea_hbm, sea_ref, sems.at[1])
-    state_copies = [
-        pltpu.make_async_copy(
-            energy_hbm.at[pl.ds(base, size), :], energy_ref.at[pl.ds(base, size), :], energy_sems.at[step]
-        )
-        for step, (base, size) in enumerate(zip(bases, sizes))
-    ]
+    state_copy = pltpu.make_async_copy(energy_hbm, energy_ref, sems.at[2])
     small.start()
     sea.start()
-    for copy in state_copies:
-        copy.start()
+    state_copy.start()
     edges_ref[...] = jnp.zeros((LANES, LANES), jnp.float32)
     small.wait()
     spread_speeds(courant_ref, speeds_ref)
     sea.wait()
     faces_ref[...] = face_rows(sea_ref[...].astype(jnp.float32))
     rank = lax.axis_index("cell")
-    for copy, base, size in zip(state_copies, bases, sizes):
-        copy.wait()
+    state_copy.wait()
+    for base, size in zip(bases, sizes):
         own = pl.multiple_of(rank * groups + base, ROWS)
         speed = speeds_ref[pl.ds(own, size), :]
         state = [
@@ -260,16 +254,17 @@
         halo = pltpu.roll(halo, at, 1) if at else halo
         halos[block] = jnp.where(lane >= at, halo, halos[block])
         halos[block + 1] = halo
+
+    def received(block):
+        pieces = []
+        for row in range(block * LANES, (block + 1) * LANES, ROWS):
+            source, at = divmod(row, groups)
+            pieces.append(blocks_ref[source, at : at + ROWS, :])
+        return jnp.concatenate(pieces, axis=0)
+
     for block in range(blocks):
         part = slice(block * LANES, (block + 1) * LANES)
-        pieces = []
-        for row in range(part.start, part.stop, ROWS):
-            source, at = divmod(row, groups)
-            pieces.append(blocks_ref[source, at : at + ROWS, :])
-        own = jnp.transpose(jnp.concatenate(pieces, axis=0))
-        ring_ref[block, :LANES, :] = own
-        ring_ref[block, LANES:, :] = halos[block]
-        half_ref[:LANES, part] = own.astype(jnp.bfloat16)
+        half_ref[:LANES, part] = jnp.transpose(received(block).astype(jnp.bfloat16))
         beside = jnp.concatenate([halos[block], jnp.zeros((padded - ring, LANES), jnp.float32)], axis=0)
         half_ref[LANES:, part] = beside.astype(jnp.bfloat16)
 
@@ -279,6 +274,9 @@
     for wide in lifts:
         lifted = dot_rows(half_ref[...], lift_ref[wide, :])
         squared_ref[:, wide] = (lifted * lifted).astype(jnp.bfloat16)
+    for block in range(blocks):
+        ring_ref[block, :LANES, :] = jnp.transpose(received(block))
+        ring_ref[block, LANES:, :] = halos[block]
 
     own_faces = faces_ref[pl.ds(rank, 1), :]
     after_faces = faces_ref[pl.ds(jnp.minimum(rank + 1, tiles - 1), 1), :]
@@ -348,8 +346,7 @@
             pltpu.VMEM(sea_mask.shape, sea_mask.dtype),
             pltpu.VMEM((components, LANES), f32),
             pltpu.VMEM((LANES, LANES), f32),
-            pltpu.SemaphoreType.DMA((2,)),
-            pltpu.SemaphoreType.DMA((-(-groups // START_ROWS),)),
+            pltpu.SemaphoreType.DMA((3,)),
         ],
         compiler_params=pltpu.CompilerParams(vmem_limit_bytes=16 << 20),
         cost_estimate=pl.CostEstimate(flops=1000000000, bytes_accessed=3 * 4 * groups * cells, transcendentals=0),

time: 53.4 us -> 53.2 us (level)
  no operation moved by 1% of the time
where the time goes in v19:
time: 53.2 us; the launch traced here: 53 us
  blocking collectives  45.7 us (86%)
  Pallas kernels  6.41 us (12%)
  local copies, waits for them, and re-layouts  0.87 us (2%)
    all_to_all x1, blocking collectives, tiled_shards(): lax.all_to_all(start, 'cell', split_axis=0, concat_axis=0, tiled=True)  25.4 us
    all_to_all x1, blocking collectives, tiled_shards(): lax.all_to_all(final, 'cell', split_axis=0, concat_axis=1, tiled=True)  20.3 us
    pallas_call x1, Pallas kernels, tiled_shards(): pl.pallas_call(middle_kernel, out_shape=jax.ShapeDtypeStruct((components,...  3.55 us
    pallas_call x1, Pallas kernels, tiled_shards(): pl.pallas_call(start_kernel, out_shape=[jax.ShapeDtypeStruct((tiles, grou...  2.86 us

profile of v19, /device:TPU:0, one launch (start us, length us, event | category | flops | bytes accessed | tf_op | source)
XLA Modules:
  0.0 53.0 jit_solution(6179356437185554034)
XLA Ops:
  0.0 0.0 copy-start
  0.0 0.0 copy-start.1
  0.0 2.9 %start.1 = (f32[16,80,128]{2,1,0:T(8,128)S(1)}, f32[9,128]{1,0:T(8,128)S(1)}, f32[16,128]{1,0:T(8,128)S(1)}) custom-call(f32[72,2048]{1,0:T(8,128)} %energy_hbm.1, f32[9,128]{1,0:T(8,128)} %bitcast.10, s32[16,128]{1,0:T(8,128)} %bitcast.11), custom_call_target="tpu_custom_call" | custom-call | flops 1000000000 | bytes 1769472 | tf_op jit(solution)/shard_map/start/pallas_call | solution.py:335
  2.9 25.4 %all_to_all.24.blocks_ref = f32[16,80,128]{2,1,0:T(8,128)S(1)} all-to-all(f32[16,80,128]{2,1,0:T(8,128)S(1)} %get-tuple-element.8), channel_id=1, replica_groups=mesh['member'=2,'cell'=16] {'cell'}, dimensions={0} | all-to-all | bytes 1310720 | tf_op jit(solution)/shard_map/all_to_all | solution.py:355
  28.3 0.0 copy-done
  28.3 0.0 copy-done.1
  28.3 3.6 %middle.1 = f32[1152,128]{1,0:T(8,128)S(1)} custom-call(f32[16,80,128]{2,1,0:T(8,128)S(1)} %all_to_all.24.blocks_ref, f32[9,128]{1,0:T(8,128)S(1)} %get-tuple-element.9.courant_ref, f32[16,128]{1,0:T(8,128)S(1)} %get-tuple-element.10.faces_ref, bf16[1024,1152]{1,0:T(8,128)(2,1)S(1)} %copy-done, bf16[1152,1024]{1,0:T(8,128)(2,1)S(1)} %copy-done.1), custom_call_target="tpu_custom_call" | custom-call | tf_op jit(solution)/shard_map/middle/pallas_call | solution.py:356
  31.8 20.3 %all_to_all.25 = f32[16,72,128]{2,1,0:T(8,128)S(1)} all-to-all(f32[16,72,128]{2,1,0:T(8,128)S(1)} %bitcast.9), channel_id=1, replica_groups=mesh['member'=2,'cell'=16] {'cell'}, dimensions={0} | all-to-all | bytes 1179648 | tf_op jit(solution)/shard_map/all_to_all | solution.py:368
  52.2 0.9 %copy_bitcast_fusion = f32[72,2048]{1,0:T(8,128)} fusion(f32[16,72,128]{2,1,0:T(8,128)S(1)} %all_to_all.25), kind=kLoop, calls=%fused_computation | loop fusion | bytes 1179648 | tf_op jit(solution)/shard_map/all_to_all | solution.py:368
Async XLA Ops:
  0.0 28.3 %copy-start = (bf16[1024,1152]{1,0:T(8,128)(2,1)S(1)}, bf16[1024,1152]{1,0:T(8,128)(2,1)}, u32[]{:S(2)}) copy-start(bf16[1024,1152]{1,0:T(8,128)(2,1)} %lift_ref.1) | copy-start | bytes 7077892
  0.0 28.3 %copy-start.1 = (bf16[1152,1024]{1,0:T(8,128)(2,1)S(1)}, bf16[1152,1024]{1,0:T(8,128)(2,1)}, u32[]{:S(2)}) copy-start(bf16[1152,1024]{1,0:T(8,128)(2,1)} %back_ref.1) | copy-start | bytes 7077892

commit v20 on v19

--- a/solution.py
+++ b/solution.py
@@ -295,6 +295,7 @@
     strided = [pl.ds(at, ROWS, stride=stride) for at in range(stride)]
     opens = [opens_ref[rows, :] for rows in strided]
 
+    chunk = 4 * LANES
     for base in range(0, modes, chunk):
         wide = slice(base, min(base + chunk, modes))
         source = dot_rows(squared_ref[...], back_ref[wide, :])
@@ -372,7 +373,7 @@
     devices = lax.axis_size("cell")
     groups, cells = wave_energy.shape
     whole = cells == devices * LANES and groups % ROWS == 0 and groups <= LANES
-    whole = whole and courant.shape[0] % LANES == 0 and courant.shape[0] <= LANES * LANES // ROWS
+    whole = whole and devices <= LANES // ROWS and courant.shape[0] % LANES == 0 and courant.shape[0] <= LANES * LANES // ROWS
     run = tiled_shards if whole else general_shards
     return run(wave_energy, courant, sea_mask, lift_weight, back_weight)
 

time: 53.2 us -> 53.2 us (level)
  no operation moved by 1% of the time
where the time goes in v20:
time: 53.2 us; the launch traced here: 53 us
  blocking collectives  45.7 us (86%)
  Pallas kernels  6.41 us (12%)
  local copies, waits for them, and re-layouts  0.87 us (2%)
    all_to_all x1, blocking collectives, tiled_shards(): lax.all_to_all(start, 'cell', split_axis=0, concat_axis=0, tiled=True)  25.4 us
    all_to_all x1, blocking collectives, tiled_shards(): lax.all_to_all(final, 'cell', split_axis=0, concat_axis=1, tiled=True)  20.3 us
    pallas_call x1, Pallas kernels, tiled_shards(): pl.pallas_call(middle_kernel, out_shape=jax.ShapeDtypeStruct((components,...  3.55 us
    pallas_call x1, Pallas kernels, tiled_shards(): pl.pallas_call(start_kernel, out_shape=[jax.ShapeDtypeStruct((tiles, grou...  2.86 us

profile of v20, /device:TPU:0, one launch (start us, length us, event | category | flops | bytes accessed | tf_op | source)
XLA Modules:
  0.0 53.0 jit_solution(6179356437185554034)
XLA Ops:
  0.0 0.0 copy-start
  0.0 0.0 copy-start.1
  0.0 2.9 %start.1 = (f32[16,80,128]{2,1,0:T(8,128)S(1)}, f32[9,128]{1,0:T(8,128)S(1)}, f32[16,128]{1,0:T(8,128)S(1)}) custom-call(f32[72,2048]{1,0:T(8,128)} %energy_hbm.1, f32[9,128]{1,0:T(8,128)} %bitcast.10, s32[16,128]{1,0:T(8,128)} %bitcast.11), custom_call_target="tpu_custom_call" | custom-call | flops 1000000000 | bytes 1769472 | tf_op jit(solution)/shard_map/start/pallas_call | solution.py:336
  2.9 25.4 %all_to_all.24.blocks_ref = f32[16,80,128]{2,1,0:T(8,128)S(1)} all-to-all(f32[16,80,128]{2,1,0:T(8,128)S(1)} %get-tuple-element.8), channel_id=1, replica_groups=mesh['member'=2,'cell'=16] {'cell'}, dimensions={0} | all-to-all | bytes 1310720 | tf_op jit(solution)/shard_map/all_to_all | solution.py:356
  28.3 0.0 copy-done
  28.3 0.0 copy-done.1
  28.3 3.6 %middle.1 = f32[1152,128]{1,0:T(8,128)S(1)} custom-call(f32[16,80,128]{2,1,0:T(8,128)S(1)} %all_to_all.24.blocks_ref, f32[9,128]{1,0:T(8,128)S(1)} %get-tuple-element.9.courant_ref, f32[16,128]{1,0:T(8,128)S(1)} %get-tuple-element.10.faces_ref, bf16[1024,1152]{1,0:T(8,128)(2,1)S(1)} %copy-done, bf16[1152,1024]{1,0:T(8,128)(2,1)S(1)} %copy-done.1), custom_call_target="tpu_custom_call" | custom-call | tf_op jit(solution)/shard_map/middle/pallas_call | solution.py:357
  31.8 20.3 %all_to_all.25 = f32[16,72,128]{2,1,0:T(8,128)S(1)} all-to-all(f32[16,72,128]{2,1,0:T(8,128)S(1)} %bitcast.9), channel_id=1, replica_groups=mesh['member'=2,'cell'=16] {'cell'}, dimensions={0} | all-to-all | bytes 1179648 | tf_op jit(solution)/shard_map/all_to_all | solution.py:369
  52.2 0.9 %copy_bitcast_fusion = f32[72,2048]{1,0:T(8,128)} fusion(f32[16,72,128]{2,1,0:T(8,128)S(1)} %all_to_all.25), kind=kLoop, calls=%fused_computation | loop fusion | bytes 1179648 | tf_op jit(solution)/shard_map/all_to_all | solution.py:369
Async XLA Ops:
  0.0 28.3 %copy-start = (bf16[1024,1152]{1,0:T(8,128)(2,1)S(1)}, bf16[1024,1152]{1,0:T(8,128)(2,1)}, u32[]{:S(2)}) copy-start(bf16[1024,1152]{1,0:T(8,128)(2,1)} %lift_ref.1) | copy-start | bytes 7077892
  0.0 28.3 %copy-start.1 = (bf16[1152,1024]{1,0:T(8,128)(2,1)S(1)}, bf16[1152,1024]{1,0:T(8,128)(2,1)}, u32[]{:S(2)}) copy-start(bf16[1152,1024]{1,0:T(8,128)(2,1)} %back_ref.1) | copy-start | bytes 7077892

commit v21 on v20

--- a/solution.py
+++ b/solution.py
@@ -147,7 +147,7 @@
     return sea * jnp.where(lane_index(sea.shape) == LANES - 1, below, turned)
 
 
-START_ROWS = 40
+START_ROWS = 24
 
 
 def start_rows(state, speed, faces_ref, out_ref, edges_ref, base):

time: 53.2 us -> 53.5 us (level)
  no operation moved by 1% of the time
where the time goes in v21:
time: 53.5 us; the launch traced here: 53.3 us
  blocking collectives  45.7 us (85%)
  Pallas kernels  6.73 us (13%)
  local copies, waits for them, and re-layouts  0.87 us (2%)
    all_to_all x1, blocking collectives, tiled_shards(): lax.all_to_all(start, 'cell', split_axis=0, concat_axis=0, tiled=True)  25.4 us
    all_to_all x1, blocking collectives, tiled_shards(): lax.all_to_all(final, 'cell', split_axis=0, concat_axis=1, tiled=True)  20.3 us
    pallas_call x1, Pallas kernels, tiled_shards(): pl.pallas_call(middle_kernel, out_shape=jax.ShapeDtypeStruct((components,...  3.56 us
    pallas_call x1, Pallas kernels, tiled_shards(): pl.pallas_call(start_kernel, out_shape=[jax.ShapeDtypeStruct((tiles, grou...  3.17 us

profile of v21, /device:TPU:0, one launch (start us, length us, event | category | flops | bytes accessed | tf_op | source)
XLA Modules:
  0.0 53.3 jit_solution(16769771120425365103)
XLA Ops:
  0.0 0.0 copy-start
  0.0 0.0 copy-start.1
  0.0 3.2 %start.1 = (f32[16,80,128]{2,1,0:T(8,128)S(1)}, f32[9,128]{1,0:T(8,128)S(1)}, f32[16,128]{1,0:T(8,128)S(1)}) custom-call(f32[72,2048]{1,0:T(8,128)} %energy_hbm.1, f32[9,128]{1,0:T(8,128)} %bitcast.10, s32[16,128]{1,0:T(8,128)} %bitcast.11), custom_call_target="tpu_custom_call" | custom-call | flops 1000000000 | bytes 1769472 | tf_op jit(solution)/shard_map/start/pallas_call | solution.py:336
  3.2 25.4 %all_to_all.24.blocks_ref = f32[16,80,128]{2,1,0:T(8,128)S(1)} all-to-all(f32[16,80,128]{2,1,0:T(8,128)S(1)} %get-tuple-element.8), channel_id=1, replica_groups=mesh['member'=2,'cell'=16] {'cell'}, dimensions={0} | all-to-all | bytes 1310720 | tf_op jit(solution)/shard_map/all_to_all | solution.py:356
  28.6 0.0 copy-done
  28.6 0.0 copy-done.1
  28.6 3.6 %middle.1 = f32[1152,128]{1,0:T(8,128)S(1)} custom-call(f32[16,80,128]{2,1,0:T(8,128)S(1)} %all_to_all.24.blocks_ref, f32[9,128]{1,0:T(8,128)S(1)} %get-tuple-element.9.courant_ref, f32[16,128]{1,0:T(8,128)S(1)} %get-tuple-element.10.faces_ref, bf16[1024,1152]{1,0:T(8,128)(2,1)S(1)} %copy-done, bf16[1152,1024]{1,0:T(8,128)(2,1)S(1)} %copy-done.1), custom_call_target="tpu_custom_call" | custom-call | tf_op jit(solution)/shard_map/middle/pallas_call | solution.py:357
  32.1 20.3 %all_to_all.25 = f32[16,72,128]{2,1,0:T(8,128)S(1)} all-to-all(f32[16,72,128]{2,1,0:T(8,128)S(1)} %bitcast.9), channel_id=1, replica_groups=mesh['member'=2,'cell'=16] {'cell'}, dimensions={0} | all-to-all | bytes 1179648 | tf_op jit(solution)/shard_map/all_to_all | solution.py:369
  52.5 0.9 %copy_bitcast_fusion = f32[72,2048]{1,0:T(8,128)} fusion(f32[16,72,128]{2,1,0:T(8,128)S(1)} %all_to_all.25), kind=kLoop, calls=%fused_computation | loop fusion | bytes 1179648 | tf_op jit(solution)/shard_map/all_to_all | solution.py:369
Async XLA Ops:
  0.0 28.6 %copy-start = (bf16[1024,1152]{1,0:T(8,128)(2,1)S(1)}, bf16[1024,1152]{1,0:T(8,128)(2,1)}, u32[]{:S(2)}) copy-start(bf16[1024,1152]{1,0:T(8,128)(2,1)} %lift_ref.1) | copy-start | bytes 7077892
  0.0 28.6 %copy-start.1 = (bf16[1152,1024]{1,0:T(8,128)(2,1)S(1)}, bf16[1152,1024]{1,0:T(8,128)(2,1)}, u32[]{:S(2)}) copy-start(bf16[1152,1024]{1,0:T(8,128)(2,1)} %back_ref.1) | copy-start | bytes 7077892

commit v22 on v21

--- a/solution.py
+++ b/solution.py
@@ -147,7 +147,7 @@
     return sea * jnp.where(lane_index(sea.shape) == LANES - 1, below, turned)
 
 
-START_ROWS = 24
+START_ROWS = LANES
 
 
 def start_rows(state, speed, faces_ref, out_ref, edges_ref, base):

time: 53.5 us -> 53.2 us (level)
  no operation moved by 1% of the time
where the time goes in v22:
time: 53.2 us; the launch traced here: 53 us
  blocking collectives  45.7 us (86%)
  Pallas kernels  6.39 us (12%)
  local copies, waits for them, and re-layouts  0.87 us (2%)
    all_to_all x1, blocking collectives, tiled_shards(): lax.all_to_all(start, 'cell', split_axis=0, concat_axis=0, tiled=True)  25.4 us
    all_to_all x1, blocking collectives, tiled_shards(): lax.all_to_all(final, 'cell', split_axis=0, concat_axis=1, tiled=True)  20.3 us
    pallas_call x1, Pallas kernels, tiled_shards(): pl.pallas_call(middle_kernel, out_shape=jax.ShapeDtypeStruct((components,...  3.56 us
    pallas_call x1, Pallas kernels, tiled_shards(): pl.pallas_call(start_kernel, out_shape=[jax.ShapeDtypeStruct((tiles, grou...  2.83 us

profile of v22, /device:TPU:0, one launch (start us, length us, event | category | flops | bytes accessed | tf_op | source)
XLA Modules:
  0.0 53.0 jit_solution(4241653068988522457)
XLA Ops:
  0.0 0.0 copy-start
  0.0 0.0 copy-start.1
  0.0 2.8 %start.1 = (f32[16,80,128]{2,1,0:T(8,128)S(1)}, f32[9,128]{1,0:T(8,128)S(1)}, f32[16,128]{1,0:T(8,128)S(1)}) custom-call(f32[72,2048]{1,0:T(8,128)} %energy_hbm.1, f32[9,128]{1,0:T(8,128)} %bitcast.10, s32[16,128]{1,0:T(8,128)} %bitcast.11), custom_call_target="tpu_custom_call" | custom-call | flops 1000000000 | bytes 1769472 | tf_op jit(solution)/shard_map/start/pallas_call | solution.py:336
  2.8 25.4 %all_to_all.24.blocks_ref = f32[16,80,128]{2,1,0:T(8,128)S(1)} all-to-all(f32[16,80,128]{2,1,0:T(8,128)S(1)} %get-tuple-element.8), channel_id=1, replica_groups=mesh['member'=2,'cell'=16] {'cell'}, dimensions={0} | all-to-all | bytes 1310720 | tf_op jit(solution)/shard_map/all_to_all | solution.py:356
  28.2 0.0 copy-done
  28.2 0.0 copy-done.1
  28.2 3.6 %middle.1 = f32[1152,128]{1,0:T(8,128)S(1)} custom-call(f32[16,80,128]{2,1,0:T(8,128)S(1)} %all_to_all.24.blocks_ref, f32[9,128]{1,0:T(8,128)S(1)} %get-tuple-element.9.courant_ref, f32[16,128]{1,0:T(8,128)S(1)} %get-tuple-element.10.faces_ref, bf16[1024,1152]{1,0:T(8,128)(2,1)S(1)} %copy-done, bf16[1152,1024]{1,0:T(8,128)(2,1)S(1)} %copy-done.1), custom_call_target="tpu_custom_call" | custom-call | tf_op jit(solution)/shard_map/middle/pallas_call | solution.py:357
  31.8 20.3 %all_to_all.25 = f32[16,72,128]{2,1,0:T(8,128)S(1)} all-to-all(f32[16,72,128]{2,1,0:T(8,128)S(1)} %bitcast.9), channel_id=1, replica_groups=mesh['member'=2,'cell'=16] {'cell'}, dimensions={0} | all-to-all | bytes 1179648 | tf_op jit(solution)/shard_map/all_to_all | solution.py:369
  52.1 0.9 %copy_bitcast_fusion = f32[72,2048]{1,0:T(8,128)} fusion(f32[16,72,128]{2,1,0:T(8,128)S(1)} %all_to_all.25), kind=kLoop, calls=%fused_computation | loop fusion | bytes 1179648 | tf_op jit(solution)/shard_map/all_to_all | solution.py:369
Async XLA Ops:
  0.0 28.2 %copy-start = (bf16[1024,1152]{1,0:T(8,128)(2,1)S(1)}, bf16[1024,1152]{1,0:T(8,128)(2,1)}, u32[]{:S(2)}) copy-start(bf16[1024,1152]{1,0:T(8,128)(2,1)} %lift_ref.1) | copy-start | bytes 7077892
  0.0 28.2 %copy-start.1 = (bf16[1152,1024]{1,0:T(8,128)(2,1)S(1)}, bf16[1152,1024]{1,0:T(8,128)(2,1)}, u32[]{:S(2)}) copy-start(bf16[1152,1024]{1,0:T(8,128)(2,1)} %back_ref.1) | copy-start | bytes 7077892

commit v23 on v22

--- a/solution.py
+++ b/solution.py
@@ -128,16 +128,14 @@
     return speed, 0.5 * size * (1.0 - size), speed >= 0.0
 
 
-def spread_speeds(courant_ref, speeds_ref):
-    parts = courant_ref.shape[0]
-    square = jnp.concatenate(
-        [courant_ref[...], jnp.zeros((LANES - parts, LANES), jnp.float32)], axis=0
-    )
-    turned = jnp.transpose(square)
-    for part in range(parts):
-        speeds_ref[pl.ds(part * LANES, LANES), :] = jnp.broadcast_to(
-            turned[:, part : part + 1], (LANES, LANES)
-        )
+def own_speeds(courant_ref, first):
+    part, at = first // LANES, first % LANES
+    this = courant_ref[pl.ds(part, 1), :]
+    following = courant_ref[pl.ds(jnp.minimum(part + 1, courant_ref.shape[0] - 1), 1), :]
+    back = (LANES - at) % LANES
+    this, following = pltpu.roll(this, back, 1), pltpu.roll(following, back, 1)
+    row = jnp.where(lane_index((1, LANES)) < LANES - at, this, following)
+    return jnp.transpose(jnp.broadcast_to(row, (LANES, LANES)))
 
 
 def face_rows(sea):
@@ -168,7 +166,7 @@
 
 def start_kernel(
     energy_hbm, courant_hbm, sea_hbm, out_ref, courant_ref, faces_ref,
-    energy_ref, sea_ref, speeds_ref, edges_ref, sems,
+    energy_ref, sea_ref, edges_ref, sems,
 ):
     groups = energy_ref.shape[0]
     tiles = out_ref.shape[0]
@@ -177,19 +175,17 @@
     small = pltpu.make_async_copy(courant_hbm, courant_ref, sems.at[0])
     sea = pltpu.make_async_copy(sea_hbm, sea_ref, sems.at[1])
     state_copy = pltpu.make_async_copy(energy_hbm, energy_ref, sems.at[2])
+    state_copy.start()
     small.start()
     sea.start()
-    state_copy.start()
     edges_ref[...] = jnp.zeros((LANES, LANES), jnp.float32)
     small.wait()
-    spread_speeds(courant_ref, speeds_ref)
+    speeds = own_speeds(courant_ref, lax.axis_index("cell") * groups)
     sea.wait()
     faces_ref[...] = face_rows(sea_ref[...].astype(jnp.float32))
-    rank = lax.axis_index("cell")
     state_copy.wait()
     for base, size in zip(bases, sizes):
-        own = pl.multiple_of(rank * groups + base, ROWS)
-        speed = speeds_ref[pl.ds(own, size), :]
+        speed = speeds[base : base + size]
         state = [
             energy_ref[base : base + size, tile * LANES : (tile + 1) * LANES] for tile in range(tiles)
         ]
@@ -345,7 +341,6 @@
         scratch_shapes=[
             pltpu.VMEM((groups, cells), f32),
             pltpu.VMEM(sea_mask.shape, sea_mask.dtype),
-            pltpu.VMEM((components, LANES), f32),
             pltpu.VMEM((LANES, LANES), f32),
             pltpu.SemaphoreType.DMA((3,)),
         ],

time: 53.2 us -> 53.2 us (level)
  no operation moved by 1% of the time
where the time goes in v23:
time: 53.2 us; the launch traced here: 53 us
  blocking collectives  45.7 us (86%)
  Pallas kernels  6.37 us (12%)
  local copies, waits for them, and re-layouts  0.87 us (2%)
    all_to_all x1, blocking collectives, tiled_shards(): lax.all_to_all(start, 'cell', split_axis=0, concat_axis=0, tiled=True)  25.4 us
    all_to_all x1, blocking collectives, tiled_shards(): lax.all_to_all(final, 'cell', split_axis=0, concat_axis=1, tiled=True)  20.3 us
    pallas_call x1, Pallas kernels, tiled_shards(): pl.pallas_call(middle_kernel, out_shape=jax.ShapeDtypeStruct((components,...  3.55 us
    pallas_call x1, Pallas kernels, tiled_shards(): pl.pallas_call(start_kernel, out_shape=[jax.ShapeDtypeStruct((tiles, grou...  2.81 us

profile of v23, /device:TPU:0, one launch (start us, length us, event | category | flops | bytes accessed | tf_op | source)
XLA Modules:
  0.0 53.0 jit_solution(7585172173951585412)
XLA Ops:
  0.0 0.0 copy-start
  0.0 0.0 copy-start.1
  0.0 2.8 %start.1 = (f32[16,80,128]{2,1,0:T(8,128)S(1)}, f32[9,128]{1,0:T(8,128)S(1)}, f32[16,128]{1,0:T(8,128)S(1)}) custom-call(f32[72,2048]{1,0:T(8,128)} %energy_hbm.1, f32[9,128]{1,0:T(8,128)} %bitcast.10, s32[16,128]{1,0:T(8,128)} %bitcast.11), custom_call_target="tpu_custom_call" | custom-call | flops 1000000000 | bytes 1769472 | tf_op jit(solution)/shard_map/start/pallas_call | solution.py:332
  2.8 25.4 %all_to_all.24.blocks_ref = f32[16,80,128]{2,1,0:T(8,128)S(1)} all-to-all(f32[16,80,128]{2,1,0:T(8,128)S(1)} %get-tuple-element.8), channel_id=1, replica_groups=mesh['member'=2,'cell'=16] {'cell'}, dimensions={0} | all-to-all | bytes 1310720 | tf_op jit(solution)/shard_map/all_to_all | solution.py:351
  28.2 0.0 copy-done
  28.2 0.0 copy-done.1
  28.2 3.6 %middle.1 = f32[1152,128]{1,0:T(8,128)S(1)} custom-call(f32[16,80,128]{2,1,0:T(8,128)S(1)} %all_to_all.24.blocks_ref, f32[9,128]{1,0:T(8,128)S(1)} %get-tuple-element.9.courant_ref, f32[16,128]{1,0:T(8,128)S(1)} %get-tuple-element.10.faces_ref, bf16[1024,1152]{1,0:T(8,128)(2,1)S(1)} %copy-done, bf16[1152,1024]{1,0:T(8,128)(2,1)S(1)} %copy-done.1), custom_call_target="tpu_custom_call" | custom-call | tf_op jit(solution)/shard_map/middle/pallas_call | solution.py:352
  31.8 20.3 %all_to_all.25 = f32[16,72,128]{2,1,0:T(8,128)S(1)} all-to-all(f32[16,72,128]{2,1,0:T(8,128)S(1)} %bitcast.9), channel_id=1, replica_groups=mesh['member'=2,'cell'=16] {'cell'}, dimensions={0} | all-to-all | bytes 1179648 | tf_op jit(solution)/shard_map/all_to_all | solution.py:364
  52.1 0.9 %copy_bitcast_fusion = f32[72,2048]{1,0:T(8,128)} fusion(f32[16,72,128]{2,1,0:T(8,128)S(1)} %all_to_all.25), kind=kLoop, calls=%fused_computation | loop fusion | bytes 1179648 | tf_op jit(solution)/shard_map/all_to_all | solution.py:364
Async XLA Ops:
  0.0 28.2 %copy-start = (bf16[1024,1152]{1,0:T(8,128)(2,1)S(1)}, bf16[1024,1152]{1,0:T(8,128)(2,1)}, u32[]{:S(2)}) copy-start(bf16[1024,1152]{1,0:T(8,128)(2,1)} %lift_ref.1) | copy-start | bytes 7077892
  0.0 28.2 %copy-start.1 = (bf16[1152,1024]{1,0:T(8,128)(2,1)S(1)}, bf16[1152,1024]{1,0:T(8,128)(2,1)}, u32[]{:S(2)}) copy-start(bf16[1152,1024]{1,0:T(8,128)(2,1)} %back_ref.1) | copy-start | bytes 7077892
